TPU v7x, 128 devices: a whole 4x4x4 slice. The times are simulated.
128 devices in a mesh: dp: 8 (over y, core), ctx: 2 (over x_hi), fsdp: 8 (over x_lo, z).
Axes of the slice: x: 4 (x_hi: 2, x_lo: 2; x = x_hi * 2 + x_lo), y: 4, z: 4, core: 2. Of those that a mesh axis runs over, the one named last changes fastest.
Arguments:
- tokens: bfloat16 [8, 2048, 1536], P('dp', ('fsdp', 'ctx')), may hold values from -6 to 6
- lengths: int32 [8], P('dp'), may hold values from 1024 to 2048, as said below
- cotangent: bfloat16 [8, 2048, 1536], P('dp', ('fsdp', 'ctx')), may hold values from -6 to 6
- attend_gain: float32 [1536], replicated, may hold values from 0.5 to 1.5
- query_weight: bfloat16 [1536, 1536], P(('ctx', 'fsdp')), may hold values from -0.21875 to 0.21875
- keyval_weight: bfloat16 [1536, 256], P(('ctx', 'fsdp')), may hold values from -0.15625 to 0.15625
- attend_output: bfloat16 [1536, 1536], P(('ctx', 'fsdp')), may hold values from -1.75 to 1.75
- lower_gain: float32 [1536], replicated, may hold values from 0.5 to 1.5
- lower_gate: bfloat16 [1536, 4608], P(('ctx', 'fsdp')), may hold values from -0.15625 to 0.15625
- lower_lift: bfloat16 [1536, 4608], P(('ctx', 'fsdp')), may hold values from -0.15625 to 0.15625
- lower_drop: bfloat16 [4608, 1536], P(('ctx', 'fsdp')), may hold values from -0.09375 to 0.09375
- recur_gain: float32 [1536], replicated, may hold values from 0.5 to 1.5
- recur_input: bfloat16 [1536, 2048], P(('ctx', 'fsdp')), may hold values from -0.15625 to 0.15625
- recur_branch: bfloat16 [1536, 2048], P(('ctx', 'fsdp')), may hold values from -0.15625 to 0.15625
- recur_output: bfloat16 [2048, 1536], P(('ctx', 'fsdp')), may hold values from -0.375 to 0.375
- temporal_kernel: float32 [4, 2048], replicated, may hold values from -3 to 3
- decay_gate: bfloat16 [16, 128, 128], replicated, may hold values from -2 to 2
- input_gate: bfloat16 [16, 128, 128], replicated, may hold values from -0.5 to 0.5
- decay_rate: float32 [2048], replicated, as said below
- upper_gain: float32 [1536], replicated, may hold values from 0.5 to 1.5
- upper_gate: bfloat16 [1536, 4608], P(('ctx', 'fsdp')), may hold values from -0.15625 to 0.15625
- upper_lift: bfloat16 [1536, 4608], P(('ctx', 'fsdp')), may hold values from -0.15625 to 0.15625
- upper_drop: bfloat16 [4608, 1536], P(('ctx', 'fsdp')), may hold values from -0.09375 to 0.09375
Outputs:
- out_tokens: bfloat16 [8, 2048, 1536], P('dp', ('fsdp', 'ctx'))
- grad_tokens: float32 [8, 2048, 1536], P('dp', ('fsdp', 'ctx'))
- grad_attend_gain: float32 [1536], replicated
- grad_query_weight: float32 [1536, 1536], P(('ctx', 'fsdp'))
- grad_keyval_weight: float32 [1536, 256], P(('ctx', 'fsdp'))
- grad_attend_output: float32 [1536, 1536], P(('ctx', 'fsdp'))
- grad_lower_gain: float32 [1536], replicated
- grad_lower_gate: float32 [1536, 4608], P(('ctx', 'fsdp'))
- grad_lower_lift: float32 [1536, 4608], P(('ctx', 'fsdp'))
- grad_lower_drop: float32 [4608, 1536], P(('ctx', 'fsdp'))
- grad_recur_gain: float32 [1536], replicated
- grad_recur_input: float32 [1536, 2048], P(('ctx', 'fsdp'))
- grad_recur_branch: float32 [1536, 2048], P(('ctx', 'fsdp'))
- grad_recur_output: float32 [2048, 1536], P(('ctx', 'fsdp'))
- grad_temporal_kernel: float32 [4, 2048], replicated
- grad_decay_gate: float32 [16, 128, 128], replicated
- grad_input_gate: float32 [16, 128, 128], replicated
- grad_decay_rate: float32 [2048], replicated
- grad_upper_gain: float32 [1536], replicated
- grad_upper_gate: float32 [1536, 4608], P(('ctx', 'fsdp'))
- grad_upper_lift: float32 [1536, 4608], P(('ctx', 'fsdp'))
- grad_upper_drop: float32 [4608, 1536], P(('ctx', 'fsdp'))
Inputs may be any that keep to these rules, and one draw needn't show every extreme that they name: `lengths`: valid slots of a sequence form a prefix of its slots. `decay_rate`: one decay parameter for each recurrence channel.
All inputs are finite; a program needn't handle non-finite values.
Results may differ from a plain program's by a relative error of at most 0.028.
Values may be sent and summed in bfloat16 or wider, within the bound.
No kernel may reach another device: no remote copies, remote signals or barrier semaphores. Data moves between devices by JAX's collectives and lax.ppermute only.
A program may use at most 384 MiB of HBM per device.

v0:
```python
import jax
import jax.numpy as jnp
from jax import lax
from jax.sharding import PartitionSpec as P

WINDOW = 1024


EPSILON = 1e-06
DECAY_SCALE = 8.0


def from_behind(shard, axis, by):
    peers = lax.axis_size(axis)
    pairs = [(i, i + by) for i in range(peers) if 0 <= i + by < peers]
    return lax.ppermute(shard, axis, pairs)


def prefix(value, axis, join, neutral, backward):
    count, mine = (lax.axis_size(axis), lax.axis_index(axis))
    pieces = jax.tree.map(lambda part: lax.all_gather(part, axis), value)
    if backward:
        pieces = jax.tree.map(lambda part: part[::-1], pieces)
        mine = count - 1 - mine
    subtotal = jax.tree.map(
        lambda part, zero: jnp.full_like(part, 0) + jnp.asarray(zero, part.dtype), value, neutral
    )

    def turn(position, subtotal):
        longer = join(subtotal, jax.tree.map(lambda part: part[position], pieces))
        return jax.tree.map(lambda new, old: jnp.where(position < mine, new, old), longer, subtotal)

    return lax.fori_loop(0, count - 1, turn, subtotal)


def normalize(values, gain):
    return values * lax.rsqrt(jnp.mean(values * values, axis=-1, keepdims=True) + EPSILON) * gain


def smooth_gelu(values):
    return jax.nn.gelu(values, approximate=True)


def gated_unit(gate_pre, lift_pre):
    return smooth_gelu(gate_pre) * lift_pre


def branch_merge(states, branch_y):
    return states * smooth_gelu(branch_y)


def compose(earlier, later):
    return (earlier[0] * later[0], later[0] * earlier[1] + later[1])


def gate_terms(pre_decay, pre_admit, conv_out, decay_rate):
    retain = jax.nn.sigmoid(pre_decay)
    admit = jax.nn.sigmoid(pre_admit)
    log_decay = -DECAY_SCALE * jax.nn.softplus(decay_rate) * (0.25 + retain)
    return (jnp.exp(log_decay), jnp.sqrt(-jnp.expm1(2.0 * log_decay)) * admit * conv_out)


def matmul(left, right):
    return jnp.dot(left, right, preferred_element_type=jnp.float32)


def times_transposed(left, right):
    return lax.dot_general(
        left, right, (((1,), (1,)), ((), ())), preferred_element_type=jnp.float32
    )


def transposed_times(left, right):
    return lax.dot_general(
        left, right, (((0,), (0,)), ((), ())), preferred_element_type=jnp.float32
    )


def collect(first, second, third, fourth, fifth, sixth):
    return (
        lax.all_gather(first, ("ctx", "fsdp"), axis=0, tiled=True),
        lax.all_gather(second, ("ctx", "fsdp"), axis=0, tiled=True),
        lax.all_gather(third, ("ctx", "fsdp"), axis=0, tiled=True),
        lax.all_gather(fourth, ("ctx", "fsdp"), axis=0, tiled=True),
        lax.all_gather(fifth, ("ctx", "fsdp"), axis=0, tiled=True),
        lax.all_gather(sixth, ("ctx", "fsdp"), axis=0, tiled=True),
    )


def reduce_three(shared, other, first, second, third):
    shards = (
        lax.psum_scatter(
            transposed_times(shared, first).astype(jnp.bfloat16),
            ("ctx", "fsdp"),
            scatter_dimension=0,
            tiled=True,
        ).astype(jnp.float32),
        lax.psum_scatter(
            transposed_times(shared, second).astype(jnp.bfloat16),
            ("ctx", "fsdp"),
            scatter_dimension=0,
            tiled=True,
        ).astype(jnp.float32),
        lax.psum_scatter(
            transposed_times(other, third).astype(jnp.bfloat16),
            ("ctx", "fsdp"),
            scatter_dimension=0,
            tiled=True,
        ).astype(jnp.float32),
    )
    return (
        lax.psum(shards[0].astype(jnp.bfloat16), "dp").astype(jnp.float32),
        lax.psum(shards[1].astype(jnp.bfloat16), "dp").astype(jnp.float32),
        lax.psum(shards[2].astype(jnp.bfloat16), "dp").astype(jnp.float32),
    )


def to_mixer(values):
    return lax.all_to_all(values, "ctx", split_axis=1, concat_axis=0, tiled=True)


def from_mixer(values):
    return lax.all_to_all(values, "ctx", split_axis=0, concat_axis=1, tiled=True)


def dense_forward(residual, gain, gate_weight, lift_weight, drop_weight):
    normed, norm_pull = jax.vjp(normalize, residual, gain)
    lowered = normed.astype(jnp.bfloat16)
    gate_pre = matmul(lowered, gate_weight)
    lift_pre = matmul(lowered, lift_weight)
    hidden, unit_pull = jax.vjp(gated_unit, gate_pre, lift_pre)
    hidden_low = hidden.astype(jnp.bfloat16)
    return (residual + matmul(hidden_low, drop_weight), (norm_pull, lowered, unit_pull, hidden_low))


def dense_backward(residual_grad, stored, gate_weight, lift_weight, drop_weight):
    norm_pull, lowered, unit_pull, hidden_low = stored
    grad_low = residual_grad.astype(jnp.bfloat16)
    hidden_grad = times_transposed(grad_low, drop_weight)
    gate_grad, lift_grad = unit_pull(hidden_grad)
    gate_low = gate_grad.astype(jnp.bfloat16)
    lift_low = lift_grad.astype(jnp.bfloat16)
    normed_grad = times_transposed(gate_low, gate_weight) + times_transposed(lift_low, lift_weight)
    input_grad, gain_grad = norm_pull(normed_grad)
    weight_grads = reduce_three(lowered, hidden_low, gate_low, lift_low, grad_low)
    return (residual_grad + input_grad, gain_grad, weight_grads)


def body(
    tokens,
    lengths,
    cotangent,
    attend_gain,
    query_weight,
    keyval_weight,
    attend_output,
    lower_gain,
    lower_gate,
    lower_lift,
    lower_drop,
    recur_gain,
    recur_input,
    recur_branch,
    recur_output,
    temporal_kernel,
    decay_gate,
    input_gate,
    decay_rate,
    upper_gain,
    upper_gate,
    upper_lift,
    upper_drop,
):
    ctx_count = lax.axis_size("ctx")
    fsdp_count = lax.axis_size("fsdp")
    ctx_index = lax.axis_index("ctx")
    fsdp_index = lax.axis_index("fsdp")
    row_count = tokens.shape[1]
    mixer_rows = row_count * ctx_count
    head_size = keyval_weight.shape[1] // 2
    local_heads = query_weight.shape[1] // head_size // ctx_count
    query_width = local_heads * head_size
    channel_count = recur_input.shape[1] // ctx_count
    block_width = decay_gate.shape[1]
    local_blocks = channel_count // block_width
    tap_count = temporal_kernel.shape[0]
    score_scale = head_size ** (-0.5)
    token_pos = (fsdp_index * ctx_count + ctx_index) * row_count + jnp.arange(
        row_count, dtype=jnp.int32
    )
    valid = (token_pos < lengths[0]).astype(jnp.float32)[:, None]
    mixer_start = fsdp_index * mixer_rows
    reach = min(-(-WINDOW // mixer_rows), fsdp_count - 1)
    query_pos = mixer_start + jnp.arange(mixer_rows, dtype=jnp.int32)
    key_pos = (
        mixer_start - reach * mixer_rows + jnp.arange((reach + 1) * mixer_rows, dtype=jnp.int32)
    )
    key_mask = (
        (key_pos[None, :] <= query_pos[:, None])
        & (query_pos[:, None] - key_pos[None, :] < WINDOW)
        & (key_pos[None, :] >= 0)
    )
    chan_start = ctx_index * channel_count
    local_decay = lax.dynamic_slice_in_dim(decay_rate, chan_start, channel_count, 0)
    local_taps = lax.dynamic_slice_in_dim(temporal_kernel, chan_start, channel_count, 1)
    local_decay_gate = lax.dynamic_slice_in_dim(
        decay_gate, ctx_index * local_blocks, local_blocks, 0
    )
    local_input_gate = lax.dynamic_slice_in_dim(
        input_gate, ctx_index * local_blocks, local_blocks, 0
    )
    start_rows = tokens[0].astype(jnp.float32)
    lower_set = collect(
        query_weight, keyval_weight, attend_output, lower_gate, lower_lift, lower_drop
    )
    normed_attend, attend_pull = jax.vjp(normalize, start_rows, attend_gain)
    attend_low = normed_attend.astype(jnp.bfloat16)
    queries = matmul(attend_low, lower_set[0]).astype(jnp.bfloat16)
    keyvals = matmul(attend_low, lower_set[1]).astype(jnp.bfloat16)
    packed = jnp.concatenate(
        [
            queries.reshape(row_count, ctx_count, query_width),
            jnp.broadcast_to(keyvals[:, None, :], (row_count, ctx_count, 2 * head_size)),
        ],
        axis=2,
    )
    mixed_in = to_mixer(packed.reshape(row_count, ctx_count * (query_width + 2 * head_size)))
    query_mix = mixed_in[:, :query_width].reshape(mixer_rows, local_heads, head_size)
    keyval_own = mixed_in[:, query_width:]
    earlier = [from_behind(keyval_own, "fsdp", distance) for distance in range(reach, 0, -1)]
    keyval_all = jnp.concatenate(earlier + [keyval_own], axis=0)
    key_all = keyval_all[:, :head_size]
    value_all = keyval_all[:, head_size:]
    scores = (
        jnp.einsum("qhd,kd->hqk", query_mix, key_all, preferred_element_type=jnp.float32)
        * score_scale
    )
    scores = jnp.where(key_mask, scores, -1e30)
    highest = jnp.max(scores, axis=-1, keepdims=True)
    log_total = highest + jnp.log(jnp.sum(jnp.exp(scores - highest), axis=-1, keepdims=True))
    probs_low = jnp.exp(scores - log_total).astype(jnp.bfloat16)
    attended = jnp.einsum("hqk,kd->qhd", probs_low, value_all, preferred_element_type=jnp.float32)
    attend_back = from_mixer(attended.reshape(mixer_rows, query_width).astype(jnp.bfloat16))
    first_rows = start_rows + matmul(attend_back, lower_set[2])
    second_rows, lower_kept = dense_forward(
        first_rows, lower_gain, lower_set[3], lower_set[4], lower_set[5]
    )
    upper_set = collect(recur_input, recur_branch, recur_output, upper_gate, upper_lift, upper_drop)
    normed_recur, recur_pull = jax.vjp(normalize, second_rows, recur_gain)
    recur_low = normed_recur.astype(jnp.bfloat16)
    branch_x = matmul(recur_low, upper_set[0]).astype(jnp.bfloat16)
    branch_y = matmul(recur_low, upper_set[1])
    x_mix = to_mixer(branch_x)
    rim_rows = from_behind(x_mix[mixer_rows - (tap_count - 1) :], "fsdp", 1)
    x_extended = jnp.concatenate([rim_rows, x_mix], axis=0).astype(jnp.float32)
    conv_out = jnp.zeros((mixer_rows, channel_count), jnp.float32)
    for tap_index in range(tap_count):
        conv_out = (
            conv_out
            + local_taps[tap_index]
            * x_extended[tap_count - 1 - tap_index : tap_count - 1 - tap_index + mixer_rows]
        )
    conv_low = conv_out.astype(jnp.bfloat16).reshape(mixer_rows, local_blocks, block_width)
    pre_decay = jnp.einsum(
        "tnr,nrs->tns", conv_low, local_decay_gate, preferred_element_type=jnp.float32
    ).reshape(mixer_rows, channel_count)
    pre_admit = jnp.einsum(
        "tnr,nrs->tns", conv_low, local_input_gate, preferred_element_type=jnp.float32
    ).reshape(mixer_rows, channel_count)
    gate_out, gate_pull = jax.vjp(gate_terms, pre_decay, pre_admit, conv_out, local_decay)
    factors, updates = gate_out
    running, local_states = lax.associative_scan(compose, (factors, updates), axis=0)
    unit_pair = (jnp.ones((channel_count,), jnp.float32), jnp.zeros((channel_count,), jnp.float32))
    state_prefix = prefix((running[-1], local_states[-1]), "fsdp", compose, unit_pair, False)
    state_in = state_prefix[1]
    states = local_states + running * state_in
    states_back = from_mixer(states.astype(jnp.bfloat16))
    merged, merge_pull = jax.vjp(branch_merge, states_back.astype(jnp.float32), branch_y)
    merged_low = merged.astype(jnp.bfloat16)
    third_rows = second_rows + matmul(merged_low, upper_set[2])
    fourth_rows, upper_kept = dense_forward(
        third_rows, upper_gain, upper_set[3], upper_set[4], upper_set[5]
    )
    out_tokens = (fourth_rows * valid).astype(jnp.bfloat16)[None]
    upper_back = collect(
        recur_input, recur_branch, recur_output, upper_gate, upper_lift, upper_drop
    )
    residual_grad = cotangent[0].astype(jnp.float32) * valid
    residual_grad, grad_upper_gain, upper_dense_grads = dense_backward(
        residual_grad, upper_kept, upper_back[3], upper_back[4], upper_back[5]
    )
    recur_grad_low = residual_grad.astype(jnp.bfloat16)
    merged_grad = times_transposed(recur_grad_low, upper_back[2])
    states_grad, branch_y_grad = merge_pull(merged_grad)
    state_grad_mix = to_mixer(states_grad.astype(jnp.bfloat16)).astype(jnp.float32)
    coefficient = jnp.concatenate([factors[1:], jnp.ones_like(factors[:1])], axis=0)
    flip_running, flip_adjoint = lax.associative_scan(
        compose, (coefficient[::-1], state_grad_mix[::-1]), axis=0
    )
    tail_product = flip_running[::-1]
    local_adjoint = flip_adjoint[::-1]
    after_prefix = prefix(
        (factors[0] * tail_product[0], factors[0] * local_adjoint[0]),
        "fsdp",
        compose,
        unit_pair,
        True,
    )
    adjoint = local_adjoint + tail_product * after_prefix[1]
    previous = jnp.concatenate([state_in[None], states[:-1]], axis=0)
    decay_grad, admit_grad, conv_grad, local_decay_grad = gate_pull((adjoint * previous, adjoint))
    decay_grad_low = decay_grad.astype(jnp.bfloat16).reshape(mixer_rows, local_blocks, block_width)
    admit_grad_low = admit_grad.astype(jnp.bfloat16).reshape(mixer_rows, local_blocks, block_width)
    conv_grad = conv_grad + (
        jnp.einsum(
            "tns,nrs->tnr", decay_grad_low, local_decay_gate, preferred_element_type=jnp.float32
        )
        + jnp.einsum(
            "tns,nrs->tnr", admit_grad_low, local_input_gate, preferred_element_type=jnp.float32
        )
    ).reshape(mixer_rows, channel_count)
    local_gate_grad = jnp.einsum(
        "tnr,tns->nrs", conv_low, decay_grad_low, preferred_element_type=jnp.float32
    )
    local_admit_grad = jnp.einsum(
        "tnr,tns->nrs", conv_low, admit_grad_low, preferred_element_type=jnp.float32
    )
    grad_decay_gate = lax.dynamic_update_slice_in_dim(
        jnp.zeros(decay_gate.shape, jnp.float32), local_gate_grad, ctx_index * local_blocks, 0
    )
    grad_input_gate = lax.dynamic_update_slice_in_dim(
        jnp.zeros(input_gate.shape, jnp.float32), local_admit_grad, ctx_index * local_blocks, 0
    )
    grad_decay_rate = lax.dynamic_update_slice_in_dim(
        jnp.zeros(decay_rate.shape, jnp.float32), local_decay_grad, chan_start, 0
    )
    extended_grad = jnp.zeros((mixer_rows + tap_count - 1, channel_count), jnp.float32)
    tap_grads = []
    for tap_index in range(tap_count):
        extended_grad = extended_grad + jnp.pad(
            local_taps[tap_index] * conv_grad, ((tap_count - 1 - tap_index, tap_index), (0, 0))
        )
        tap_grads.append(
            jnp.sum(
                conv_grad
                * x_extended[tap_count - 1 - tap_index : tap_count - 1 - tap_index + mixer_rows],
                axis=0,
            )
        )
    grad_temporal_kernel = lax.dynamic_update_slice_in_dim(
        jnp.zeros(temporal_kernel.shape, jnp.float32), jnp.stack(tap_grads), chan_start, 1
    )
    spill_rows = from_behind(extended_grad[: tap_count - 1], "fsdp", -1)
    x_mix_grad = extended_grad[tap_count - 1 :] + jnp.pad(
        spill_rows, ((mixer_rows - (tap_count - 1), 0), (0, 0))
    )
    branch_x_grad = from_mixer(x_mix_grad.astype(jnp.bfloat16))
    branch_y_low = branch_y_grad.astype(jnp.bfloat16)
    recur_normed_grad = times_transposed(branch_x_grad, upper_back[0]) + times_transposed(
        branch_y_low, upper_back[1]
    )
    upper_mixer_grads = reduce_three(
        recur_low, merged_low, branch_x_grad, branch_y_low, recur_grad_low
    )
    recur_input_grad, grad_recur_gain = recur_pull(recur_normed_grad)
    residual_grad = residual_grad + recur_input_grad
    lower_back = collect(
        query_weight, keyval_weight, attend_output, lower_gate, lower_lift, lower_drop
    )
    residual_grad, grad_lower_gain, lower_dense_grads = dense_backward(
        residual_grad, lower_kept, lower_back[3], lower_back[4], lower_back[5]
    )
    grad_low = residual_grad.astype(jnp.bfloat16)
    attend_grad = times_transposed(grad_low, lower_back[2]).astype(jnp.bfloat16)
    attend_grad_mix = to_mixer(attend_grad).reshape(mixer_rows, local_heads, head_size)
    scores = (
        jnp.einsum("qhd,kd->hqk", query_mix, key_all, preferred_element_type=jnp.float32)
        * score_scale
    )
    scores = jnp.where(key_mask, scores, -1e30)
    probs = jnp.exp(scores - log_total)
    probs_low = probs.astype(jnp.bfloat16)
    prob_grad = jnp.einsum(
        "qhd,kd->hqk", attend_grad_mix, value_all, preferred_element_type=jnp.float32
    )
    delta = jnp.einsum("qhd,qhd->hq", attend_grad_mix.astype(jnp.float32), attended)
    score_grad = (probs * (prob_grad - delta[:, :, None])).astype(jnp.bfloat16)
    query_grad = (
        jnp.einsum("hqk,kd->qhd", score_grad, key_all, preferred_element_type=jnp.float32)
        * score_scale
    ).astype(jnp.bfloat16)
    key_grad = (
        jnp.einsum("hqk,qhd->kd", score_grad, query_mix, preferred_element_type=jnp.float32)
        * score_scale
    )
    value_grad = jnp.einsum(
        "hqk,qhd->kd", probs_low, attend_grad_mix, preferred_element_type=jnp.float32
    )
    keyval_grad = jnp.concatenate([key_grad, value_grad], axis=1)
    own_grad = keyval_grad[reach * mixer_rows :]
    for distance in range(1, reach + 1):
        piece = keyval_grad[(reach - distance) * mixer_rows : (reach - distance + 1) * mixer_rows]
        own_grad = own_grad + from_behind(piece.astype(jnp.bfloat16), "fsdp", -distance).astype(
            piece.dtype
        )
    packed_grad = jnp.concatenate(
        [query_grad.reshape(mixer_rows, query_width), own_grad.astype(jnp.bfloat16)], axis=1
    )
    returned = from_mixer(packed_grad).reshape(row_count, ctx_count, query_width + 2 * head_size)
    query_token_grad = returned[:, :, :query_width].reshape(row_count, ctx_count * query_width)
    keyval_token_grad = jnp.sum(returned[:, :, query_width:].astype(jnp.float32), axis=1).astype(
        jnp.bfloat16
    )
    attend_normed_grad = times_transposed(query_token_grad, lower_back[0]) + times_transposed(
        keyval_token_grad, lower_back[1]
    )
    lower_mixer_grads = reduce_three(
        attend_low, attend_back, query_token_grad, keyval_token_grad, grad_low
    )
    attend_input_grad, grad_attend_gain = attend_pull(attend_normed_grad)
    residual_grad = residual_grad + attend_input_grad
    small = lax.psum(
        (
            grad_attend_gain,
            grad_lower_gain,
            grad_recur_gain,
            grad_upper_gain,
            grad_temporal_kernel,
            grad_decay_gate,
            grad_input_gate,
            grad_decay_rate,
        ),
        ("dp", "ctx", "fsdp"),
    )
    return (
        out_tokens,
        residual_grad[None],
        small[0],
        lower_mixer_grads[0],
        lower_mixer_grads[1],
        lower_mixer_grads[2],
        small[1],
        lower_dense_grads[0],
        lower_dense_grads[1],
        lower_dense_grads[2],
        small[2],
        upper_mixer_grads[0],
        upper_mixer_grads[1],
        upper_mixer_grads[2],
        small[4],
        small[5],
        small[6],
        small[7],
        small[3],
        upper_dense_grads[0],
        upper_dense_grads[1],
        upper_dense_grads[2],
    )


def solution(mesh):
    return jax.shard_map(
        body,
        mesh=mesh,
        in_specs=(
            P("dp", ("fsdp", "ctx"), None),
            P("dp"),
            P("dp", ("fsdp", "ctx"), None),
            P(),
            P(("ctx", "fsdp"), None),
            P(("ctx", "fsdp"), None),
            P(("ctx", "fsdp"), None),
            P(),
            P(("ctx", "fsdp"), None),
            P(("ctx", "fsdp"), None),
            P(("ctx", "fsdp"), None),
            P(),
            P(("ctx", "fsdp"), None),
            P(("ctx", "fsdp"), None),
            P(("ctx", "fsdp"), None),
            P(),
            P(),
            P(),
            P(),
            P(),
            P(("ctx", "fsdp"), None),
            P(("ctx", "fsdp"), None),
            P(("ctx", "fsdp"), None),
        ),
        out_specs=(
            P("dp", ("fsdp", "ctx"), None),
            P("dp", ("fsdp", "ctx"), None),
            P(),
            P(("ctx", "fsdp"), None),
            P(("ctx", "fsdp"), None),
            P(("ctx", "fsdp"), None),
            P(),
            P(("ctx", "fsdp"), None),
            P(("ctx", "fsdp"), None),
            P(("ctx", "fsdp"), None),
            P(),
            P(("ctx", "fsdp"), None),
            P(("ctx", "fsdp"), None),
            P(("ctx", "fsdp"), None),
            P(),
            P(),
            P(),
            P(),
            P(),
            P(("ctx", "fsdp"), None),
            P(("ctx", "fsdp"), None),
            P(("ctx", "fsdp"), None),
        ),
        check_vma=False,
    )
```

profile of v0, /device:TPU:1, one launch (start us, length us, event | category | flops | bytes accessed | tf_op | source)
XLA Modules:
  0.0 2888.7 jit_solution(18071656655110703599)
XLA Ops:
  14.9 23.4 all_gather.63
  39.5 28.3 all-gather.16.cloned.1.call-done
  133.5 95.5 %all-gather.20.cloned.1.call-done = bf16[1536,4608]{1,0:T(8,128)(2,1)} async-done(((bf16[96,4608]{1,0:T(8,128)(2,1)}), bf16[1536,4608]{1,0:T(8,128)(2,1)}) %all-gather.20.cloned.1.call-update) | async-done | bytes 14155792 | tf_op jit(solution)/shard_map/all_gather | solution.py:84
  237.4 91.3 %all-gather.22.cloned.1.call-done = bf16[1536,4608]{1,0:T(8,128)(2,1)} async-done(((bf16[96,4608]{1,0:T(8,128)(2,1)}), bf16[1536,4608]{1,0:T(8,128)(2,1)}) %all-gather.22.cloned.1.call-update) | async-done | bytes 14155792 | tf_op jit(solution)/shard_map/all_gather | solution.py:85
  338.8 89.6 %all-gather.24.cloned.1.call-done = bf16[4608,1536]{1,0:T(8,128)(2,1)} async-done(((bf16[288,1536]{1,0:T(8,128)(2,1)}), bf16[4608,1536]{1,0:T(8,128)(2,1)}) %all-gather.24.cloned.1.call-update) | async-done | bytes 14155792 | tf_op jit(solution)/shard_map/all_gather | solution.py:86
  436.4 55.0 %all-gather.26.cloned.1.call-done = bf16[1536,2048]{1,0:T(8,128)(2,1)} async-done(((bf16[96,2048]{1,0:T(8,128)(2,1)}), bf16[1536,2048]{1,0:T(8,128)(2,1)}) %all-gather.26.cloned.1.call-update) | async-done | bytes 6291472 | tf_op jit(solution)/shard_map/all_gather | solution.py:81
  701.4 24.7 all-gather.1
  738.0 22.0 all-gather
  832.9 91.5 %all-gather.36.cloned.1.call-done = bf16[4608,1536]{1,0:T(8,128)(2,1)} async-done(((bf16[288,1536]{1,0:T(8,128)(2,1)}), bf16[4608,1536]{1,0:T(8,128)(2,1)}) %all-gather.36.cloned.1.call-update) | async-done | bytes 14155792 | tf_op jit(solution)/shard_map/all_gather | solution.py:86
  1487.7 43.3 %reduce-scatter.13.cloned.1.call-done = bf16[96,1536]{1,0:T(8,128)(2,1)} async-done(((bf16[1536,1536]{1,0:T(8,128)(2,1)}), bf16[96,1536]{1,0:T(8,128)(2,1)}) %reduce-scatter.13.cloned.1.call-update) | async-done | bytes 294928 | tf_op jit(solution)/shard_map/reduce_scatter | solution.py:92
  1531.0 84.5 %reduce-scatter.29.cloned.1.call-done = bf16[128,1536]{1,0:T(8,128)(2,1)} async-done(((bf16[2048,1536]{1,0:T(8,128)(2,1)}), bf16[128,1536]{1,0:T(8,128)(2,1)}) %reduce-scatter.29.cloned.1.call-update) | async-done | bytes 393232 | tf_op jit(solution)/shard_map/reduce_scatter | solution.py:104
  1615.4 84.0 %reduce-scatter.27.cloned.1.call-done = bf16[96,2048]{1,0:T(8,128)(2,1)} async-done(((bf16[1536,2048]{1,0:T(8,128)(2,1)}), bf16[96,2048]{1,0:T(8,128)(2,1)}) %reduce-scatter.27.cloned.1.call-update) | async-done | bytes 393232 | tf_op jit(solution)/shard_map/reduce_scatter | solution.py:98
  1699.4 84.2 %reduce-scatter.25.cloned.1.call-done = bf16[96,2048]{1,0:T(8,128)(2,1)} async-done(((bf16[1536,2048]{1,0:T(8,128)(2,1)}), bf16[96,2048]{1,0:T(8,128)(2,1)}) %reduce-scatter.25.cloned.1.call-update) | async-done | bytes 393232 | tf_op jit(solution)/shard_map/reduce_scatter | solution.py:92
  1783.7 103.4 %reduce-scatter.31.cloned.1.call-done = bf16[96,4608]{1,0:T(8,128)(2,1)} async-done(((bf16[1536,4608]{1,0:T(8,128)(2,1)}), bf16[96,4608]{1,0:T(8,128)(2,1)}) %reduce-scatter.31.cloned.1.call-update) | async-done | bytes 884752 | tf_op jit(solution)/shard_map/reduce_scatter | solution.py:92
  1887.0 102.3 %reduce-scatter.33.cloned.1.call-done = bf16[96,4608]{1,0:T(8,128)(2,1)} async-done(((bf16[1536,4608]{1,0:T(8,128)(2,1)}), bf16[96,4608]{1,0:T(8,128)(2,1)}) %reduce-scatter.33.cloned.1.call-update) | async-done | bytes 884752 | tf_op jit(solution)/shard_map/reduce_scatter | solution.py:98
  1989.3 102.0 %reduce-scatter.35.cloned.1.call-done = bf16[288,1536]{1,0:T(8,128)(2,1)} async-done(((bf16[4608,1536]{1,0:T(8,128)(2,1)}), bf16[288,1536]{1,0:T(8,128)(2,1)}) %reduce-scatter.35.cloned.1.call-update) | async-done | bytes 884752 | tf_op jit(solution)/shard_map/reduce_scatter | solution.py:104
  2091.3 102.3 %reduce-scatter.23.cloned.1.call-done = bf16[288,1536]{1,0:T(8,128)(2,1)} async-done(((bf16[4608,1536]{1,0:T(8,128)(2,1)}), bf16[288,1536]{1,0:T(8,128)(2,1)}) %reduce-scatter.23.cloned.1.call-update) | async-done | bytes 884752 | tf_op jit(solution)/shard_map/reduce_scatter | solution.py:104
  2193.6 102.2 %reduce-scatter.19.cloned.1.call-done = bf16[96,4608]{1,0:T(8,128)(2,1)} async-done(((bf16[1536,4608]{1,0:T(8,128)(2,1)}), bf16[96,4608]{1,0:T(8,128)(2,1)}) %reduce-scatter.19.cloned.1.call-update) | async-done | bytes 884752 | tf_op jit(solution)/shard_map/reduce_scatter | solution.py:92
  2295.8 102.5 %reduce-scatter.21.cloned.1.call-done = bf16[96,4608]{1,0:T(8,128)(2,1)} async-done(((bf16[1536,4608]{1,0:T(8,128)(2,1)}), bf16[96,4608]{1,0:T(8,128)(2,1)}) %reduce-scatter.21.cloned.1.call-update) | async-done | bytes 884752 | tf_op jit(solution)/shard_map/reduce_scatter | solution.py:98
  2419.1 53.1 %reduce-scatter.15.cloned.1.call-done = bf16[96,256]{1,0:T(8,128)(2,1)} async-done(((bf16[1536,256]{1,0:T(8,128)(2,1)}), bf16[96,256]{1,0:T(8,128)(2,1)}) %reduce-scatter.15.cloned.1.call-update) | async-done | bytes 49168 | tf_op jit(solution)/shard_map/reduce_scatter | solution.py:98
  2472.2 25.0 psum.142
  2497.9 71.7 %all-reduce.82.cloned.1.call-done = (bf16[96,1536]{1,0:T(8,128)(2,1)}, bf16[96,1536]{1,0:T(8,128)(2,1)}, bf16[96,4608]{1,0:T(8,128)(2,1)}, bf16[96,4608]{1,0:T(8...) async-done(((bf16[96,1536]{1,0:T(8,128)(2,1)}, ...) | async-done | bytes 7077904 | tf_op jit(solution)/shard_map/psum | solution.py:112
  2583.7 134.1 %all-reduce.78.cloned.1.call-done = (f32[1536]{0:T(1024)}, f32[1536]{0:T(1024)}, f32[1536]{0:T(1024)}, f32[4,2048]{1,0:T(4,128)}, f32[2048]{0:T(1024)}, /*index=5*/f32[1536]{0:T(1024)}) async-done(((f32[1536]{0:T(1024)}, f32[1536]{0:T(1024)}, f32[1536]{0:T(1024)}, f32[4,2048]{1,0:T(4,128)}, f32[2048]{0:T(1024)}, /*index=5*/f32[1536]{0:T(1024)}), (f32[1536]{0:T(1024)}, f32[1536]{0:T(1024)}, f32[1536]{0:T(1024)}, ...) | async-done | bytes 65552 | tf_op jit(solution)/shard_map/psum | solution.py:422
  2717.8 154.3 %all-reduce.80.cloned.1.call-done = (f32[16,128,128]{2,1,0:T(8,128)}, f32[16,128,128]{2,1,0:T(8,128)}) async-done(((f32[16,128,128]{2,1,0:T(8,128)}, f32[16,128,128]{2,1,0:T(8,128)}), (f32[16,128,128]{2,1,0:T(8,128)}, f32[16,128,128]{2,1,0:T(8,128)})) %all-reduce.80.cloned.1.call-update) | async-done | bytes 2097168 | tf_op jit(solution)/shard_map/psum | solution.py:422
  (818 shorter events, 1007.5 us)
Async XLA Ops:
  8.7 220.2 %all-gather.20.cloned.1.call-start = ((), (), s32[]{:S(2)}) async-start(), calls=%async_computation.22 | async-start | bytes 15040512 | tf_op jit(solution)/shard_map/all_gather | solution.py:84
  9.4 319.2 %all-gather.22.cloned.1.call-start = ((), (), s32[]{:S(2)}) async-start(), calls=%async_computation.23 | async-start | bytes 15040512 | tf_op jit(solution)/shard_map/all_gather | solution.py:85
  10.0 418.4 %all-gather.24.cloned.1.call-start = ((), (), s32[]{:S(2)}) async-start(), calls=%async_computation.24 | async-start | bytes 15040512 | tf_op jit(solution)/shard_map/all_gather | solution.py:86
  10.6 480.8 %all-gather.26.cloned.1.call-start = ((), (), s32[]{:S(2)}) async-start(), calls=%async_computation.25 | async-start | bytes 6684672 | tf_op jit(solution)/shard_map/all_gather | solution.py:81
  11.2 772.3 %all-gather.28.cloned.1.call-start = ((), (), s32[]{:S(2)}) async-start(), calls=%async_computation.26 | async-start | bytes 6684672 | tf_op jit(solution)/shard_map/all_gather | solution.py:82
  11.9 777.3 %all-gather.30.cloned.1.call-start = ((), (), s32[]{:S(2)}) async-start(), calls=%async_computation.27 | async-start | bytes 6684672 | tf_op jit(solution)/shard_map/all_gather | solution.py:83
  12.7 782.6 %all-gather.32.cloned.1.call-start = ((), (), s32[]{:S(2)}) async-start(), calls=%async_computation.28 | async-start | bytes 15040512 | tf_op jit(solution)/shard_map/all_gather | solution.py:84
  13.4 810.9 %all-gather.34.cloned.1.call-start = ((), (), s32[]{:S(2)}) async-start(), calls=%async_computation.29 | async-start | bytes 15040512 | tf_op jit(solution)/shard_map/all_gather | solution.py:85
  14.0 910.4 %all-gather.36.cloned.1.call-start = ((), (), s32[]{:S(2)}) async-start(), calls=%async_computation.30 | async-start | bytes 15040512 | tf_op jit(solution)/shard_map/all_gather | solution.py:86
  972.1 515.6 %reduce-scatter.17.cloned.1.call-start = ((), (), s32[]{:S(2)}) async-start(), calls=%async_computation.33 | async-start | bytes 5013504 | tf_op jit(solution)/shard_map/reduce_scatter | solution.py:104
  1353.5 177.5 %reduce-scatter.13.cloned.1.call-start = ((), (), s32[]{:S(2)}) async-start(), calls=%async_computation.31 | async-start | bytes 5013504 | tf_op jit(solution)/shard_map/reduce_scatter | solution.py:92
  1415.3 200.1 %reduce-scatter.29.cloned.1.call-start = ((), (), s32[]{:S(2)}) async-start(), calls=%async_computation.39 | async-start | bytes 6684672 | tf_op jit(solution)/shard_map/reduce_scatter | solution.py:104
  1421.0 278.4 %reduce-scatter.27.cloned.1.call-start = ((), (), s32[]{:S(2)}) async-start(), calls=%async_computation.38 | async-start | bytes 6684672 | tf_op jit(solution)/shard_map/reduce_scatter | solution.py:98
  1426.7 357.0 %reduce-scatter.25.cloned.1.call-start = ((), (), s32[]{:S(2)}) async-start(), calls=%async_computation.37 | async-start | bytes 6684672 | tf_op jit(solution)/shard_map/reduce_scatter | solution.py:92
  1432.2 454.9 %reduce-scatter.31.cloned.1.call-start = ((), (), s32[]{:S(2)}) async-start(), calls=%async_computation.40 | async-start | bytes 15040512 | tf_op jit(solution)/shard_map/reduce_scatter | solution.py:92
  1441.5 547.8 %reduce-scatter.33.cloned.1.call-start = ((), (), s32[]{:S(2)}) async-start(), calls=%async_computation.41 | async-start | bytes 15040512 | tf_op jit(solution)/shard_map/reduce_scatter | solution.py:98
  1450.0 641.3 %reduce-scatter.35.cloned.1.call-start = ((), (), s32[]{:S(2)}) async-start(), calls=%async_computation.42 | async-start | bytes 15040512 | tf_op jit(solution)/shard_map/reduce_scatter | solution.py:104
  1458.6 735.1 %reduce-scatter.23.cloned.1.call-start = ((), (), s32[]{:S(2)}) async-start(), calls=%async_computation.36 | async-start | bytes 15040512 | tf_op jit(solution)/shard_map/reduce_scatter | solution.py:104
  1467.1 828.7 %reduce-scatter.19.cloned.1.call-start = ((), (), s32[]{:S(2)}) async-start(), calls=%async_computation.34 | async-start | bytes 15040512 | tf_op jit(solution)/shard_map/reduce_scatter | solution.py:92
  1476.6 921.7 %reduce-scatter.21.cloned.1.call-start = ((), (), s32[]{:S(2)}) async-start(), calls=%async_computation.35 | async-start | bytes 15040512 | tf_op jit(solution)/shard_map/reduce_scatter | solution.py:98
  1485.2 987.0 %reduce-scatter.15.cloned.1.call-start = ((), (), s32[]{:S(2)}) async-start(), calls=%async_computation.32 | async-start | bytes 835584 | tf_op jit(solution)/shard_map/reduce_scatter | solution.py:98
  1487.6 1081.9 %all-reduce.82.cloned.1.call-start = ((), (), s32[]{:S(2)}) async-start(), calls=%async_computation.45 | async-start | bytes 14155776 | tf_op jit(solution)/shard_map/psum | solution.py:112
  2398.4 319.4 %all-reduce.78.cloned.1.call-start = ((), (), s32[]{:S(2)}) async-start(), calls=%async_computation.43 | async-start | bytes 147456 | tf_op jit(solution)/shard_map/psum | solution.py:422
  2407.4 464.7 %all-reduce.80.cloned.1.call-start = ((), (), s32[]{:S(2)}) async-start(), calls=%async_computation.44 | async-start | bytes 4194304 | tf_op jit(solution)/shard_map/psum | solution.py:422
  (157 other events, 3605.7 us)
Sparse Core Ops, SparseCore 0:
  131.0 97.8 all-gather.19
  231.0 97.6 all-gather.21
  330.7 97.6 all-gather.23
  430.4 60.9 all-gather.25
  493.6 62.3 all-gather.27
  558.2 60.9 all-gather.29
  621.4 97.7 all-gather.31
  721.3 103.0 all-gather.33
  826.5 97.8 all-gather.35
  1353.6 96.2 reduce-scatter.16
  1453.3 77.6 reduce-scatter.12
  1534.3 81.1 reduce-scatter.28
  1618.7 80.6 reduce-scatter.26
  1702.7 80.9 reduce-scatter.24
  1787.0 99.9 reduce-scatter.30
  1890.8 98.4 reduce-scatter.32
  1992.8 98.4 reduce-scatter.34
  2095.1 98.4 reduce-scatter.22
  2197.1 98.6 reduce-scatter.18
  2299.7 98.5 reduce-scatter.20
  2402.1 70.0 reduce-scatter.14
  2475.2 94.2 all-reduce.81
  2577.1 140.6 all-reduce.77
  2724.7 147.4 all-reduce.79
  (2 shorter events, 116.2 us)
where the time goes:
time: 2910 us; the launch traced here: 2890 us
  waiting for transfers between devices  1870 us (64%)
  local copies, waits for them, and re-layouts  372 us (13%)
  matrix products  260 us (9%)
  blocking collectives  170 us (6%)
  other arithmetic  159 us (5%)
  starting transfers between devices  41.6 us (1%)
    reduce_scatter x4, waiting for transfers between devices, reduce_three(): lax.psum_scatter(transposed_times(shared, second).astype(jnp.bfloat16), (...  342 us
    reduce_scatter x4, waiting for transfers between devices, reduce_three(): lax.psum_scatter(transposed_times(shared, first).astype(jnp.bfloat16), ('...  333 us
    reduce_scatter x4, waiting for transfers between devices, reduce_three(): lax.psum_scatter(transposed_times(other, third).astype(jnp.bfloat16), ('c...  289 us
    psum x2, waiting for transfers between devices, body(): lax.psum((grad_attend_gain, grad_lower_gain, grad_recur_gain, grad_upper_...  288 us
    all_gather x2, waiting for transfers between devices, collect(): lax.all_gather(sixth, ('ctx', 'fsdp'), axis=0, tiled=True)  181 us
    all_gather x2, waiting for transfers between devices, collect(): lax.all_gather(fifth, ('ctx', 'fsdp'), axis=0, tiled=True)  111 us
    slice x57, local copies, waits for them, and re-layouts, body(): lax.associative_scan(compose, (coefficient[::-1], state_grad_mix[::-1]),...  108 us
    all_gather x2, waiting for transfers between devices, collect(): lax.all_gather(fourth, ('ctx', 'fsdp'), axis=0, tiled=True)  95.5 us
  transfers between devices with their start and end apart: 41, of which 31 were waited for; matrix products, arithmetic and copies ran while one was open for 15% of the time, Pallas kernels for 0%

commit v1 on v0

v1 whole, which is shorter than its diff:
```python
import functools

import jax
import jax.numpy as jnp
from jax import lax
from jax.experimental import pallas as pl
from jax.experimental.pallas import tpu as pltpu
from jax.sharding import Mesh, PartitionSpec as P

WINDOW = 1024
EPSILON = 1e-06
DECAY_SCALE = 8.0

X = ("xh", "xl")
ZN = 4
F32 = jnp.float32
BF16 = jnp.bfloat16


def from_z(value, by):
    return lax.ppermute(value, "z", [((i + by) % ZN, i) for i in range(ZN)])


def to_z(value, by):
    return lax.ppermute(value, "z", [(i, (i + by) % ZN) for i in range(ZN)])


def swap(value):
    return lax.ppermute(value, "c", [(0, 1), (1, 0)])


def transpose_xz(value):
    pairs = [(x * ZN + z, z * ZN + x) for x in range(4) for z in range(ZN)]
    return lax.ppermute(value, ("xh", "xl", "z"), pairs)


def exchange_z(value):
    z = lax.axis_index("z")
    out = jnp.zeros_like(value)
    for r in range(ZN):
        piece = lax.dynamic_index_in_dim(value, (z + r) % ZN, 0, keepdims=True)
        if r:
            piece = to_z(piece, r)
        out = lax.dynamic_update_slice_in_dim(out, piece, (z + ZN - r) % ZN, 0)
    return out


def by_core(mine, other):
    first = lax.axis_index("c") == 0
    return jnp.where(first, mine, other), jnp.where(first, other, mine)


def core_pick(zero, one):
    return jnp.where(lax.axis_index("c") == 0, zero, one)


def core_join(mine, other):
    return jnp.concatenate(by_core(mine, other), axis=-1)


def normalize(values, gain):
    return values * lax.rsqrt(jnp.mean(values * values, axis=-1, keepdims=True) + EPSILON) * gain


def smooth_gelu(values):
    return jax.nn.gelu(values, approximate=True)


def gated_unit(gate_pre, lift_pre):
    return smooth_gelu(gate_pre) * lift_pre


def branch_merge(states, branch_y):
    return states * smooth_gelu(branch_y)


def gate_terms(pre_decay, pre_admit, conv_out, decay_rate):
    retain = jax.nn.sigmoid(pre_decay)
    admit = jax.nn.sigmoid(pre_admit)
    log_decay = -DECAY_SCALE * jax.nn.softplus(decay_rate) * (0.25 + retain)
    return (jnp.exp(log_decay), jnp.sqrt(-jnp.expm1(2.0 * log_decay)) * admit * conv_out)


def matmul(left, right):
    return jnp.dot(left, right, preferred_element_type=F32)


def times_transposed(left, right):
    return lax.dot_general(left, right, (((1,), (1,)), ((), ())), preferred_element_type=F32)


def transposed_times(left, right):
    return lax.dot_general(left, right, (((0,), (0,)), ((), ())), preferred_element_type=F32)


def gather_z(low):
    return [low] + [from_z(low, r) for r in range(1, ZN)]


def gather_rows(low):
    mine = gather_z(low)
    return jnp.concatenate(mine + [swap(block) for block in mine], axis=0)


def scatter_z(part):
    rows = part.shape[0] // ZN
    total = part[:rows].astype(F32)
    for r in range(1, ZN):
        total = total + to_z(part[r * rows : (r + 1) * rows].astype(BF16), r).astype(F32)
    return total


def scatter_rows(part):
    half = part.shape[0] // 2
    return scatter_z(part[:half] + swap(part[half:].astype(BF16)).astype(F32))


def kv_places(rows):
    places = []
    for x in range(4):
        for z in range(ZN):
            for j in range(2):
                position = ((x % 2) * ZN + 2 * (z // 2) + j) * 2 + x // 2
                places.append((x * ZN + z, j, z % 2, WINDOW + position * rows))
    return places


def attend_scores(pos_ref, q_ref, key_s, scale):
    rows, size = q_ref.shape[1], key_s.shape[1]
    heads = q_ref.shape[2] // size
    start = pl.multiple_of(pos_ref[pl.program_id(0)] * rows, rows)
    query = q_ref[0]
    query = jnp.concatenate([query[:, h * size : (h + 1) * size] for h in range(heads)], axis=0)
    key = key_s[pl.ds(start, WINDOW + rows), :]
    scores = times_transposed(query, key) * scale
    row = lax.broadcasted_iota(jnp.int32, scores.shape, 0) % rows
    col = lax.broadcasted_iota(jnp.int32, scores.shape, 1)
    allowed = (col > row) & (col <= row + WINDOW) & (col >= WINDOW - start)
    return start, query, key, jnp.where(allowed, scores, -1e30)


def load_kv(kv_ref, key_s, value_s):
    rows = kv_ref.shape[2]
    key_s[:WINDOW, :] = jnp.zeros((WINDOW, key_s.shape[1]), key_s.dtype)
    value_s[:WINDOW, :] = jnp.zeros((WINDOW, key_s.shape[1]), key_s.dtype)
    for source, j, kind, first in kv_places(rows):
        (value_s if kind else key_s)[first : first + rows, :] = kv_ref[source, j]


def attend_forward_kernel(scale, pos_ref, q_ref, kv_ref, out_ref, lse_ref, key_s, value_s):
    rows, size = q_ref.shape[1], key_s.shape[1]

    @pl.when(pl.program_id(0) == 0)
    def _():
        load_kv(kv_ref, key_s, value_s)

    start, query, key, scores = attend_scores(pos_ref, q_ref, key_s, scale)
    highest = jnp.max(scores, axis=-1, keepdims=True)
    lse = highest + jnp.log(jnp.sum(jnp.exp(scores - highest), axis=-1, keepdims=True))
    probs = jnp.exp(scores - lse).astype(BF16)
    mixed = matmul(probs, value_s[pl.ds(start, WINDOW + rows), :]).astype(BF16)
    out_ref[0] = jnp.concatenate(
        [mixed[h * rows : (h + 1) * rows] for h in range(q_ref.shape[2] // size)], axis=1
    )
    lse_ref[0] = lse


def attend_backward_kernel(
    scale, pos_ref, q_ref, kv_ref, grad_ref, lse_ref, dq_ref, dkv_ref, key_s, value_s, dk_s, dv_s
):
    rows, size = q_ref.shape[1], key_s.shape[1]
    heads = q_ref.shape[2] // size

    @pl.when(pl.program_id(0) == 0)
    def _():
        load_kv(kv_ref, key_s, value_s)
        dk_s[...] = jnp.zeros_like(dk_s)
        dv_s[...] = jnp.zeros_like(dv_s)

    start, query, key, scores = attend_scores(pos_ref, q_ref, key_s, scale)
    span = pl.ds(start, WINDOW + rows)
    probs = jnp.exp(scores - lse_ref[0])
    grad = grad_ref[0]
    grad = jnp.concatenate([grad[:, h * size : (h + 1) * size] for h in range(heads)], axis=0)
    prob_grad = times_transposed(grad, value_s[span, :])
    delta = jnp.sum(probs * prob_grad, axis=-1, keepdims=True)
    score_grad = (probs * (prob_grad - delta)).astype(BF16)
    query_grad = (matmul(score_grad, key) * scale).astype(BF16)
    dq_ref[0] = jnp.concatenate(
        [query_grad[h * rows : (h + 1) * rows] for h in range(heads)], axis=1
    )
    dk_s[span, :] += transposed_times(score_grad, query) * scale
    dv_s[span, :] += transposed_times(probs.astype(BF16), grad)

    @pl.when(pl.program_id(0) == pl.num_programs(0) - 1)
    def _():
        for source, j, kind, first in kv_places(rows):
            dkv_ref[source, j] = (dv_s if kind else dk_s)[first : first + rows, :].astype(BF16)


def whole(array):
    return pl.BlockSpec(array.shape, lambda r: (0,) * len(array.shape))


def by_block(*shape):
    return pl.BlockSpec((1,) + shape, lambda r: (r, 0, 0))


def kv_scratch(kv, dtype):
    return pltpu.VMEM((WINDOW + 16 * kv.shape[2], kv.shape[3]), dtype)


def attend_forward(positions, query, kv):
    blocks, rows, width = query.shape
    size = kv.shape[3]
    stacked = rows * (width // size)
    return pl.pallas_call(
        functools.partial(attend_forward_kernel, size**-0.5),
        grid=(blocks,),
        in_specs=[pl.BlockSpec(memory_space=pltpu.SMEM), by_block(rows, width), whole(kv)],
        out_specs=[by_block(rows, width), by_block(stacked, 1)],
        out_shape=[
            jax.ShapeDtypeStruct(query.shape, BF16),
            jax.ShapeDtypeStruct((blocks, stacked, 1), F32),
        ],
        scratch_shapes=[kv_scratch(kv, BF16), kv_scratch(kv, BF16)],
        compiler_params=pltpu.CompilerParams(vmem_limit_bytes=40 << 20),
    )(positions, query, kv)


def attend_backward(positions, query, kv, grad, lse):
    blocks, rows, width = query.shape
    size = kv.shape[3]
    stacked = rows * (width // size)
    return pl.pallas_call(
        functools.partial(attend_backward_kernel, size**-0.5),
        grid=(blocks,),
        in_specs=[
            pl.BlockSpec(memory_space=pltpu.SMEM),
            by_block(rows, width),
            whole(kv),
            by_block(rows, width),
            by_block(stacked, 1),
        ],
        out_specs=[by_block(rows, width), whole(kv)],
        out_shape=[
            jax.ShapeDtypeStruct(query.shape, BF16),
            jax.ShapeDtypeStruct(kv.shape, BF16),
        ],
        scratch_shapes=[
            kv_scratch(kv, BF16),
            kv_scratch(kv, BF16),
            kv_scratch(kv, F32),
            kv_scratch(kv, F32),
        ],
        compiler_params=pltpu.CompilerParams(vmem_limit_bytes=40 << 20),
    )(positions, query, kv, grad, lse)


def scan_kernel(backward, factor_ref, update_ref, state_ref):
    tiles = factor_ref.shape[0] // 8
    width = factor_ref.shape[1]
    row = lax.broadcasted_iota(jnp.int32, (8, width), 0)

    def turn(index, carry):
        tile = tiles - 1 - index if backward else index
        span = pl.ds(pl.multiple_of(tile * 8, 8), 8)
        factor, update = factor_ref[span, :], update_ref[span, :]
        for reach in (1, 2, 4):
            shift = 8 - reach if backward else reach
            inside = row < 8 - reach if backward else row >= reach
            far_update = pltpu.roll(update, shift, 0)
            far_factor = pltpu.roll(factor, shift, 0)
            update = jnp.where(inside, factor * far_update + update, update)
            factor = jnp.where(inside, factor * far_factor, factor)
        state = factor * carry + update
        state_ref[span, :] = state
        last = state[0:1] if backward else state[7:8]
        return jnp.broadcast_to(last, (8, width))

    lax.fori_loop(0, tiles, turn, jnp.zeros((8, width), F32), unroll=8)


def linear_scan(factors, updates, backward):
    return pl.pallas_call(
        functools.partial(scan_kernel, backward),
        out_shape=jax.ShapeDtypeStruct(factors.shape, F32),
        compiler_params=pltpu.CompilerParams(vmem_limit_bytes=24 << 20),
    )(factors, updates)


def to_sequence(part, blocks):
    rows = part.shape[0] // 8
    width = part.shape[1] // blocks
    z = lax.axis_index("z")
    sent = part.reshape(2, ZN, rows, blocks, width).transpose(0, 3, 1, 2, 4)
    got = lax.all_to_all(sent.reshape(4, ZN, rows, width), X, 0, 0)
    got = jnp.roll(got, z, axis=1).reshape(2, 2, ZN, rows, width)
    return got.transpose(1, 2, 0, 3, 4).reshape(16 * rows, width)


def from_sequence(values, blocks):
    rows, width = values.shape[0] // 16, values.shape[1]
    z = lax.axis_index("z")
    sent = values.reshape(2, ZN, 2, rows, width).transpose(2, 0, 1, 3, 4)
    sent = jnp.roll(sent.reshape(4, ZN, rows, width), -z, axis=1)
    got = lax.all_to_all(sent, X, 0, 0).reshape(2, blocks, ZN, rows, width)
    return got.transpose(0, 2, 3, 1, 4).reshape(8 * rows, blocks * width)


def shift_down(values, by):
    if by == 0:
        return values
    return jnp.concatenate([jnp.zeros_like(values[:by]), values[:-by]], axis=0)


def shift_up(values, by):
    if by == 0:
        return values
    return jnp.concatenate([values[by:], jnp.zeros_like(values[:by])], axis=0)


def unit_slices(weight):
    quarter = weight.shape[1] // ZN
    wide = quarter * 5 // 9
    skip = quarter - wide
    keep = lax.broadcasted_iota(jnp.int32, (weight.shape[0], wide), 1) >= wide - skip
    picked = []
    for member in range(ZN):
        columns = weight[:, member * quarter : (member + 1) * quarter]
        picked.append(core_pick(columns[:, :wide], jnp.where(keep, columns[:, skip:], 0)))
    return jnp.stack(picked)


def half_slices(weight):
    quarter = weight.shape[1] // ZN
    half = quarter // 2
    picked = []
    for member in range(ZN):
        columns = weight[:, member * quarter : (member + 1) * quarter]
        picked.append(core_pick(columns[:, :half], columns[:, half:]))
    return jnp.stack(picked)


def own_half(weight):
    half = weight.shape[-1] // 2
    return core_pick(weight[..., :half], weight[..., half:])


def other_half(weight):
    half = weight.shape[-1] // 2
    return core_pick(weight[..., half:], weight[..., :half])


def gather_x(value):
    return lax.all_gather(value, X, axis=0, tiled=True)


def columns_of(picked):
    turned = exchange_z(picked)
    return gather_x(turned.reshape(-1, turned.shape[2]))


def core_rows(stacked, wide):
    skip = stacked.shape[0] - wide
    low, high = stacked[:wide], stacked[skip:]
    return core_join(core_pick(low, high), swap(core_pick(high, low)))


def reduce_columns(grad):
    part = lax.psum_scatter(grad.astype(BF16), X, scatter_dimension=0, tiled=True)
    part = lax.psum(part, "y")
    return exchange_z(part.reshape(ZN, part.shape[0] // ZN, part.shape[1]))


def reduce_rows(grad):
    part = lax.psum_scatter(grad.astype(BF16), X, scatter_dimension=0, tiled=True)
    part = transpose_xz(lax.psum(part, "y"))
    return core_join(part, swap(part)).astype(F32)


def unit_grads(grad):
    mine = reduce_columns(grad)
    zero, one = by_core(mine, swap(mine))
    wide = grad.shape[1] // 2
    skip = wide * 4 // 5
    gates, lifts = [], []
    for member in range(ZN):
        for out, first in ((gates, 0), (lifts, wide)):
            out.append(zero[member, :, first : first + wide])
            out.append(one[member, :, first + wide - skip : first + wide])
    return (
        jnp.concatenate(gates, axis=1).astype(F32),
        jnp.concatenate(lifts, axis=1).astype(F32),
    )


def half_grads(grad):
    mine = reduce_columns(grad)
    zero, one = by_core(mine, swap(mine))
    half = grad.shape[1] // 2
    outs = []
    for first in (0, half):
        pieces = []
        for member in range(ZN):
            pieces.append(zero[member, :, first : first + half])
            pieces.append(one[member, :, first : first + half])
        outs.append(jnp.concatenate(pieces, axis=1).astype(F32))
    return outs


def member_rows(grad, wide):
    low = grad.astype(BF16)
    zero, one = by_core(own_half(low), swap(other_half(low)))
    return jnp.concatenate([zero, one[zero.shape[0] - wide :]], axis=0)


def dense_forward(residual, gain, unit_weight, drop_weight):
    normed, norm_pull = jax.vjp(normalize, residual, gain)
    rows = gather_rows(normed.astype(BF16))
    pre = matmul(rows, unit_weight)
    wide = pre.shape[1] // 2
    hidden, unit_pull = jax.vjp(gated_unit, pre[:, :wide], pre[:, wide:])
    hidden_low = hidden.astype(BF16)
    out = residual + scatter_rows(matmul(hidden_low, drop_weight))
    return out, (norm_pull, rows, unit_pull, hidden_low)


def dense_backward(residual_grad, stored, unit_weight, drop_weight):
    norm_pull, rows, unit_pull, hidden_low = stored
    grad_rows = gather_rows(residual_grad.astype(BF16))
    hidden_grad = times_transposed(grad_rows, drop_weight)
    pre_low = jnp.concatenate([part.astype(BF16) for part in unit_pull(hidden_grad)], axis=1)
    normed_grad = scatter_rows(times_transposed(pre_low, unit_weight))
    input_grad, gain_grad = norm_pull(normed_grad)
    unit_grad = transposed_times(rows, pre_low)
    drop_grad = transposed_times(hidden_low, grad_rows)
    wide = drop_grad.shape[0]
    gate_grad, lift_grad = unit_grads(unit_grad)
    drop_grad = reduce_rows(member_rows(drop_grad, wide * 4 // 5))
    return residual_grad + input_grad, gain_grad, (gate_grad, lift_grad, drop_grad)


def body(
    tokens,
    lengths,
    cotangent,
    attend_gain,
    query_weight,
    keyval_weight,
    attend_output,
    lower_gain,
    lower_gate,
    lower_lift,
    lower_drop,
    recur_gain,
    recur_input,
    recur_branch,
    recur_output,
    temporal_kernel,
    decay_gate,
    input_gate,
    decay_rate,
    upper_gain,
    upper_gate,
    upper_lift,
    upper_drop,
):
    c, xh, xl, z = (lax.axis_index(name) for name in ("c", "xh", "xl", "z"))
    row_count, features = tokens.shape[1:]
    size = keyval_weight.shape[1] // 2
    query_width = query_weight.shape[1] // ZN
    drop_rows, recur_rows = lower_drop.shape[0], recur_output.shape[0]
    channels = 2 * recur_rows
    tap_count = temporal_kernel.shape[0]
    even = z % 2 == 0
    positions = ((xl * ZN + (z + jnp.arange(ZN, dtype=jnp.int32)) % ZN) * 2 + xh).astype(jnp.int32)
    token_pos = positions[0] * row_count + jnp.arange(row_count, dtype=jnp.int32)
    valid = (token_pos < lengths[0]).astype(F32)[:, None]

    member_query = query_weight.reshape(-1, ZN, query_width).transpose(1, 0, 2)
    member_kv = jnp.stack([keyval_weight[:, (m % 2) * size : (m % 2 + 1) * size] for m in range(ZN)])
    attend_columns = jnp.concatenate([member_query, member_kv], axis=2)
    half_in = columns_of(own_half(attend_columns))
    half_out = gather_x(transpose_xz(own_half(attend_output)))
    attend_in = core_join(half_in, swap(half_in))
    attend_out = core_join(half_out, swap(half_out))

    lower_unit = columns_of(
        jnp.concatenate([unit_slices(lower_gate), unit_slices(lower_lift)], axis=2)
    )
    upper_columns = columns_of(
        jnp.concatenate(
            [
                unit_slices(upper_gate),
                unit_slices(upper_lift),
                half_slices(recur_input),
                half_slices(recur_branch),
            ],
            axis=2,
        )
    )
    unit_width = lower_unit.shape[1]
    wide = unit_width // 2
    upper_unit = upper_columns[:, :unit_width]
    recur_in = upper_columns[:, unit_width:]
    drops = transpose_xz(
        own_half(jnp.concatenate([lower_drop, recur_output, upper_drop], axis=0))
    )
    drops = lax.all_gather(drops, X, axis=0, tiled=False)
    half_width = features // 2
    lower_down = core_rows(drops[:, :drop_rows].reshape(-1, half_width), wide)
    recur_out = core_rows(
        drops[:, drop_rows : drop_rows + recur_rows].reshape(-1, half_width), channels
    )
    upper_down = core_rows(drops[:, drop_rows + recur_rows :].reshape(-1, half_width), wide)

    start_rows = tokens[0].astype(F32)
    normed_attend, attend_pull = jax.vjp(normalize, start_rows, attend_gain)
    attend_rows = jnp.concatenate(gather_z(normed_attend.astype(BF16)), axis=0)
    mixed_in = matmul(attend_rows, attend_in).astype(BF16).reshape(ZN, row_count, -1)
    queries = mixed_in[:, :, :query_width]
    kv_part = mixed_in[:, :, query_width:]
    kv_send = jnp.stack(
        [jnp.where(even, kv_part[0], kv_part[3]), jnp.where(even, kv_part[1], kv_part[0])]
    )
    kv = lax.all_to_all(
        jnp.broadcast_to(kv_send[None], (16,) + kv_send.shape), X + ("z",), 0, 0
    )
    attended, log_total = attend_forward(positions, queries, kv)
    attend_back = attended.reshape(ZN * row_count, query_width)
    first_rows = start_rows + scatter_z(matmul(attend_back, attend_out))

    second_rows, lower_kept = dense_forward(first_rows, lower_gain, lower_unit, lower_down)

    normed_recur, recur_pull = jax.vjp(normalize, second_rows, recur_gain)
    recur_low_rows = gather_rows(normed_recur.astype(BF16))
    branches = matmul(recur_low_rows, recur_in)
    branch_y = branches[:, channels:]
    x_seq = to_sequence(branches[:, :channels].astype(BF16), 2).astype(F32)
    block = (z * 2 + c) * 2 + xl
    width = decay_gate.shape[1]
    own_decay = lax.dynamic_slice_in_dim(decay_rate, block * width, width, 0)
    own_taps = lax.dynamic_slice_in_dim(temporal_kernel, block * width, width, 1)
    own_decay_gate = lax.dynamic_index_in_dim(decay_gate, block, 0, keepdims=False)
    own_input_gate = lax.dynamic_index_in_dim(input_gate, block, 0, keepdims=False)
    shifted = [shift_down(x_seq, k) for k in range(tap_count)]
    conv_out = sum(own_taps[k] * shifted[k] for k in range(tap_count))
    conv_low = conv_out.astype(BF16)
    pre_decay = matmul(conv_low, own_decay_gate)
    pre_admit = matmul(conv_low, own_input_gate)
    (factors, updates), gate_pull = jax.vjp(gate_terms, pre_decay, pre_admit, conv_out, own_decay)
    states = linear_scan(factors, updates, False)
    states_back = from_sequence(states.astype(BF16), 2)
    merged, merge_pull = jax.vjp(branch_merge, states_back.astype(F32), branch_y)
    merged_low = merged.astype(BF16)
    third_rows = second_rows + scatter_rows(matmul(merged_low, recur_out))

    fourth_rows, upper_kept = dense_forward(third_rows, upper_gain, upper_unit, upper_down)
    out_tokens = (fourth_rows * valid).astype(BF16)[None]

    residual_grad = cotangent[0].astype(F32) * valid
    residual_grad, grad_upper_gain, upper_grads = dense_backward(
        residual_grad, upper_kept, upper_unit, upper_down
    )

    recur_grad_rows = gather_rows(residual_grad.astype(BF16))
    merged_grad = times_transposed(recur_grad_rows, recur_out)
    states_grad, branch_y_grad = merge_pull(merged_grad)
    state_grad = to_sequence(states_grad.astype(BF16), 2).astype(F32)
    adjoint = linear_scan(shift_up(factors, 1), state_grad, True)
    decay_grad, admit_grad, conv_grad, own_decay_grad = gate_pull(
        (adjoint * shift_down(states, 1), adjoint)
    )
    decay_grad_low, admit_grad_low = decay_grad.astype(BF16), admit_grad.astype(BF16)
    conv_grad = (
        conv_grad
        + times_transposed(decay_grad_low, own_decay_gate)
        + times_transposed(admit_grad_low, own_input_gate)
    )
    own_gate_grad = transposed_times(conv_low, decay_grad_low)
    own_admit_grad = transposed_times(conv_low, admit_grad_low)
    tap_grads = jnp.stack([jnp.sum(conv_grad * shifted[k], axis=0) for k in range(tap_count)])
    x_seq_grad = sum(own_taps[k] * shift_up(conv_grad, k) for k in range(tap_count))
    branch_x_grad = from_sequence(x_seq_grad.astype(BF16), 2)
    branch_grad = jnp.concatenate([branch_x_grad, branch_y_grad.astype(BF16)], axis=1)
    normed_grad = scatter_rows(times_transposed(branch_grad, recur_in))
    recur_input_grad, grad_recur_gain = recur_pull(normed_grad)
    grad_recur_input, grad_recur_branch = half_grads(transposed_times(recur_low_rows, branch_grad))
    grad_recur_output = reduce_rows(
        member_rows(transposed_times(merged_low, recur_grad_rows), channels)
    )
    residual_grad = residual_grad + recur_input_grad
    channel_grads = jnp.concatenate(
        [
            own_gate_grad,
            own_admit_grad,
            tap_grads,
            own_decay_grad[None],
            jnp.zeros((3, width), F32),
        ],
        axis=0,
    )
    channel_grads = lax.all_gather(lax.psum(channel_grads, ("y", "xh")), ("z", "c", "xl"), axis=0)
    grad_decay_gate = channel_grads[:, :width]
    grad_input_gate = channel_grads[:, width : 2 * width]
    grad_temporal_kernel = (
        channel_grads[:, 2 * width : 2 * width + tap_count]
        .transpose(1, 0, 2)
        .reshape(tap_count, -1)
    )
    grad_decay_rate = channel_grads[:, 2 * width + tap_count].reshape(-1)

    residual_grad, grad_lower_gain, lower_grads = dense_backward(
        residual_grad, lower_kept, lower_unit, lower_down
    )

    grad_rows = jnp.concatenate(gather_z(residual_grad.astype(BF16)), axis=0)
    attend_grad = times_transposed(grad_rows, attend_out).astype(BF16)
    query_grad, kv_grad = attend_backward(
        positions, queries, kv, attend_grad.reshape(queries.shape), log_total
    )
    kv_grad = lax.all_to_all(kv_grad, X + ("z",), 0, 0)
    kv_grad = jnp.sum(kv_grad.astype(F32), axis=0).astype(BF16)
    nothing = jnp.zeros_like(kv_grad[0])
    kv_grad = jnp.stack(
        [
            jnp.where(even, kv_grad[0], kv_grad[1]),
            jnp.where(even, kv_grad[1], nothing),
            nothing,
            jnp.where(even, nothing, kv_grad[0]),
        ]
    )
    mixed_grad = jnp.concatenate([query_grad, kv_grad], axis=2).reshape(ZN * row_count, -1)
    normed_grad = scatter_z(times_transposed(mixed_grad, attend_in))
    in_grad = transposed_times(attend_rows, mixed_grad).astype(BF16)
    out_grad = transposed_times(attend_back, grad_rows).astype(BF16)
    in_grad = own_half(in_grad).astype(F32) + swap(other_half(in_grad)).astype(F32)
    out_grad = own_half(out_grad).astype(F32) + swap(other_half(out_grad)).astype(F32)
    grad_attend_output = reduce_rows(out_grad)
    in_grad = reduce_columns(in_grad)
    in_grad = core_join(in_grad, swap(in_grad)).astype(F32)
    grad_query_weight = jnp.concatenate([in_grad[m, :, :query_width] for m in range(ZN)], axis=1)
    grad_keyval_weight = jnp.concatenate(
        [in_grad[m, :, query_width:] + in_grad[m + 2, :, query_width:] for m in range(2)], axis=1
    )
    attend_input_grad, grad_attend_gain = attend_pull(normed_grad)
    residual_grad = residual_grad + attend_input_grad
    gains = lax.psum(
        jnp.stack([grad_attend_gain, grad_lower_gain, grad_recur_gain, grad_upper_gain]),
        ("y", "c", "xh", "xl", "z"),
    )
    return (
        out_tokens,
        residual_grad[None],
        gains[0],
        grad_query_weight,
        grad_keyval_weight,
        grad_attend_output,
        gains[1],
        *lower_grads,
        gains[2],
        grad_recur_input,
        grad_recur_branch,
        grad_recur_output,
        grad_temporal_kernel,
        grad_decay_gate,
        grad_input_gate,
        grad_decay_rate,
        gains[3],
        *upper_grads,
    )


def solution(mesh):
    grid = Mesh(mesh.devices.reshape(-1, 2, 2, 2, ZN), ("y", "c", "xh", "xl", "z"))
    rows = P(("y", "c"), ("xl", "z", "xh"), None)
    weight = P(("xh", "xl", "z"), None)
    same = P()
    return jax.shard_map(
        body,
        mesh=grid,
        in_specs=(
            (rows, P(("y", "c")), rows)
            + (same, weight, weight, weight)
            + (same, weight, weight, weight)
            + (same, weight, weight, weight, same, same, same, same)
            + (same, weight, weight, weight)
        ),
        out_specs=(
            (rows, rows)
            + (same, weight, weight, weight)
            + (same, weight, weight, weight)
            + (same, weight, weight, weight, same, same, same, same)
            + (same, weight, weight, weight)
        ),
        check_vma=False,
    )
```

time: 2910 us -> 1200 us (0.41)
  waiting for transfers between devices: 1870 us -> 511 us
  local copies, waits for them, and re-layouts: 372 us -> 81.1 us
  starting transfers between devices: 41.6 us -> 239 us
  matrix products: 260 us -> 93.5 us
  other arithmetic: 159 us -> 83.6 us
  blocking collectives: 170 us -> 134 us
    reduce_scatter x12 -> x8, waiting for transfers between devices: 964 us -> 128 us  [the longest x4 74.1 us: reduce_columns(): lax.psum_scatter(grad.astype(BF16), X, scatter_dimension=0, tiled=True)]
    all_gather x11 -> x4, waiting for transfers between devices: 490 us -> 49 us  [the longest x1 49 us: body(): lax.all_gather(lax.psum(channel_grads, ('y', 'xh')), ('z', 'c', 'xl'), ax...]
    psum x3 -> x2, waiting for transfers between devices: 360 us -> 0.02 us  [the longest x1 0.02 us: body(): lax.psum(channel_grads, ('y', 'xh'))]
    ppermute x10 -> x123, waiting for transfers between devices: 17.5 us -> 297 us  [the longest x45 220 us: to_z(): return lax.ppermute(value, 'z', [(i, (i + by) % ZN) for i in range(ZN)])]
    ppermute x10 -> x123, starting transfers between devices: 19.7 us -> 216 us  [the longest x24 79.3 us: from_z(): return lax.ppermute(value, 'z', [((i + by) % ZN, i) for i in range(ZN)])]
    slice x117 -> x24, local copies, waits for them, and re-layouts: 191 us -> 13.2 us  [the longest x1 3.44 us: body(): drops[:, drop_rows + recur_rows:].reshape(-1, half_width)]
    pad x56 -> x0, local copies, waits for them, and re-layouts: 107 us -> none  [the longest x28 53.6 us: body(): lax.associative_scan(compose, (coefficient[::-1], state_grad_mix[::-1]),...]
    all_gather x5 -> x2, blocking collectives: 114 us -> 36.7 us  [gather_x(): return lax.all_gather(value, X, axis=0, tiled=True)]
  transfers between devices with their start and end apart: 41 -> 142, of which waited for: 31 -> 66; matrix products, arithmetic and copies ran while one was open for 15% -> 18% of each run, Pallas kernels for 0% -> 1%
where the time goes in v1:
time: 1200 us; the launch traced here: 1180 us
  waiting for transfers between devices  511 us (43%)
  starting transfers between devices  239 us (20%)
  blocking collectives  134 us (11%)
  matrix products  93.5 us (8%)
  other arithmetic  83.6 us (7%)
  local copies, waits for them, and re-layouts  81.1 us (7%)
  between operations  18.1 us (2%)
  Pallas kernels  17.2 us (1%)
    ppermute x45, waiting for transfers between devices, to_z(): return lax.ppermute(value, 'z', [(i, (i + by) % ZN) for i in range(ZN)])  220 us
    ppermute x24, starting transfers between devices, from_z(): return lax.ppermute(value, 'z', [((i + by) % ZN, i) for i in range(ZN)])  79.3 us
    reduce_scatter x4, waiting for transfers between devices, reduce_columns(): lax.psum_scatter(grad.astype(BF16), X, scatter_dimension=0, tiled=True)  74.1 us
    psum x1, blocking collectives, body(): lax.psum(jnp.stack([grad_attend_gain, grad_lower_gain, grad_recur_gain, g...  68.8 us
    ppermute x45, starting transfers between devices, to_z(): return lax.ppermute(value, 'z', [(i, (i + by) % ZN) for i in range(ZN)])  65.8 us
    ppermute x24, waiting for transfers between devices, from_z(): return lax.ppermute(value, 'z', [((i + by) % ZN, i) for i in range(ZN)])  64.6 us
    ppermute x48, starting transfers between devices, swap(): return lax.ppermute(value, 'c', [(0, 1), (1, 0)])  63.9 us
    reduce_scatter x4, waiting for transfers between devices, reduce_rows(): lax.psum_scatter(grad.astype(BF16), X, scatter_dimension=0, tiled=True)  54 us
  transfers between devices with their start and end apart: 142, of which 66 were waited for; matrix products, arithmetic and copies ran while one was open for 18% of the time, Pallas kernels for 1%

profile of v1, /device:TPU:1, one launch (start us, length us, event | category | flops | bytes accessed | tf_op | source)
XLA Modules:
  0.0 1177.8 jit_solution(8350797351282237677)
XLA Ops:
  14.0 57.1 %collective-permute-start = (bf16[128,1536]{1,0:T(8,128)(2,1)}, bf16[128,1536]{1,0:T(8,128)(2,1)}, u32[]{:S(2)}, u32[]{:S(2)}) collective-permute-start(bf16[128,1536]{1,0:T(8,128)(2,1)} %fusion.48), channel_id=1, source_target_pairs={{1,0},{2,1},{3,2},{0,3},{5,4},{6,5},{7,6},{4,7},{9,8},{10,9},{11,1... | collective-permute-start | bytes 1179656 | tf_op jit(solution)/shard_map/ppermute | solution.py:21
  77.3 15.5 %collective-permute-done.3 = bf16[1,96,256]{2,1,0:T(8,128)(2,1)S(1)} collective-permute-done((bf16[1,96,256]{2,1,0:T(8,128)(2,1)S(1)}, bf16[1,96,256]{2,1,0:T(8,128)(2,1)S(1)}, u32[]{:S(2)}, u32[]{:S(2)}) %collective-permute-start.3) | collective-permute-done | bytes 49184 | tf_op jit(solution)/shard_map/ppermute | solution.py:25
  102.3 16.2 %all_gather.24 = bf16[1536,256]{1,0:T(8,128)(2,1)S(1)} all-gather(bf16[384,256]{1,0:T(8,128)(2,1)S(1)} %bitcast.444), channel_id=1, replica_groups=mesh['y'=4,'c'=2,'xh'=2,'xl'=2,'z'=4] {'xh','xl'}, dimensions={0}, use_global_device_ids=true | all-gather | bytes 983040 | tf_op jit(solution)/shard_map/all_gather | solution.py:356
  129.3 20.5 %all_gather.25 = bf16[384,768]{1,0:T(8,128)(2,1)S(1)} all-gather(bf16[96,768]{1,0:T(8,128)(2,1)S(1)} %collective-permute-done.7), channel_id=1, replica_groups=mesh['y'=4,'c'=2,'xh'=2,'xl'=2,'z'=4] {'xh','xl'}, dimensions={0}, use_global_device_ids=true | all-gather | bytes 737280 | tf_op jit(solution)/shard_map/all_gather | solution.py:356
  178.4 14.1 %all-to-all-done.kv_ref = bf16[16,2,128,128]{3,2,1,0:T(8,128)(2,1)S(1)} async-done(((bf16[16,2,128,128]{3,2,1,0:T(8,128)(2,1)}), bf16[16,2,128,128]{3,2,1,0:T(8,128)(2,1)S(1)}, u32[]{:S(2)}, u32[]{:S(2)}) %all-to-all-start) | async-done | bytes 1048608 | tf_op jit(solution)/shard_map/all_to_all | solution.py:527
  278.9 9.0 collective-permute-start.25
  297.3 9.4 collective-permute-done.26
  320.5 9.0 collective-permute-start.32
  402.5 15.6 %collective-permute-done.40 = bf16[128,1536]{1,0:T(8,128)(2,1)S(1)} collective-permute-done((bf16[128,1536]{1,0:T(8,128)(2,1)S(1)}, bf16[128,1536]{1,0:T(8,128)(2,1)S(1)}, u32[]{:S(2)}, u32[]{:S(2)}) %collective-permute-start.40) | collective-permute-done | bytes 393248 | tf_op jit(solution)/shard_map/ppermute | solution.py:25
  424.1 14.2 %collective-permute-done.43 = bf16[128,1536]{1,0:T(8,128)(2,1)S(1)} collective-permute-done((bf16[128,1536]{1,0:T(8,128)(2,1)S(1)}, bf16[128,1536]{1,0:T(8,128)(2,1)S(1)}, u32[]{:S(2)}, u32[]{:S(2)}) %collective-permute-start.43) | collective-permute-done | bytes 393248 | tf_op jit(solution)/shard_map/ppermute | solution.py:21
  486.0 8.8 collective-permute-done.63
  578.0 9.6 all-to-all-done.4
  605.7 9.4 collective-permute-done.74
  683.4 9.5 collective-permute-done.86
  708.3 9.3 collective-permute-done.90
  736.9 28.6 %all_to_all.30 = bf16[16,2,128,128]{3,2,1,0:T(8,128)(2,1)S(1)} all-to-all(bf16[16,2,128,128]{3,2,1,0:T(8,128)(2,1)S(1)} %get-tuple-element.30), channel_id=1, replica_groups=mesh['y'=4,'c'=2,'xh'=2,'xl'=2,'z'=4] {'xh','xl','z'}, dimensions={0} | all-to-all | bytes 2097152 | tf_op jit(solution)/shard_map/all_to_all | solution.py:623
  784.3 22.5 %reduce-scatter.11.cloned.1.call-done = bf16[96,768]{1,0:T(8,128)(2,1)} async-done(((bf16[384,768]{1,0:T(8,128)(2,1)}), bf16[96,768]{1,0:T(8,128)(2,1)}) %reduce-scatter.11.cloned.1.call-update) | async-done | bytes 147472 | tf_op jit(solution)/shard_map/reduce_scatter | solution.py:377
  806.9 31.5 %reduce-scatter.15.cloned.1.call-done = bf16[288,768]{1,0:T(8,128)(2,1)} async-done(((bf16[1152,768]{1,0:T(8,128)(2,1)}), bf16[288,768]{1,0:T(8,128)(2,1)}) %reduce-scatter.15.cloned.1.call-update) | async-done | bytes 442384 | tf_op jit(solution)/shard_map/reduce_scatter | solution.py:377
  838.3 24.2 %reduce-scatter.9.cloned.1.call-done = bf16[384,256]{1,0:T(8,128)(2,1)} async-done(((bf16[1536,256]{1,0:T(8,128)(2,1)}), bf16[384,256]{1,0:T(8,128)(2,1)}) %reduce-scatter.9.cloned.1.call-update) | async-done | bytes 196624 | tf_op jit(solution)/shard_map/reduce_scatter | solution.py:371
  862.5 47.9 %reduce-scatter.13.cloned.1.call-done = bf16[384,1280]{1,0:T(8,128)(2,1)} async-done(((bf16[1536,1280]{1,0:T(8,128)(2,1)}), bf16[384,1280]{1,0:T(8,128)(2,1)}) %reduce-scatter.13.cloned.1.call-update) | async-done | bytes 983056 | tf_op jit(solution)/shard_map/reduce_scatter | solution.py:371
  910.5 49.0 %all-gather.10.cloned.1.call-done = f32[16,264,128]{2,1,0:T(8,128)} async-done(((f32[1,264,128]{2,1,0:T(8,128)}), f32[16,264,128]{2,1,0:T(8,128)}) %all-gather.10.cloned.1.call-update) | async-done | bytes 2162704 | tf_op jit(solution)/shard_map/all_gather | solution.py:604
  978.0 9.2 collective-permute-done.92
  987.7 68.8 %psum.70 = f32[4,1536]{1,0:T(4,128)S(1)} all-reduce(f32[4,1536]{1,0:T(4,128)S(1)} %pad_maximum_fusion.40), channel_id=1, replica_groups=mesh['y'=4,'c'=2,'xh'=2,'xl'=2,'z'=4] {'y','c','xh','xl','z'}, use_global_device_ids=true, to_apply=%region_13.15 | all-reduce | flops 6144 | bytes 49152 | tf_op jit(solution)/shard_map/psum | solution.py:649
  1070.6 37.0 %collective-permute-done.95 = bf16[1,96,256]{2,1,0:T(8,128)(2,1)S(1)} collective-permute-done((bf16[1,96,256]{2,1,0:T(8,128)(2,1)S(1)}, bf16[1,96,256]{2,1,0:T(8,128)(2,1)S(1)}, u32[]{:S(2)}, u32[]{:S(2)}) %collective-permute-start.95) | collective-permute-done | bytes 49184 | tf_op jit(solution)/shard_map/ppermute | solution.py:25
  (828 shorter events, 614.1 us)
Async XLA Ops:
  7.2 247.2 %all-gather.12.cloned.1.call-start = ((), (), s32[]{:S(2)}) async-start(), calls=%async_computation.26 | async-start | bytes 5406720 | tf_op jit(solution)/shard_map/all_gather | solution.py:510
  12.8 247.3 %all-gather.6.cloned.1.call-start = ((), (), s32[]{:S(2)}) async-start(), calls=%async_computation.14 | async-start | bytes 4915200 | tf_op jit(solution)/shard_map/all_gather | solution.py:356
  14.0 144.4 %collective-permute-start = (bf16[128,1536]{1,0:T(8,128)(2,1)}, bf16[128,1536]{1,0:T(8,128)(2,1)}, u32[]{:S(2)}, u32[]{:S(2)}) collective-permute-start(bf16[128,1536]{1,0:T(8,128)(2,1)} %fusion.48), channel_id=1, source_target_pairs={{1,0},{2,1},{3,2},{0,3},{5,4},{6,5},{7,6},{4,7},{9,8},{10,9},{11,1... | collective-permute-start | bytes 1179656 | tf_op jit(solution)/shard_map/ppermute | solution.py:21
  71.1 87.4 %collective-permute-start.1 = (bf16[128,1536]{1,0:T(8,128)(2,1)}, bf16[128,1536]{1,0:T(8,128)(2,1)}, u32[]{:S(2)}, u32[]{:S(2)}) collective-permute-start(bf16[128,1536]{1,0:T(8,128)(2,1)} %fusion.48), channel_id=1, source_target_pairs={{2,0},{3,1},{0,2},{1,3},{6,4},{7,5},{4,6},{5,7},{10,8},{11,9},{8,1... | collective-permute-start | bytes 1179656 | tf_op jit(solution)/shard_map/ppermute | solution.py:21
  71.1 87.4 %collective-permute-start.2 = (bf16[128,1536]{1,0:T(8,128)(2,1)}, bf16[128,1536]{1,0:T(8,128)(2,1)}, u32[]{:S(2)}, u32[]{:S(2)}) collective-permute-start(bf16[128,1536]{1,0:T(8,128)(2,1)} %fusion.48), channel_id=1, source_target_pairs={{3,0},{0,1},{1,2},{2,3},{7,4},{4,5},{5,6},{6,7},{11,8},{8,9},{9,10... | collective-permute-start | bytes 1179656 | tf_op jit(solution)/shard_map/ppermute | solution.py:21
  77.2 41.3 %collective-permute-start.19 = (bf16[1,96,1280]{2,1,0:T(8,128)(2,1)S(1)}, bf16[1,96,1280]{2,1,0:T(8,128)(2,1)S(1)}, u32[]{:S(2)}, u32[]{:S(2)}) collective-permute-start(bf16[1,96,1280]{2,1,0:T(8,128)(2,1)S(1)} %get-tuple-element.204), channel_id=1, source_target_pairs={{0,1},{1,2},{2,3},{3,0},{4,5},{5,6},{6,7},{7,4},{8,9},{9,10},{10,1... | collective-permute-start | bytes 737288 | tf_op jit(solution)/shard_map/ppermute | solution.py:25
  119.3 37.9 %collective-permute-start.6 = (bf16[1536,256]{1,0:T(8,128)(2,1)S(1)}, bf16[1536,256]{1,0:T(8,128)(2,1)}, u32[]{:S(2)}, u32[]{:S(2)}) collective-permute-start(bf16[1536,256]{1,0:T(8,128)(2,1)S(1)} %all_gather.24), channel_id=1, source_target_pairs={{0,16},{16,0},{1,17},{17,1},{2,18},{18,2},{3,19},{19,3},{4,20},{20... | collective-permute-start | bytes 2359304 | tf_op jit(solution)/shard_map/ppermute | solution.py:29
  169.8 168.7 %all-gather.8.cloned.1.call-start = ((), (), s32[]{:S(2)}) async-start(), calls=%async_computation.15 | async-start | bytes 6881280 | tf_op jit(solution)/shard_map/all_gather | solution.py:356
  542.6 238.9 %all-reduce.12.cloned.1.call-start = ((), (), s32[]{:S(2)}) async-start(), calls=%async_computation.22 | async-start | bytes 270336 | tf_op jit(solution)/shard_map/psum | solution.py:604
  564.4 217.8 %reduce-scatter.23.cloned.1.call-start = ((), (), s32[]{:S(2)}) async-start(), calls=%async_computation.25 | async-start | bytes 2211840 | tf_op jit(solution)/shard_map/reduce_scatter | solution.py:377
  576.8 205.5 %reduce-scatter.19.cloned.1.call-start = ((), (), s32[]{:S(2)}) async-start(), calls=%async_computation.21 | async-start | bytes 983040 | tf_op jit(solution)/shard_map/reduce_scatter | solution.py:377
  577.9 204.4 %reduce-scatter.17.cloned.1.call-start = ((), (), s32[]{:S(2)}) async-start(), calls=%async_computation.20 | async-start | bytes 1966080 | tf_op jit(solution)/shard_map/reduce_scatter | solution.py:371
  599.6 184.8 %reduce-scatter.21.cloned.1.call-start = ((), (), s32[]{:S(2)}) async-start(), calls=%async_computation.24 | async-start | bytes 4915200 | tf_op jit(solution)/shard_map/reduce_scatter | solution.py:371
  634.5 172.4 %reduce-scatter.11.cloned.1.call-start = ((), (), s32[]{:S(2)}) async-start(), calls=%async_computation.17 | async-start | bytes 737280 | tf_op jit(solution)/shard_map/reduce_scatter | solution.py:377
  721.8 116.5 %reduce-scatter.15.cloned.1.call-start = ((), (), s32[]{:S(2)}) async-start(), calls=%async_computation.19 | async-start | bytes 2211840 | tf_op jit(solution)/shard_map/reduce_scatter | solution.py:377
  726.1 136.4 %reduce-scatter.9.cloned.1.call-start = ((), (), s32[]{:S(2)}) async-start(), calls=%async_computation.16 | async-start | bytes 983040 | tf_op jit(solution)/shard_map/reduce_scatter | solution.py:371
  772.7 137.7 %reduce-scatter.13.cloned.1.call-start = ((), (), s32[]{:S(2)}) async-start(), calls=%async_computation.18 | async-start | bytes 4915200 | tf_op jit(solution)/shard_map/reduce_scatter | solution.py:371
  781.4 178.0 %all-gather.10.cloned.1.call-start = ((), (), s32[]{:S(2)}) async-start(), calls=%async_computation.23 | async-start | bytes 2297856 | tf_op jit(solution)/shard_map/all_gather | solution.py:604
  782.2 276.0 %all-reduce.14.cloned.1.call-start = ((), (), s32[]{:S(2)}) async-start(), calls=%async_computation.27 | async-start | bytes 7569408 | tf_op jit(solution)/shard_map/psum | solution.py:372
  1058.2 100.6 %collective-permute-start.107 = (bf16[288,768]{1,0:T(8,128)(2,1)}, bf16[288,768]{1,0:T(8,128)(2,1)S(1)}, u32[]{:S(2)}, u32[]{:S(2)}) collective-permute-start(bf16[288,768]{1,0:T(8,128)(2,1)} %get-tuple-element.50), channel_id=1, source_target_pairs={{0,0},{1,4},{2,8},{3,12},{4,1},{5,5},{6,9},{7,13},{8,2},{9,6},{10,... | collective-permute-start | bytes 1327112 | tf_op jit(solution)/shard_map/ppermute | solution.py:34
  1060.0 98.8 %collective-permute-start.121 = (bf16[288,768]{1,0:T(8,128)(2,1)}, bf16[288,768]{1,0:T(8,128)(2,1)S(1)}, u32[]{:S(2)}, u32[]{:S(2)}) collective-permute-start(bf16[288,768]{1,0:T(8,128)(2,1)} %get-tuple-element.54), channel_id=1, source_target_pairs={{0,0},{1,4},{2,8},{3,12},{4,1},{5,5},{6,9},{7,13},{8,2},{9,6},{10,... | collective-permute-start | bytes 1327112 | tf_op jit(solution)/shard_map/ppermute | solution.py:34
  1063.2 66.9 %collective-permute-start.116 = (bf16[1,96,1280]{2,1,0:T(8,128)(2,1)S(1)}, bf16[1,96,1280]{2,1,0:T(8,128)(2,1)S(1)}, u32[]{:S(2)}, u32[]{:S(2)}) collective-permute-start(bf16[1,96,1280]{2,1,0:T(8,128)(2,1)S(1)} %get-tuple-element.180), channel_id=1, source_target_pairs={{0,1},{1,2},{2,3},{3,0},{4,5},{5,6},{6,7},{7,4},{8,9},{9,10},{10,1... | collective-permute-start | bytes 737288 | tf_op jit(solution)/shard_map/ppermute | solution.py:25
  1065.7 51.5 %collective-permute-start.109 = (bf16[1,96,512]{2,1,0:T(8,128)(2,1)S(1)}, bf16[1,96,512]{2,1,0:T(8,128)(2,1)S(1)}, u32[]{:S(2)}, u32[]{:S(2)}) collective-permute-start(bf16[1,96,512]{2,1,0:T(8,128)(2,1)S(1)} %get-tuple-element.257), channel_id=1, source_target_pairs={{0,1},{1,2},{2,3},{3,0},{4,5},{5,6},{6,7},{7,4},{8,9},{9,10},{10,1... | collective-permute-start | bytes 294920 | tf_op jit(solution)/shard_map/ppermute | solution.py:25
  1070.4 37.2 %collective-permute-start.95 = (bf16[1,96,256]{2,1,0:T(8,128)(2,1)S(1)}, bf16[1,96,256]{2,1,0:T(8,128)(2,1)S(1)}, u32[]{:S(2)}, u32[]{:S(2)}) collective-permute-start(bf16[1,96,256]{2,1,0:T(8,128)(2,1)S(1)} %get-tuple-element.275), channel_id=1, source_target_pairs={{0,1},{1,2},{2,3},{3,0},{4,5},{5,6},{6,7},{7,4},{8,9},{9,10},{10,1... | collective-permute-start | bytes 147464 | tf_op jit(solution)/shard_map/ppermute | solution.py:25
  (244 other events, 4123.2 us)
Sparse Core Ops, SparseCore 0:
  13.0 108.5 all-gather.11
  125.5 60.9 all-gather.5
  235.5 60.5 all-gather.7
  564.5 75.2 all-reduce.11
  642.8 29.9 reduce-scatter.22
  675.7 21.0 reduce-scatter.18
  699.7 25.4 reduce-scatter.16
  727.6 56.6 reduce-scatter.20
  787.3 19.5 reduce-scatter.10
  809.7 28.5 reduce-scatter.14
  841.5 21.0 reduce-scatter.8
  864.9 45.4 reduce-scatter.12
  912.2 47.2 all-gather.9
  962.5 90.4 all-reduce.13

commit v2 on v1

v2 whole, which is shorter than its diff:
```python
import functools
import math

import jax
import jax.numpy as jnp
from jax import lax
from jax.experimental import pallas as pl
from jax.experimental.pallas import tpu as pltpu
from jax.sharding import Mesh, PartitionSpec as P

WINDOW = 1024
EPSILON = 1e-06
DECAY_SCALE = 8.0

X = ("xh", "xl")
XN = 4
F32 = jnp.float32
BF16 = jnp.bfloat16


def x_index():
    return lax.axis_index("xh") * 2 + lax.axis_index("xl")


def from_x(value, by):
    return lax.ppermute(value, X, [((i + by) % XN, i) for i in range(XN)])


def to_x(value, by):
    return lax.ppermute(value, X, [(i, (i + by) % XN) for i in range(XN)])


def flip(value, axis, by):
    return lax.ppermute(value, axis, [(i, i ^ by) for i in range(lax.axis_size(axis))])


def tie(main, *side):
    return lax.optimization_barrier((main, *side))


def after(value, *done):
    return lax.optimization_barrier((value, done))[0]


def swap(value):
    return lax.ppermute(value, "c", [(0, 1), (1, 0)])


def exchange_x(value):
    return lax.all_to_all(value, X, 0, 0)


def by_core(mine, other):
    first = lax.axis_index("c") == 0
    return jnp.where(first, mine, other), jnp.where(first, other, mine)


def core_pick(zero, one):
    return jnp.where(lax.axis_index("c") == 0, zero, one)


def core_join(mine, other):
    return jnp.concatenate(by_core(mine, other), axis=-1)


def normalize(values, gain):
    return values * lax.rsqrt(jnp.mean(values * values, axis=-1, keepdims=True) + EPSILON) * gain


def smooth_gelu(values):
    return jax.nn.gelu(values, approximate=True)


def gated_unit(gate_pre, lift_pre):
    return smooth_gelu(gate_pre) * lift_pre


def branch_merge(states, branch_y):
    return states * smooth_gelu(branch_y)


def gate_terms(pre_decay, pre_admit, conv_out, decay_rate):
    retain = jax.nn.sigmoid(pre_decay)
    admit = jax.nn.sigmoid(pre_admit)
    log_decay = -DECAY_SCALE * jax.nn.softplus(decay_rate) * (0.25 + retain)
    return (jnp.exp(log_decay), jnp.sqrt(-jnp.expm1(2.0 * log_decay)) * admit * conv_out)


def matmul(left, right):
    return jnp.dot(left, right, preferred_element_type=F32)


def times_transposed(left, right):
    return lax.dot_general(left, right, (((1,), (1,)), ((), ())), preferred_element_type=F32)


def transposed_times(left, right):
    return lax.dot_general(left, right, (((0,), (0,)), ((), ())), preferred_element_type=F32)


def gather_rows(low):
    return [low] + [from_x(low, r) for r in range(1, XN)]


def chunked(low, begin, end, side=()):
    near = {1: from_x(low, 1), 3: from_x(low, 3)}
    first, later = tie(begin(0, low), low)
    far, side = tie(from_x(later, 2), side)
    chunks = [low, near[1], far, near[3]]
    outs = [end(0, first)] + [None] * (XN - 1)
    for k in (1, 3, 2):
        outs[k] = end(k, begin(k, chunks[k]))
    return chunks, outs, side


def scatter_chunks(parts):
    total = parts[0]
    for r in (2, 1, 3):
        total = total + to_x(parts[r].astype(BF16), r).astype(F32)
    return total


def cost(microseconds):
    return pl.CostEstimate(flops=0, bytes_accessed=int(microseconds * 3.6e6), transcendentals=0)


def core_scalar():
    return lax.axis_index("c").astype(jnp.int32)[None]


def product_kernel(count, pieces, split, core_ref, *refs):
    lefts, rights = refs[:count], refs[count : 2 * count]
    mine_ref, other_ref, right = refs[2 * count :]
    rows = lefts[0].shape[0]

    @pl.when(pl.program_id(0) == 0)
    def _():
        for k in range(count):
            right[k * rows : (k + 1) * rows, :] = rights[k][...]

    left = jnp.concatenate([ref[...] for ref in lefts], axis=0)
    total = transposed_times(left, right[...]).astype(BF16)
    first = core_ref[0] == 0
    at = 0
    for low, high, width in pieces:
        zero, one = total[:, low : low + width], total[:, high : high + width]
        for ref, value in ((mine_ref, jnp.where(first, zero, one)), (other_ref, jnp.where(first, one, zero))):
            if split:
                each = ref.shape[2]
                for z in range(ref.shape[0]):
                    ref[z, 0, :, at : at + width] = value[z * each : (z + 1) * each]
            else:
                ref[:, at : at + width] = value
        at += width


def chunk_product(lefts, rights, pieces, split):
    rows, deep = lefts[0].shape
    width = rights[0].shape[1]
    count = len(lefts)
    kept = sum(piece[2] for piece in pieces)
    if split:
        tile = deep // XN
        shape = (4, XN, tile // 4, kept)
        spec = pl.BlockSpec((4, 1, tile // 4, kept), lambda i: (0, i, 0, 0))
    else:
        tile = next((t for t in (384, 256, 128) if deep % t == 0), deep)
        shape = (deep, kept)
        spec = pl.BlockSpec((tile, kept), lambda i: (i, 0))
    mine, other = pl.pallas_call(
        functools.partial(product_kernel, count, pieces, split),
        grid=(deep // tile,),
        in_specs=[pl.BlockSpec(memory_space=pltpu.SMEM)]
        + [pl.BlockSpec((rows, tile), lambda i: (0, i)) for _ in lefts]
        + [pl.BlockSpec((rows, width), lambda i: (0, 0)) for _ in rights],
        out_specs=[spec, spec],
        out_shape=[jax.ShapeDtypeStruct(shape, BF16)] * 2,
        scratch_shapes=[pltpu.VMEM((count * rows, width), BF16)],
        compiler_params=pltpu.CompilerParams(vmem_limit_bytes=48 << 20),
        cost_estimate=pl.CostEstimate(
            flops=2 * count * rows * deep * width,
            bytes_accessed=2 * (count * rows * (deep + width) + 2 * deep * kept),
            transcendentals=0,
        ),
    )(core_scalar(), *lefts, *rights)
    total = (mine.astype(F32) + swap(other).astype(F32)).astype(BF16)
    return total.reshape(-1, kept)


def unit_pieces(quarter):
    wide = quarter * 5 // 9
    return ((0, quarter - wide, wide), (quarter, 2 * quarter - wide, wide))


def half_pieces(width):
    half = width // 4
    return ((0, half, half), (2 * half, 3 * half, half))


def row_pieces(width):
    return ((0, width // 2, width // 2),)


def kv_places(rows):
    places = []
    for x in range(XN):
        for z in range(4):
            for j in range(2):
                position = (j * 4 + z) * 2 + x // 2
                places.append((x * 4 + z, j, x % 2, WINDOW + position * rows))
    return places


def attend_scores(pos_ref, q_ref, key_s, scale):
    rows, size = q_ref.shape[1], key_s.shape[1]
    heads = q_ref.shape[2] // size
    start = pl.multiple_of(pos_ref[pl.program_id(0)] * rows, rows)
    query = q_ref[0]
    query = jnp.concatenate([query[:, h * size : (h + 1) * size] for h in range(heads)], axis=0)
    key = key_s[pl.ds(start, WINDOW + rows), :]
    scores = times_transposed(query, key) * scale
    row = lax.broadcasted_iota(jnp.int32, scores.shape, 0) % rows
    col = lax.broadcasted_iota(jnp.int32, scores.shape, 1)
    allowed = (col > row) & (col <= row + WINDOW) & (col >= WINDOW - start)
    return start, query, key, jnp.where(allowed, scores, -1e30)


def load_kv(kv_ref, key_s, value_s):
    rows = kv_ref.shape[2]
    key_s[:WINDOW, :] = jnp.zeros((WINDOW, key_s.shape[1]), key_s.dtype)
    value_s[:WINDOW, :] = jnp.zeros((WINDOW, key_s.shape[1]), key_s.dtype)
    for source, j, kind, first in kv_places(rows):
        (value_s if kind else key_s)[first : first + rows, :] = kv_ref[source, j]


def attend_forward_kernel(scale, pos_ref, q_ref, kv_ref, out_ref, lse_ref, key_s, value_s):
    rows, size = q_ref.shape[1], key_s.shape[1]

    @pl.when(pl.program_id(0) == 0)
    def _():
        load_kv(kv_ref, key_s, value_s)

    start, query, key, scores = attend_scores(pos_ref, q_ref, key_s, scale)
    highest = jnp.max(scores, axis=-1, keepdims=True)
    lse = highest + jnp.log(jnp.sum(jnp.exp(scores - highest), axis=-1, keepdims=True))
    probs = jnp.exp(scores - lse).astype(BF16)
    mixed = matmul(probs, value_s[pl.ds(start, WINDOW + rows), :]).astype(BF16)
    out_ref[0] = jnp.concatenate(
        [mixed[h * rows : (h + 1) * rows] for h in range(q_ref.shape[2] // size)], axis=1
    )
    lse_ref[0] = lse


def attend_backward_kernel(
    scale, pos_ref, q_ref, kv_ref, grad_ref, lse_ref, dq_ref, dkv_ref, key_s, value_s, dk_s, dv_s
):
    rows, size = q_ref.shape[1], key_s.shape[1]
    heads = q_ref.shape[2] // size

    @pl.when(pl.program_id(0) == 0)
    def _():
        load_kv(kv_ref, key_s, value_s)
        dk_s[...] = jnp.zeros_like(dk_s)
        dv_s[...] = jnp.zeros_like(dv_s)

    start, query, key, scores = attend_scores(pos_ref, q_ref, key_s, scale)
    span = pl.ds(start, WINDOW + rows)
    probs = jnp.exp(scores - lse_ref[0])
    grad = grad_ref[0]
    grad = jnp.concatenate([grad[:, h * size : (h + 1) * size] for h in range(heads)], axis=0)
    prob_grad = times_transposed(grad, value_s[span, :])
    delta = jnp.sum(probs * prob_grad, axis=-1, keepdims=True)
    score_grad = (probs * (prob_grad - delta)).astype(BF16)
    query_grad = (matmul(score_grad, key) * scale).astype(BF16)
    dq_ref[0] = jnp.concatenate(
        [query_grad[h * rows : (h + 1) * rows] for h in range(heads)], axis=1
    )
    dk_s[span, :] += transposed_times(score_grad, query) * scale
    dv_s[span, :] += transposed_times(probs.astype(BF16), grad)

    @pl.when(pl.program_id(0) == pl.num_programs(0) - 1)
    def _():
        for source, j, kind, first in kv_places(rows):
            dkv_ref[source, j] = (dv_s if kind else dk_s)[first : first + rows, :].astype(BF16)


def whole(array):
    return pl.BlockSpec(array.shape, lambda r: (0,) * len(array.shape))


def by_block(*shape):
    return pl.BlockSpec((1,) + shape, lambda r: (r, 0, 0))


def kv_scratch(kv, dtype):
    return pltpu.VMEM((WINDOW + 16 * kv.shape[2], kv.shape[3]), dtype)


def attend_forward(positions, query, kv):
    blocks, rows, width = query.shape
    size = kv.shape[3]
    stacked = rows * (width // size)
    return pl.pallas_call(
        functools.partial(attend_forward_kernel, size**-0.5),
        grid=(blocks,),
        in_specs=[pl.BlockSpec(memory_space=pltpu.SMEM), by_block(rows, width), whole(kv)],
        out_specs=[by_block(rows, width), by_block(stacked, 1)],
        out_shape=[
            jax.ShapeDtypeStruct(query.shape, BF16),
            jax.ShapeDtypeStruct((blocks, stacked, 1), F32),
        ],
        scratch_shapes=[kv_scratch(kv, BF16), kv_scratch(kv, BF16)],
        cost_estimate=cost(7),
        compiler_params=pltpu.CompilerParams(vmem_limit_bytes=40 << 20),
    )(positions, query, kv)


def attend_backward(positions, query, kv, grad, lse):
    blocks, rows, width = query.shape
    size = kv.shape[3]
    stacked = rows * (width // size)
    return pl.pallas_call(
        functools.partial(attend_backward_kernel, size**-0.5),
        grid=(blocks,),
        in_specs=[
            pl.BlockSpec(memory_space=pltpu.SMEM),
            by_block(rows, width),
            whole(kv),
            by_block(rows, width),
            by_block(stacked, 1),
        ],
        out_specs=[by_block(rows, width), whole(kv)],
        out_shape=[
            jax.ShapeDtypeStruct(query.shape, BF16),
            jax.ShapeDtypeStruct(kv.shape, BF16),
        ],
        scratch_shapes=[
            kv_scratch(kv, BF16),
            kv_scratch(kv, BF16),
            kv_scratch(kv, F32),
            kv_scratch(kv, F32),
        ],
        cost_estimate=cost(9),
        compiler_params=pltpu.CompilerParams(vmem_limit_bytes=40 << 20),
    )(positions, query, kv, grad, lse)


def scan_kernel(backward, factor_ref, update_ref, state_ref):
    tiles = factor_ref.shape[0] // 8
    width = factor_ref.shape[1]
    row = lax.broadcasted_iota(jnp.int32, (8, width), 0)

    def turn(index, carry):
        tile = tiles - 1 - index if backward else index
        span = pl.ds(pl.multiple_of(tile * 8, 8), 8)
        factor, update = factor_ref[span, :], update_ref[span, :]
        for reach in (1, 2, 4):
            shift = 8 - reach if backward else reach
            inside = row < 8 - reach if backward else row >= reach
            far_update = pltpu.roll(update, shift, 0)
            far_factor = pltpu.roll(factor, shift, 0)
            update = jnp.where(inside, factor * far_update + update, update)
            factor = jnp.where(inside, factor * far_factor, factor)
        state = factor * carry + update
        state_ref[span, :] = state
        last = state[0:1] if backward else state[7:8]
        return jnp.broadcast_to(last, (8, width))

    lax.fori_loop(0, tiles, turn, jnp.zeros((8, width), F32), unroll=8)


def linear_scan(factors, updates, backward):
    return pl.pallas_call(
        functools.partial(scan_kernel, backward),
        out_shape=jax.ShapeDtypeStruct(factors.shape, F32),
        cost_estimate=cost(1.5),
        compiler_params=pltpu.CompilerParams(vmem_limit_bytes=24 << 20),
    )(factors, updates)


def to_sequence(chunks):
    rows, width = chunks[0].shape[0], chunks[0].shape[1] // 4
    sent = jnp.stack(
        [jnp.stack([part[:, b * width : (b + 1) * width] for part in chunks]) for b in range(4)]
    )
    got = lax.all_to_all(sent, "z", 0, 0)
    got = jnp.roll(got, x_index(), axis=1).reshape(4, 2, 2, rows, width)
    return got.transpose(2, 0, 1, 3, 4).reshape(16 * rows, width)


def from_sequence(values):
    rows, width = values.shape[0] // 16, values.shape[1]
    sent = values.reshape(2, 4, 2, rows, width).transpose(1, 2, 0, 3, 4)
    sent = jnp.roll(sent.reshape(4, XN, rows, width), -x_index(), axis=1)
    got = lax.all_to_all(sent, "z", 0, 0)
    return [jnp.concatenate([got[b, k] for b in range(4)], axis=1) for k in range(XN)]


def shift_down(values, by):
    if by == 0:
        return values
    return jnp.concatenate([jnp.zeros_like(values[:by]), values[:-by]], axis=0)


def shift_up(values, by):
    if by == 0:
        return values
    return jnp.concatenate([values[by:], jnp.zeros_like(values[:by])], axis=0)


def unit_slices(weight):
    quarter = weight.shape[1] // XN
    wide = quarter * 5 // 9
    skip = quarter - wide
    keep = lax.broadcasted_iota(jnp.int32, (weight.shape[0], wide), 1) >= wide - skip
    picked = []
    for member in range(XN):
        columns = weight[:, member * quarter : (member + 1) * quarter]
        picked.append(core_pick(columns[:, :wide], jnp.where(keep, columns[:, skip:], 0)))
    return jnp.stack(picked)


def half_slices(weight):
    quarter = weight.shape[1] // XN
    half = quarter // 2
    picked = []
    for member in range(XN):
        columns = weight[:, member * quarter : (member + 1) * quarter]
        picked.append(core_pick(columns[:, :half], columns[:, half:]))
    return jnp.stack(picked)


def own_half(weight):
    half = weight.shape[-1] // 2
    return core_pick(weight[..., :half], weight[..., half:])


def other_half(weight):
    half = weight.shape[-1] // 2
    return core_pick(weight[..., half:], weight[..., :half])


def gather_direct(value):
    z = lax.axis_index("z")
    out = jnp.zeros((value.shape[0], 4) + value.shape[1:], value.dtype)
    for by in range(4):
        piece = flip(value, "z", by) if by else value
        out = lax.dynamic_update_slice_in_dim(out, piece[:, None], z ^ by, 1)
    return out


def row_join(rows):
    return core_join(rows, swap(rows))


def join_kernel(plans, core_ref, mine_ref, other_ref, *outs):
    first = core_ref[0] == 0
    each = mine_ref.shape[2]
    for z in range(mine_ref.shape[0]):
        mine, other = mine_ref[z, 0], other_ref[z, 0]
        zero, one = jnp.where(first, mine, other), jnp.where(first, other, mine)
        for out, pieces in zip(outs, plans):
            at = 0
            for core, low, high in pieces:
                out[z * each : (z + 1) * each, at : at + high - low] = (one if core else zero)[:, low:high]
                at += high - low


def column_join(columns, plans):
    zs, xs, rows, width = columns.shape
    spec = pl.BlockSpec((zs, 1, rows, width), lambda i: (0, i, 0, 0))
    widths = [sum(high - low for _, low, high in pieces) for pieces in plans]
    return pl.pallas_call(
        functools.partial(join_kernel, plans),
        grid=(xs,),
        in_specs=[pl.BlockSpec(memory_space=pltpu.SMEM), spec, spec],
        out_specs=[pl.BlockSpec((zs * rows, out), lambda i: (i, 0)) for out in widths],
        out_shape=[jax.ShapeDtypeStruct((zs * xs * rows, out), BF16) for out in widths],
        cost_estimate=cost(6),
        compiler_params=pltpu.CompilerParams(vmem_limit_bytes=40 << 20),
    )(core_scalar(), columns, swap(columns))


def unit_plan(unit_width):
    wide = unit_width // 2
    skip = wide * 4 // 5
    return (
        (0, 0, wide),
        (1, wide - skip, wide),
        (0, wide, 2 * wide),
        (1, 2 * wide - skip, 2 * wide),
    )


def half_plan(first, width):
    half = width // 2
    return tuple(
        (core, first + side * half, first + (side + 1) * half) for side in range(2) for core in range(2)
    )


def reduce_z(grad):
    return lax.psum_scatter(grad, "z", scatter_dimension=0, tiled=True)


def reduce_z_direct(grad):
    z = lax.axis_index("z")
    parts = grad.reshape(4, -1, grad.shape[1])
    total = lax.dynamic_index_in_dim(parts, z, 0, keepdims=False).astype(F32)
    for by in range(1, 4):
        piece = lax.dynamic_index_in_dim(parts, z ^ by, 0, keepdims=False)
        total = total + flip(piece, "z", by).astype(F32)
    return total.astype(BF16)


def units_of(columns, rows):
    own = columns[0].shape[0] // XN
    unit = functools.reduce(math.gcd, [own] + [array.shape[0] for array in rows])
    half = rows[0].shape[1]
    chunk = functools.reduce(math.gcd, [half] + [array.shape[1] // 2 for array in columns])
    column_units = [
        (a, lane, part)
        for a, array in enumerate(columns)
        for lane in range(array.shape[1] // chunk)
        for part in range(own // unit)
    ]
    row_units = [
        (a, part, lane)
        for a, array in enumerate(rows)
        for part in range(array.shape[0] // unit)
        for lane in range(half // chunk)
    ]
    column_slots, row_slots = -(-len(column_units) // 4), -(-len(row_units) // 4)
    return unit, chunk, own, column_units, row_units, column_slots, row_slots


def pack_kernel(plan, column_count, *refs):
    unit, chunk, own, column_units, row_units, column_slots, row_slots = plan
    columns, rows, out = refs[:column_count], refs[column_count:-1], refs[-1]
    slots = XN * column_slots + row_slots
    for n, (a, lane, part) in enumerate(column_units):
        for x in range(XN):
            first = ((n % 4) * slots + x * column_slots + n // 4) * unit
            out[first : first + unit, :] = columns[a][
                x * own + part * unit : x * own + (part + 1) * unit,
                lane * chunk : (lane + 1) * chunk,
            ]
    for n, (a, part, lane) in enumerate(row_units):
        first = ((n % 4) * slots + XN * column_slots + n // 4) * unit
        out[first : first + unit, :] = rows[a][
            part * unit : (part + 1) * unit, lane * chunk : (lane + 1) * chunk
        ]
    empty = jnp.zeros((unit, chunk), BF16)
    for n in range(len(column_units), 4 * column_slots):
        for x in range(XN):
            first = ((n % 4) * slots + x * column_slots + n // 4) * unit
            out[first : first + unit, :] = empty
    for n in range(len(row_units), 4 * row_slots):
        first = ((n % 4) * slots + XN * column_slots + n // 4) * unit
        out[first : first + unit, :] = empty


def unpack_kernel(plan, kinds, packed, *outs):
    unit, chunk, own, column_units, row_units, column_slots, row_slots = plan
    slots = XN * column_slots + row_slots

    def block(n, c, slot):
        first = (((n % 4) * 2 + c) * slots + slot + n // 4) * unit
        return packed[first : first + unit, :].astype(F32)

    for n, (a, lane, part) in enumerate(column_units):
        kind, width, first_out = kinds[a]
        rows = slice(part * unit, (part + 1) * unit)
        for c in range(2):
            got = [block(n, c, x * column_slots) for x in range(XN)]
            if kind == "attend":
                at = c * width + lane * chunk
                query = 2 * width * 3 // 4
                for x in range(XN):
                    if at < query:
                        to = x * query + at
                        outs[first_out][rows, to : to + chunk] = got[x]
                if at >= query:
                    size = 2 * width - query
                    to = at - query
                    outs[first_out + 1][rows, to : to + chunk] = got[0] + got[2]
                    outs[first_out + 1][rows, size + to : size + to + chunk] = got[1] + got[3]
                continue
            each = width // 2
            which, at = divmod(lane * chunk, each)
            if kind == "unit":
                skip = each * 4 // 5
                quarter = each + skip
                at = at + c * skip
                if c == 1 and at < each:
                    continue
            else:
                quarter = 2 * each
                at = at + c * each
            for x in range(XN):
                to = x * quarter + at
                outs[first_out + which][rows, to : to + chunk] = got[x]
    row_outs = outs[-(1 + max(a for a, _, _ in row_units)) :]
    half = row_outs[0].shape[1] // 2
    for n, (a, part, lane) in enumerate(row_units):
        for c in range(2):
            to = c * half + lane * chunk
            row_outs[a][part * unit : (part + 1) * unit, to : to + chunk] = block(
                n, c, XN * column_slots
            )


def pack(columns, rows):
    plan = units_of(columns, rows)
    unit, chunk, _, _, _, column_slots, row_slots = plan
    return pl.pallas_call(
        functools.partial(pack_kernel, plan, len(columns)),
        out_shape=jax.ShapeDtypeStruct(
            (4 * (XN * column_slots + row_slots) * unit, chunk), BF16
        ),
        cost_estimate=cost(2),
        compiler_params=pltpu.CompilerParams(vmem_limit_bytes=40 << 20),
    )(*columns, *rows), plan


def to_owners(part, plan):
    unit, chunk, _, _, _, column_slots, row_slots = plan
    split = XN * column_slots * unit
    columns = exchange_x(part[:split].reshape(XN, column_slots * unit, chunk))
    return jnp.concatenate([columns.reshape(split, chunk), part[split:]], axis=0)


def spread(part):
    return lax.all_gather(part, ("y", "c"), axis=0, tiled=True)


def unpack(packed, plan, kinds, shapes):
    return pl.pallas_call(
        functools.partial(unpack_kernel, plan, kinds),
        out_shape=[jax.ShapeDtypeStruct(shape, F32) for shape in shapes],
        cost_estimate=cost(4),
        compiler_params=pltpu.CompilerParams(vmem_limit_bytes=48 << 20),
    )(packed)


def butterfly(value, axes):
    for axis in axes:
        by = 1
        while by < lax.axis_size(axis):
            value = value + flip(value, axis, by)
            by *= 2
    return value


def dense_forward(residual, gain, unit_weight, drop_weight):
    normed, norm_pull = jax.vjp(normalize, residual, gain)
    wide = unit_weight.shape[1] // 2
    kept = [None] * XN

    def begin(k, rows):
        return matmul(rows, unit_weight)

    def end(k, pre):
        hidden, unit_pull = jax.vjp(gated_unit, pre[:, :wide], pre[:, wide:])
        kept[k] = (hidden.astype(BF16), unit_pull)
        return matmul(kept[k][0], drop_weight)

    chunks, parts, _ = chunked(normed.astype(BF16), begin, end)
    return parts, (norm_pull, chunks, kept)


def dense_backward(residual_grad, stored, unit_weight, drop_weight, grad_chunks=None, side=()):
    norm_pull, chunks, kept = stored
    pre_grads = [None] * XN

    def begin(k, rows):
        return times_transposed(rows, drop_weight)

    def end(k, hidden_grad):
        pre_grad = kept[k][1](hidden_grad)
        pre_grads[k] = jnp.concatenate([part.astype(BF16) for part in pre_grad], axis=1)
        return times_transposed(pre_grads[k], unit_weight)

    if grad_chunks is None:
        grad_chunks, parts, side = chunked(residual_grad.astype(BF16), begin, end, side)
    else:
        parts = [None] * XN
        for k in (0, 1, 3, 2):
            parts[k] = end(k, begin(k, grad_chunks[k]))
    input_grad, gain_grad = norm_pull(scatter_chunks(parts))
    residual_grad = residual_grad + input_grad
    pre_grads, grad_chunks = after((pre_grads, grad_chunks), residual_grad)
    unit_grad = chunk_product(chunks, pre_grads, unit_pieces(unit_weight.shape[1] // 2), True)
    drop_grad = chunk_product(
        [hidden for hidden, _ in kept], grad_chunks, row_pieces(drop_weight.shape[1]), False
    )
    return residual_grad, gain_grad, unit_grad, drop_grad, side


def body(
    tokens,
    lengths,
    cotangent,
    attend_gain,
    query_weight,
    keyval_weight,
    attend_output,
    lower_gain,
    lower_gate,
    lower_lift,
    lower_drop,
    recur_gain,
    recur_input,
    recur_branch,
    recur_output,
    temporal_kernel,
    decay_gate,
    input_gate,
    decay_rate,
    upper_gain,
    upper_gate,
    upper_lift,
    upper_drop,
):
    x, z = x_index(), lax.axis_index("z")
    row_count, features = tokens.shape[1:]
    size = keyval_weight.shape[1] // 2
    query_width = query_weight.shape[1] // XN
    drop_rows, recur_rows = lower_drop.shape[0], recur_output.shape[0]
    channels = 4 * recur_rows
    tap_count = temporal_kernel.shape[0]
    even = x % 2 == 0
    members = (x + jnp.arange(XN, dtype=jnp.int32)) % XN
    positions = ((members % 2 * 4 + z) * 2 + members // 2).astype(jnp.int32)
    token_pos = positions[0] * row_count + jnp.arange(row_count, dtype=jnp.int32)
    valid = (token_pos < lengths[0]).astype(F32)[:, None]

    start_rows = tokens[0].astype(F32)
    normed_attend, attend_pull = jax.vjp(normalize, start_rows, attend_gain)
    member_query = query_weight.reshape(-1, XN, query_width).transpose(1, 0, 2)
    member_kv = jnp.stack([keyval_weight[:, (m % 2) * size : (m % 2 + 1) * size] for m in range(XN)])
    attend_columns = exchange_x(own_half(jnp.concatenate([member_query, member_kv], axis=2)))
    lower_gate, lower_lift = after((lower_gate, lower_lift), attend_columns)
    lower_columns = exchange_x(
        jnp.concatenate([unit_slices(lower_gate), unit_slices(lower_lift)], axis=2)
    )
    unit_width = lower_columns.shape[2]
    lower_rows = lax.all_gather(own_half(lower_drop), "z", axis=0, tiled=True)
    half_in = gather_direct(attend_columns).reshape(features, -1)
    attend_in = row_join(half_in)

    attend_rows = jnp.concatenate(gather_rows(normed_attend.astype(BF16)), axis=0)
    attend_rows, lower_columns = tie(attend_rows, lower_columns)
    later = (recur_input, recur_branch, upper_gate, upper_lift)
    recur_input, recur_branch, upper_gate, upper_lift = after(later, lower_columns)
    upper_columns = exchange_x(
        jnp.concatenate(
            [
                unit_slices(upper_gate),
                unit_slices(upper_lift),
                half_slices(recur_input),
                half_slices(recur_branch),
            ],
            axis=2,
        )
    )
    lower_columns = lax.all_gather(lower_columns, "z", axis=0)
    mixed_in = matmul(attend_rows, attend_in).astype(BF16).reshape(XN, row_count, -1)
    mixed_in, lower_rows, upper_columns = tie(mixed_in, lower_rows, upper_columns)
    half_out = own_half(after(attend_output, mixed_in))
    attend_out = row_join(gather_direct(half_out[None]).reshape(query_width, -1))
    queries = mixed_in[:, :, :query_width]
    kv_part = mixed_in[:, :, query_width:]
    kv_send = jnp.stack(
        [jnp.where(even, kv_part[0], kv_part[3]), jnp.where(even, kv_part[1], kv_part[0])]
    )
    kv = lax.all_to_all(
        jnp.broadcast_to(kv_send[None], (16,) + kv_send.shape), X + ("z",), 0, 0
    )
    kv, attend_out = tie(kv, attend_out)
    attended, log_total = attend_forward(positions, queries, kv)
    attend_back = attended.reshape(XN * row_count, query_width)
    parts = [matmul(attended[k], attend_out) for k in range(XN)]
    first_rows = start_rows + scatter_chunks(parts)

    lower_columns = after(lower_columns, parts)
    (lower_unit,) = column_join(lower_columns, (unit_plan(unit_width),))
    lower_down = row_join(lower_rows)
    upper_rows = own_half(jnp.concatenate([recur_output, upper_drop], axis=0))
    upper_rows = lax.all_gather(after(upper_rows, parts), "z", axis=0)
    upper_columns = lax.all_gather(upper_columns, "z", axis=0)
    upper_unit, recur_in = column_join(
        upper_columns, (unit_plan(unit_width), half_plan(unit_width, channels))
    )
    recur_out = row_join(upper_rows[:, :recur_rows].reshape(4 * recur_rows, -1))
    upper_down = row_join(upper_rows[:, recur_rows:].reshape(4 * drop_rows, -1))

    parts, lower_kept = dense_forward(first_rows, lower_gain, lower_unit, lower_down)
    second_rows = first_rows + scatter_chunks(parts)

    normed_recur, recur_pull = jax.vjp(normalize, second_rows, recur_gain)
    recur_chunks, branches, _ = chunked(
        normed_recur.astype(BF16), lambda k, rows: matmul(rows, recur_in), lambda k, branch: branch
    )
    branch_y = [part[:, channels:] for part in branches]
    x_seq = to_sequence([part[:, :channels].astype(BF16) for part in branches]).astype(F32)
    block = x * 4 + z
    width = decay_gate.shape[1]
    own_decay = lax.dynamic_slice_in_dim(decay_rate, block * width, width, 0)
    own_taps = lax.dynamic_slice_in_dim(temporal_kernel, block * width, width, 1)
    own_decay_gate = lax.dynamic_index_in_dim(decay_gate, block, 0, keepdims=False)
    own_input_gate = lax.dynamic_index_in_dim(input_gate, block, 0, keepdims=False)
    shifted = [shift_down(x_seq, k) for k in range(tap_count)]
    conv_out = sum(own_taps[k] * shifted[k] for k in range(tap_count))
    conv_low = conv_out.astype(BF16)
    pre_decay = matmul(conv_low, own_decay_gate)
    pre_admit = matmul(conv_low, own_input_gate)
    (factors, updates), gate_pull = jax.vjp(gate_terms, pre_decay, pre_admit, conv_out, own_decay)
    states = linear_scan(factors, updates, False)
    out_grad = cotangent[0].astype(F32) * valid
    out_grad_chunks = gather_rows(after(out_grad.astype(BF16), x_seq))
    states_back = from_sequence(states.astype(BF16))
    states_back, out_grad_chunks = tie(states_back, out_grad_chunks)
    merge_pulls, merged_low, parts = [], [], []
    for part, y_part in zip(states_back, branch_y):
        merged, merge_pull = jax.vjp(branch_merge, part.astype(F32), y_part)
        merge_pulls.append(merge_pull)
        merged_low.append(merged.astype(BF16))
        parts.append(matmul(merged_low[-1], recur_out))
    third_rows = second_rows + scatter_chunks(parts)

    out_parts, upper_kept = dense_forward(third_rows, upper_gain, upper_unit, upper_down)

    residual_grad, grad_upper_gain, upper_unit_grad, upper_drop_grad, _ = dense_backward(
        out_grad, upper_kept, upper_unit, upper_down, out_grad_chunks
    )
    upper_unit_grad = reduce_z(upper_unit_grad)
    upper_drop_grad = reduce_z(upper_drop_grad)

    recur_grad_chunks, merged_grads, _ = chunked(
        residual_grad.astype(BF16),
        lambda k, rows: times_transposed(rows, recur_out),
        lambda k, merged_grad: merge_pulls[k](merged_grad),
    )
    fourth_rows = third_rows + scatter_chunks(after(out_parts, merged_grads))
    out_tokens = (fourth_rows * valid).astype(BF16)[None]
    state_grad = to_sequence([part[0].astype(BF16) for part in merged_grads]).astype(F32)
    adjoint = linear_scan(shift_up(factors, 1), state_grad, True)
    decay_grad, admit_grad, conv_grad, own_decay_grad = gate_pull(
        (adjoint * shift_down(states, 1), adjoint)
    )
    decay_grad_low, admit_grad_low = decay_grad.astype(BF16), admit_grad.astype(BF16)
    conv_grad = (
        conv_grad
        + times_transposed(decay_grad_low, own_decay_gate)
        + times_transposed(admit_grad_low, own_input_gate)
    )
    own_gate_grad = transposed_times(conv_low, decay_grad_low)
    own_admit_grad = transposed_times(conv_low, admit_grad_low)
    tap_grads = jnp.stack([jnp.sum(conv_grad * shifted[k], axis=0) for k in range(tap_count)])
    x_seq_grad = sum(own_taps[k] * shift_up(conv_grad, k) for k in range(tap_count))
    channel_grads = jnp.concatenate(
        [
            own_gate_grad,
            own_admit_grad,
            tap_grads,
            own_decay_grad[None],
            jnp.zeros((3, width), F32),
        ],
        axis=0,
    )
    channel_grads = butterfly(channel_grads, ("c", "y"))
    branch_x_grad = from_sequence(x_seq_grad.astype(BF16))
    branch_x_grad, out_tokens = tie(branch_x_grad, out_tokens)
    branch_grad = [
        jnp.concatenate([x_part, part[1].astype(BF16)], axis=1)
        for x_part, part in zip(branch_x_grad, merged_grads)
    ]
    normed_grad = scatter_chunks([times_transposed(part, recur_in) for part in branch_grad])
    recur_input_grad, grad_recur_gain = recur_pull(normed_grad)
    residual_grad = residual_grad + recur_input_grad
    residual_grad, upper_unit_grad, upper_drop_grad, channel_grads = tie(
        residual_grad, upper_unit_grad, upper_drop_grad, channel_grads
    )
    branch_grad, recur_grad_chunks = after((branch_grad, recur_grad_chunks), residual_grad)
    recur_in_grad = chunk_product(recur_chunks, branch_grad, half_pieces(2 * channels), True)
    recur_out_grad = chunk_product(merged_low, recur_grad_chunks, row_pieces(features), False)
    channel_grads = lax.all_gather(channel_grads, X + ("z",), axis=0)

    residual_grad, grad_lower_gain, lower_unit_grad, lower_drop_grad, recur_grads = dense_backward(
        residual_grad, lower_kept, lower_unit, lower_down, None, (recur_in_grad, recur_out_grad)
    )
    recur_in_grad, recur_out_grad = (reduce_z(grad) for grad in recur_grads)
    residual_grad, channel_grads = tie(residual_grad, channel_grads)
    grad_chunks = gather_rows(residual_grad.astype(BF16))
    grad_chunks, lower_unit_grad, lower_drop_grad = tie(
        grad_chunks, lower_unit_grad, lower_drop_grad
    )
    grad_rows = jnp.concatenate(grad_chunks, axis=0)
    lower_unit_grad = reduce_z(lower_unit_grad)
    lower_drop_grad = reduce_z(lower_drop_grad)
    attend_grad = times_transposed(grad_rows, attend_out).astype(BF16)
    query_grad, kv_grad = attend_backward(
        positions, queries, kv, attend_grad.reshape(queries.shape), log_total
    )
    kv_grad = lax.all_to_all(kv_grad, X + ("z",), 0, 0)
    packed, upper_plan = pack([upper_unit_grad, recur_in_grad], [upper_drop_grad, recur_out_grad])
    kv_grad, query_grad, packed = tie(kv_grad, query_grad, packed)
    packed = lax.psum_scatter(packed, "y", scatter_dimension=0, tiled=True)
    upper_packed = to_owners(packed, upper_plan)
    kv_grad = jnp.sum(kv_grad.astype(F32), axis=0).astype(BF16)
    nothing = jnp.zeros_like(kv_grad[0])
    kv_grad = jnp.stack(
        [
            jnp.where(even, kv_grad[0], kv_grad[1]),
            jnp.where(even, kv_grad[1], nothing),
            nothing,
            jnp.where(even, nothing, kv_grad[0]),
        ]
    )
    mixed_grad = jnp.concatenate([query_grad, kv_grad], axis=2).reshape(XN * row_count, -1)
    normed_grad = scatter_chunks(
        [
            times_transposed(mixed_grad[k * row_count : (k + 1) * row_count], attend_in)
            for k in range(XN)
        ]
    )
    mixed_chunks = [mixed_grad[k * row_count : (k + 1) * row_count] for k in range(XN)]
    attend_chunks = [attend_rows[k * row_count : (k + 1) * row_count] for k in range(XN)]
    in_grad = reduce_z_direct(
        chunk_product(attend_chunks, mixed_chunks, row_pieces(mixed_grad.shape[1]), True)
    )
    out_grad = reduce_z_direct(
        chunk_product([attended[k] for k in range(XN)], grad_chunks, row_pieces(features), False)
    )
    packed, lower_plan = pack([lower_unit_grad, in_grad], [lower_drop_grad, out_grad])
    packed = lax.psum_scatter(packed, "y", scatter_dimension=0, tiled=True)
    packed, normed_grad, upper_packed = tie(packed, normed_grad, upper_packed)
    upper_packed = spread(upper_packed)
    lower_packed = spread(to_owners(packed, lower_plan))
    attend_input_grad, grad_attend_gain = attend_pull(normed_grad)
    residual_grad = residual_grad + attend_input_grad
    grad_decay_gate = channel_grads[:, :width]
    grad_input_gate = channel_grads[:, width : 2 * width]
    grad_temporal_kernel = (
        channel_grads[:, 2 * width : 2 * width + tap_count]
        .transpose(1, 0, 2)
        .reshape(tap_count, -1)
    )
    grad_decay_rate = channel_grads[:, 2 * width + tap_count].reshape(-1)
    gains = butterfly(
        jnp.stack([grad_attend_gain, grad_lower_gain, grad_recur_gain, grad_upper_gain]),
        ("c", "xl", "xh", "z", "y"),
    )
    upper_grads = unpack(
        upper_packed,
        upper_plan,
        (("unit", unit_width, 0), ("half", channels, 2)),
        [a.shape for a in (upper_gate, upper_lift, recur_input, recur_branch, upper_drop, recur_output)],
    )
    lower_grads = unpack(
        lower_packed,
        lower_plan,
        (("unit", unit_width, 0), ("attend", in_grad.shape[1], 2)),
        [a.shape for a in (lower_gate, lower_lift, query_weight, keyval_weight, lower_drop, attend_output)],
    )
    return (
        out_tokens,
        residual_grad[None],
        gains[0],
        *lower_grads[2:4],
        lower_grads[5],
        gains[1],
        *lower_grads[:2],
        lower_grads[4],
        gains[2],
        *upper_grads[2:4],
        upper_grads[5],
        grad_temporal_kernel,
        grad_decay_gate,
        grad_input_gate,
        grad_decay_rate,
        gains[3],
        *upper_grads[:2],
        upper_grads[4],
    )


def solution(mesh):
    grid = Mesh(mesh.devices.reshape(-1, 2, 2, 2, 4), ("y", "c", "xh", "xl", "z"))
    rows = P(("y", "c"), ("xl", "z", "xh"), None)
    weight = P(("xh", "xl", "z"), None)
    same = P()
    return jax.shard_map(
        body,
        mesh=grid,
        in_specs=(
            (rows, P(("y", "c")), rows)
            + (same, weight, weight, weight)
            + (same, weight, weight, weight)
            + (same, weight, weight, weight, same, same, same, same)
            + (same, weight, weight, weight)
        ),
        out_specs=(
            (rows, rows)
            + (same, weight, weight, weight)
            + (same, weight, weight, weight)
            + (same, weight, weight, weight, same, same, same, same)
            + (same, weight, weight, weight)
        ),
        check_vma=False,
    )
```

time: 1200 us -> 905 us (0.75)
  waiting for transfers between devices: 511 us -> 375 us
  blocking collectives: 134 us -> 0 us
  starting transfers between devices: 239 us -> 165 us
  Pallas kernels: 17.2 us -> 69.2 us
  matrix products: 93.5 us -> 120 us
  local copies, waits for them, and re-layouts: 81.1 us -> 59.6 us
    ppermute x75 -> x70, waiting for transfers between devices: 284 us -> 211 us  [the longest x24 98.4 us: from_x(): return lax.ppermute(value, X, [((i + by) % XN, i) for i in range(XN)])]
    psum x1 -> x0, blocking collectives: 68.8 us -> none  [body(): lax.psum(jnp.stack([grad_attend_gain, grad_lower_gain, grad_recur_gain, g...]
    ppermute x75 -> x70, starting transfers between devices: 152 us -> 88.6 us  [the longest x22 33.3 us: flip(): lax.ppermute(value, axis, [(i, i ^ by) for i in range(lax.axis_size(axis))])]
    reduce_scatter x8, waiting for transfers between devices: 128 us -> 64.8 us  [the longest x2 33.2 us: body(): packed = lax.psum_scatter(packed, 'y', scatter_dimension=0, tiled=True)]
    pallas_call x0 -> x14, Pallas kernels: none -> 51 us  [the longest x8 31.7 us: chunk_product(): pl.pallas_call(functools.partial(product_kernel, count, pieces, split), g...]
    dot_general x10 -> x31, matrix products: 34.7 us -> 81.8 us  [times_transposed(): lax.dot_general(left, right, (((1,), (1,)), ((), ())), preferred_element_...]
    all_gather x2 -> x0, blocking collectives: 36.7 us -> none  [gather_x(): return lax.all_gather(value, X, axis=0, tiled=True)]
    ppermute x48 -> x15, starting transfers between devices: 63.9 us -> 29.1 us  [swap(): return lax.ppermute(value, 'c', [(0, 1), (1, 0)])]
  transfers between devices with their start and end apart: 142 -> 111, of which waited for: 66 -> 53; matrix products, arithmetic and copies ran while one was open for 18% -> 25% of each run, Pallas kernels for 1% -> 7%
where the time goes in v2:
time: 905 us; the launch traced here: 893 us
  waiting for transfers between devices  375 us (41%)
  starting transfers between devices  165 us (18%)
  matrix products  120 us (13%)
  other arithmetic  85 us (9%)
  Pallas kernels  69.2 us (8%)
  local copies, waits for them, and re-layouts  59.6 us (7%)
  between operations  18.6 us (2%)
    ppermute x24, waiting for transfers between devices, from_x(): return lax.ppermute(value, X, [((i + by) % XN, i) for i in range(XN)])  98.4 us
    dot_general x31, matrix products, times_transposed(): lax.dot_general(left, right, (((1,), (1,)), ((), ())), preferred_element_...  81.8 us
    ppermute x24, waiting for transfers between devices, to_x(): return lax.ppermute(value, X, [(i, (i + by) % XN) for i in range(XN)])  71.3 us
    ppermute x22, waiting for transfers between devices, flip(): lax.ppermute(value, axis, [(i, i ^ by) for i in range(lax.axis_size(axis))])  41.8 us
    dot_general x31, matrix products, matmul(): return jnp.dot(left, right, preferred_element_type=F32)  36.9 us
    ppermute x22, starting transfers between devices, flip(): lax.ppermute(value, axis, [(i, i ^ by) for i in range(lax.axis_size(axis))])  33.3 us
    reduce_scatter x2, waiting for transfers between devices, body(): packed = lax.psum_scatter(packed, 'y', scatter_dimension=0, tiled=True)  33.2 us
    ppermute x24, starting transfers between devices, to_x(): return lax.ppermute(value, X, [(i, (i + by) % XN) for i in range(XN)])  32.6 us
  transfers between devices with their start and end apart: 111, of which 53 were waited for; matrix products, arithmetic and copies ran while one was open for 25% of the time, Pallas kernels for 7%

profile of v2, /device:TPU:1, one launch (start us, length us, event | category | flops | bytes accessed | tf_op | source)
XLA Modules:
  0.0 893.1 jit_solution(18120231224796382710)
XLA Ops:
  31.7 15.2 %collective-permute-done = bf16[128,1536]{1,0:T(8,128)(2,1)S(1)} collective-permute-done((bf16[128,1536]{1,0:T(8,128)(2,1)S(1)}, bf16[128,1536]{1,0:T(8,128)(2,1)S(1)}, u32[]{:S(2)}, u32[]{:S(2)}) %collective-permute-start) | collective-permute-done | bytes 393248 | tf_op jit(solution)/shard_map/ppermute | solution.py:26
  48.5 8.5 collective-permute-done.2
  85.4 15.3 %all-to-all-done.2 = bf16[4,96,1792]{2,1,0:T(8,128)(2,1)} async-done(((bf16[4,96,1792]{2,1,0:T(8,128)(2,1)}), bf16[4,96,1792]{2,1,0:T(8,128)(2,1)}, u32[]{:S(2)}, u32[]{:S(2)}) %all-to-all-start.2) | async-done | bytes 1376288 | tf_op jit(solution)/shard_map/all_to_all | solution.py:50
  122.1 15.6 %all-to-all-done.3.kv_ref = bf16[16,2,128,128]{3,2,1,0:T(8,128)(2,1)S(1)} async-done(((bf16[16,2,128,128]{3,2,1,0:T(8,128)(2,1)}), bf16[16,2,128,128]{3,2,1,0:T(8,128)(2,1)S(1)}, u32[]{:S(2)}, u32[]{:S(2)}) %all-to-all-start.3) | async-done | bytes 1048608 | tf_op jit(solution)/shard_map/all_to_all | solution.py:777
  137.7 6.8 shard_map.390
  149.0 7.1 collective-permute-done.11
  156.1 10.7 %collective-permute-done.12 = bf16[128,1536]{1,0:T(8,128)(2,1)S(1)} collective-permute-done((bf16[128,1536]{1,0:T(8,128)(2,1)S(1)}, bf16[128,1536]{1,0:T(8,128)(2,1)S(1)}, u32[]{:S(2)}, u32[]{:S(2)}) %collective-permute-start.12) | collective-permute-done | bytes 393248 | tf_op jit(solution)/shard_map/ppermute | solution.py:30
  214.0 7.6 collective-permute-done.17
  281.8 8.0 collective-permute-done.26.refs_5_
  291.4 8.7 collective-permute-done.28.refs_7_
  312.5 9.2 %collective-permute-done.32 = bf16[128,1536]{1,0:T(8,128)(2,1)S(1)} collective-permute-done((bf16[128,1536]{1,0:T(8,128)(2,1)S(1)}, bf16[128,1536]{1,0:T(8,128)(2,1)S(1)}, u32[]{:S(2)}, u32[]{:S(2)}) %collective-permute-start.32) | collective-permute-done | bytes 393248 | tf_op jit(solution)/shard_map/ppermute | solution.py:30
  328.2 13.2 %collective-permute-done.34.refs_2_ = bf16[128,1536]{1,0:T(8,128)(2,1)S(1)} collective-permute-done((bf16[128,1536]{1,0:T(8,128)(2,1)S(1)}, bf16[128,1536]{1,0:T(8,128)(2,1)S(1)}, u32[]{:S(2)}, u32[]{:S(2)}) %collective-permute-start.34) | collective-permute-done | bytes 393248 | tf_op jit(solution)/shard_map/ppermute | solution.py:26
  363.8 7.6 collective-permute-done.37
  403.3 14.6 %collective-permute-done.41.refs_6_ = bf16[128,1536]{1,0:T(8,128)(2,1)S(1)} collective-permute-done((bf16[128,1536]{1,0:T(8,128)(2,1)S(1)}, bf16[128,1536]{1,0:T(8,128)(2,1)S(1)}, u32[]{:S(2)}, u32[]{:S(2)}) %collective-permute-start.41) | collective-permute-done | bytes 393248 | tf_op jit(solution)/shard_map/ppermute | solution.py:26
  505.0 7.8 collective-permute-done.47
  540.8 6.4 convolution_convert_fusion.7
  572.5 10.2 %collective-permute-done.57 = bf16[128,1536]{1,0:T(8,128)(2,1)S(1)} collective-permute-done((bf16[128,1536]{1,0:T(8,128)(2,1)S(1)}, bf16[128,1536]{1,0:T(8,128)(2,1)S(1)}, u32[]{:S(2)}, u32[]{:S(2)}) %collective-permute-start.57) | collective-permute-done | bytes 393248 | tf_op jit(solution)/shard_map/ppermute | solution.py:30
  634.6 9.3 %collective-permute-done.64.refs_7_ = bf16[128,1536]{1,0:T(8,128)(2,1)S(1)} collective-permute-done((bf16[128,1536]{1,0:T(8,128)(2,1)S(1)}, bf16[128,1536]{1,0:T(8,128)(2,1)S(1)}, u32[]{:S(2)}, u32[]{:S(2)}) %collective-permute-start.64) | collective-permute-done | bytes 393248 | tf_op jit(solution)/shard_map/ppermute | solution.py:26
  647.1 9.0 %shard_map.401 = (bf16[4,128,384]{2,1,0:T(8,128)(2,1)S(1)}, bf16[16,2,128,128]{3,2,1,0:T(8,128)(2,1)}) custom-call(s32[4]{0:T(128)S(1)} %copy-done.65, bf16[4,128,384]{2,1,0:T(8,128)(2,1)S(1)} %copy-done.9, bf16[16,2,128,128]{3,2,1,0:T(8,128)(2,1)S(1)} %all-to-all-done.3.kv_ref, bf16[4,128,384]{2,1,0:T(8,128)(2,1)S(1)} %bitcast.445, f32[4,384,1]{2,1,0:T(8,128)S(1)} %copy-done.23), custom_call_target="tpu_custom_call" | custom-call | bytes 32400000 | tf_op jit(solution)/shard_map/pallas_call | solution.py:322
  665.0 12.0 %all-to-all-done.8 = bf16[16,2,128,128]{3,2,1,0:T(8,128)(2,1)} async-done(((bf16[16,2,128,128]{3,2,1,0:T(8,128)(2,1)}), bf16[16,2,128,128]{3,2,1,0:T(8,128)(2,1)}, u32[]{:S(2)}, u32[]{:S(2)}) %all-to-all-start.8) | async-done | bytes 1048608 | tf_op jit(solution)/shard_map/all_to_all | solution.py:906
  711.4 31.6 %reduce-scatter.13.cloned.1.call-done.refs_0_ = bf16[384,1280]{1,0:T(8,128)(2,1)} async-done(((bf16[1536,1280]{1,0:T(8,128)(2,1)}), bf16[384,1280]{1,0:T(8,128)(2,1)}) %reduce-scatter.13.cloned.1.call-update) | async-done | bytes 983056 | tf_op jit(solution)/shard_map/reduce_scatter | solution.py:503
  757.5 16.4 %reduce-scatter.23.cloned.1.call-done = bf16[2048,128]{1,0:T(8,128)(2,1)} async-done(((bf16[8192,128]{1,0:T(8,128)(2,1)}), bf16[2048,128]{1,0:T(8,128)(2,1)}) %reduce-scatter.23.cloned.1.call-update) | async-done | bytes 524304 | tf_op jit(solution)/shard_map/reduce_scatter | solution.py:909
  787.1 16.8 %reduce-scatter.21.cloned.1.call-done = bf16[1728,128]{1,0:T(8,128)(2,1)} async-done(((bf16[6912,128]{1,0:T(8,128)(2,1)}), bf16[1728,128]{1,0:T(8,128)(2,1)}) %reduce-scatter.21.cloned.1.call-update) | async-done | bytes 442384 | tf_op jit(solution)/shard_map/reduce_scatter | solution.py:937
  852.0 28.5 %all-gather.16.cloned.1.call-done.packed = bf16[16384,128]{1,0:T(8,128)(2,1)} async-done(((bf16[2048,128]{1,0:T(8,128)(2,1)}), bf16[16384,128]{1,0:T(8,128)(2,1)}) %all-gather.16.cloned.1.call-update) | async-done | bytes 4194320 | tf_op jit(solution)/shard_map/all_gather | solution.py:634
  (911 shorter events, 578.4 us)
Async XLA Ops:
  7.2 93.6 %all-gather.12.cloned.1.call-start = ((), (), s32[]{:S(2)}) async-start(), calls=%async_computation.19 | async-start | bytes 2211840 | tf_op jit(solution)/shard_map/all_gather | solution.py:748
  24.2 32.9 %all-to-all-start.1 = ((bf16[4,96,1280]{2,1,0:T(8,128)(2,1)}), bf16[4,96,1280]{2,1,0:T(8,128)(2,1)S(1)}, u32[]{:S(2)}, u32[]{:S(2)}) async-start(bf16[4,96,1280]{2,1,0:T(8,128)(2,1)} %maximum_maximum_fusion.1), calls=%async_computation.1 | async-start | bytes 1966080 | tf_op jit(solution)/shard_map/all_to_all | solution.py:50
  27.7 140.5 %all-gather.18.cloned.1.call-start = ((), (), s32[]{:S(2)}) async-start(), calls=%async_computation.30 | async-start | bytes 4915200 | tf_op jit(solution)/shard_map/all_gather | solution.py:767
  82.0 105.6 %all-gather.20.cloned.1.call-start = ((), (), s32[]{:S(2)}) async-start(), calls=%async_computation.31 | async-start | bytes 6881280 | tf_op jit(solution)/shard_map/all_gather | solution.py:791
  120.7 128.9 %all-gather.22.cloned.1.call-start = ((), (), s32[]{:S(2)}) async-start(), calls=%async_computation.32 | async-start | bytes 3194880 | tf_op jit(solution)/shard_map/all_gather | solution.py:790
  187.6 38.1 %collective-permute-start.22 = (bf16[4,4,96,1792]{3,2,1,0:T(8,128)(2,1)}, bf16[4,4,96,1792]{3,2,1,0:T(8,128)(2,1)S(1)}, u32[]{:S(2)}, u32[]{:S(2)}) collective-permute-start(bf16[4,4,96,1792]{3,2,1,0:T(8,128)(2,1)} %bitcast.438), channel_id=1, source_target_pairs={{0,16},{16,0},{1,17},{17,1},{2,18},{18,2},{3,19},{19,3},{4,20},{20... | collective-permute-start | bytes 16515080 | tf_op jit(solution)/shard_map/ppermute | solution.py:46
  267.3 250.3 %reduce-scatter.11.cloned.1.call-start = ((), (), s32[]{:S(2)}) async-start(), calls=%async_computation.21 | async-start | bytes 2211840 | tf_op jit(solution)/shard_map/reduce_scatter | solution.py:503
  271.4 33.2 %collective-permute-start.29 = (bf16[1152,768]{1,0:T(8,128)(2,1)}, bf16[1152,768]{1,0:T(8,128)(2,1)}, u32[]{:S(2)}, u32[]{:S(2)}) collective-permute-start(bf16[1152,768]{1,0:T(8,128)(2,1)} %bitcast.101), channel_id=1, source_target_pairs={{0,16},{16,0},{1,17},{17,1},{2,18},{18,2},{3,19},{19,3},{4,20},{20... | collective-permute-start | bytes 5308424 | tf_op jit(solution)/shard_map/ppermute | solution.py:46
  322.5 32.3 %collective-permute-start.36 = (bf16[128,1536]{1,0:T(8,128)(2,1)S(1)}, bf16[128,1536]{1,0:T(8,128)(2,1)S(1)}, u32[]{:S(2)}, u32[]{:S(2)}) collective-permute-start(bf16[128,1536]{1,0:T(8,128)(2,1)S(1)} %multiply_convert_fusion.1.refs_0_), channel_id=1, source_target_pairs={{4,0},{8,4},{12,8},{0,12},{5,1},{9,5},{13,9},{1,13},{6,2},{10,6},{... | collective-permute-start | bytes 1179656 | tf_op jit(solution)/shard_map/ppermute | solution.py:26
  389.7 33.9 %collective-permute-start.49 = (bf16[4,4,96,1280]{3,2,1,0:T(8,128)(2,1)}, bf16[4,4,96,1280]{3,2,1,0:T(8,128)(2,1)}, u32[]{:S(2)}, u32[]{:S(2)}) collective-permute-start(bf16[4,4,96,1280]{3,2,1,0:T(8,128)(2,1)} %get-tuple-element.196), channel_id=1, source_target_pairs={{0,16},{16,0},{1,17},{17,1},{2,18},{18,2},{3,19},{19,3},{4,20},{20... | collective-permute-start | bytes 11796488 | tf_op jit(solution)/shard_map/ppermute | solution.py:46
  391.5 126.1 %reduce-scatter.9.cloned.1.call-start = ((), (), s32[]{:S(2)}) async-start(), calls=%async_computation.20 | async-start | bytes 4915200 | tf_op jit(solution)/shard_map/reduce_scatter | solution.py:503
  445.1 33.6 %collective-permute-start.43 = (bf16[128,1536]{1,0:T(8,128)(2,1)}, bf16[128,1536]{1,0:T(8,128)(2,1)}, u32[]{:S(2)}, u32[]{:S(2)}) collective-permute-start(bf16[128,1536]{1,0:T(8,128)(2,1)} %fusion.186), channel_id=1, source_target_pairs={{0,8},{4,12},{8,0},{12,4},{1,9},{5,13},{9,1},{13,5},{2,10},{6,14},... | collective-permute-start | bytes 1179656 | tf_op jit(solution)/shard_map/ppermute | solution.py:30
  446.6 32.1 %collective-permute-start.44 = (bf16[128,1536]{1,0:T(8,128)(2,1)}, bf16[128,1536]{1,0:T(8,128)(2,1)}, u32[]{:S(2)}, u32[]{:S(2)}) collective-permute-start(bf16[128,1536]{1,0:T(8,128)(2,1)} %fusion.187), channel_id=1, source_target_pairs={{0,4},{4,8},{8,12},{12,0},{1,5},{5,9},{9,13},{13,1},{2,6},{6,10},{... | collective-permute-start | bytes 1179656 | tf_op jit(solution)/shard_map/ppermute | solution.py:30
  446.6 32.1 %collective-permute-start.45 = (bf16[128,1536]{1,0:T(8,128)(2,1)}, bf16[128,1536]{1,0:T(8,128)(2,1)}, u32[]{:S(2)}, u32[]{:S(2)}) collective-permute-start(bf16[128,1536]{1,0:T(8,128)(2,1)} %fusion.185), channel_id=1, source_target_pairs={{0,12},{4,0},{8,4},{12,8},{1,13},{5,1},{9,5},{13,9},{2,14},{6,2},{... | collective-permute-start | bytes 1179656 | tf_op jit(solution)/shard_map/ppermute | solution.py:30
  476.2 143.7 %all-gather.24.cloned.1.call-start = ((), (), s32[]{:S(2)}) async-start(), calls=%async_computation.33 | async-start | bytes 2297856 | tf_op jit(solution)/shard_map/all_gather | solution.py:888
  532.8 29.1 %collective-permute-start.54 = (bf16[128,1536]{1,0:T(8,128)(2,1)}, bf16[128,1536]{1,0:T(8,128)(2,1)S(1)}, u32[]{:S(2)}, u32[]{:S(2)}) collective-permute-start(bf16[128,1536]{1,0:T(8,128)(2,1)} %convert_element_type.583.refs_4_), channel_id=1, source_target_pairs={{8,0},{12,4},{0,8},{4,12},{9,1},{13,5},{1,9},{5,13},{10,2},{14,6},... | collective-permute-start | bytes 1179656 | tf_op jit(solution)/shard_map/ppermute | solution.py:26
  535.0 126.4 %reduce-scatter.17.cloned.1.call-start = ((), (), s32[]{:S(2)}) async-start(), calls=%async_computation.24 | async-start | bytes 983040 | tf_op jit(solution)/shard_map/reduce_scatter | solution.py:503
  603.1 58.2 %reduce-scatter.15.cloned.1.call-start = ((), (), s32[]{:S(2)}) async-start(), calls=%async_computation.23 | async-start | bytes 1966080 | tf_op jit(solution)/shard_map/reduce_scatter | solution.py:503
  612.8 98.5 %reduce-scatter.19.cloned.1.call-start = ((), (), s32[]{:S(2)}) async-start(), calls=%async_computation.25 | async-start | bytes 2211840 | tf_op jit(solution)/shard_map/reduce_scatter | solution.py:503
  643.9 99.1 %reduce-scatter.13.cloned.1.call-start = ((), (), s32[]{:S(2)}) async-start(), calls=%async_computation.22 | async-start | bytes 4915200 | tf_op jit(solution)/shard_map/reduce_scatter | solution.py:503
  661.3 112.7 %reduce-scatter.23.cloned.1.call-start = ((), (), s32[]{:S(2)}) async-start(), calls=%async_computation.27 | async-start | bytes 2621440 | tf_op jit(solution)/shard_map/reduce_scatter | solution.py:909
  677.0 126.8 %reduce-scatter.21.cloned.1.call-start = ((), (), s32[]{:S(2)}) async-start(), calls=%async_computation.26 | async-start | bytes 2211840 | tf_op jit(solution)/shard_map/reduce_scatter | solution.py:937
  809.5 37.4 %all-gather.14.cloned.1.call-start = ((), (), s32[]{:S(2)}) async-start(), calls=%async_computation.28 | async-start | bytes 3981312 | tf_op jit(solution)/shard_map/all_gather | solution.py:634
  816.2 64.3 %all-gather.16.cloned.1.call-start = ((), (), s32[]{:S(2)}) async-start(), calls=%async_computation.29 | async-start | bytes 4718592 | tf_op jit(solution)/shard_map/all_gather | solution.py:634
  (302 other events, 3439.4 us)
Sparse Core Ops, SparseCore 0:
  10.3 31.5 all-gather.11
  58.3 50.3 all-gather.17
  110.3 70.5 all-gather.19
  183.0 34.3 all-gather.21
  391.6 28.4 reduce-scatter.10
  429.7 52.1 reduce-scatter.8
  535.1 44.6 all-gather.23
  603.3 20.4 reduce-scatter.16
  626.9 25.7 reduce-scatter.14
  655.6 35.9 reduce-scatter.18
  694.1 48.7 reduce-scatter.12
  745.2 28.6 reduce-scatter.22
  777.1 26.6 reduce-scatter.20
  816.3 29.1 all-gather.13
  847.6 32.7 all-gather.15

commit v3 on v2

--- a/solution.py
+++ b/solution.py
@@ -50,6 +50,17 @@
     return lax.all_to_all(value, X, 0, 0)
 
 
+def exchange_direct(value):
+    x = x_index()
+    out = jnp.zeros_like(value)
+    for r in range(XN):
+        piece = lax.dynamic_index_in_dim(value, (x + r) % XN, 0, keepdims=True)
+        if r:
+            piece = to_x(piece, r)
+        out = lax.dynamic_update_slice_in_dim(out, piece, (x + XN - r) % XN, 0)
+    return out
+
+
 def by_core(mine, other):
     first = lax.axis_index("c") == 0
     return jnp.where(first, mine, other), jnp.where(first, other, mine)
@@ -102,15 +113,17 @@
     return [low] + [from_x(low, r) for r in range(1, XN)]
 
 
-def chunked(low, begin, end, side=()):
+def chunked(low, begin, end, side=None):
     near = {1: from_x(low, 1), 3: from_x(low, 3)}
     first, later = tie(begin(0, low), low)
-    far, side = tie(from_x(later, 2), side)
-    chunks = [low, near[1], far, near[3]]
+    far = from_x(later, 2)
     outs = [end(0, first)] + [None] * (XN - 1)
-    for k in (1, 3, 2):
-        outs[k] = end(k, begin(k, chunks[k]))
-    return chunks, outs, side
+    extra = side((outs[0], near[1], near[3])) if side else None
+    for k in (1, 3):
+        outs[k] = end(k, begin(k, near[k]))
+    far, outs[1], outs[3] = tie(far, outs[1], outs[3])
+    outs[2] = end(2, begin(2, far))
+    return [low, near[1], far, near[3]], outs, extra
 
 
 def scatter_chunks(parts):
@@ -503,13 +516,13 @@
     return lax.psum_scatter(grad, "z", scatter_dimension=0, tiled=True)
 
 
-def reduce_z_direct(grad):
-    z = lax.axis_index("z")
+def reduce_direct(grad, axis):
+    at = lax.axis_index(axis)
     parts = grad.reshape(4, -1, grad.shape[1])
-    total = lax.dynamic_index_in_dim(parts, z, 0, keepdims=False).astype(F32)
-    for by in range(1, 4):
-        piece = lax.dynamic_index_in_dim(parts, z ^ by, 0, keepdims=False)
-        total = total + flip(piece, "z", by).astype(F32)
+    total = lax.dynamic_index_in_dim(parts, at, 0, keepdims=False).astype(F32)
+    for by in (2, 1, 3):
+        piece = lax.dynamic_index_in_dim(parts, at ^ by, 0, keepdims=False)
+        total = total + flip(piece, axis, by).astype(F32)
     return total.astype(BF16)
 
 
@@ -634,6 +647,15 @@
     return lax.all_gather(part, ("y", "c"), axis=0, tiled=True)
 
 
+def spread_direct(part):
+    y = lax.axis_index("y")
+    out = jnp.zeros((4,) + part.shape, part.dtype)
+    for by in range(4):
+        piece = flip(part, "y", by) if by else part
+        out = lax.dynamic_update_slice_in_dim(out, piece[None], y ^ by, 0)
+    return jnp.stack(by_core(out, swap(out)), axis=1).reshape(-1, part.shape[1])
+
+
 def unpack(packed, plan, kinds, shapes):
     return pl.pallas_call(
         functools.partial(unpack_kernel, plan, kinds),
@@ -669,7 +691,7 @@
     return parts, (norm_pull, chunks, kept)
 
 
-def dense_backward(residual_grad, stored, unit_weight, drop_weight, grad_chunks=None, side=()):
+def dense_backward(residual_grad, stored, unit_weight, drop_weight, grad_chunks=None, side=None):
     norm_pull, chunks, kept = stored
     pre_grads = [None] * XN
 
@@ -681,20 +703,25 @@
         pre_grads[k] = jnp.concatenate([part.astype(BF16) for part in pre_grad], axis=1)
         return times_transposed(pre_grads[k], unit_weight)
 
+    extra = None
     if grad_chunks is None:
-        grad_chunks, parts, side = chunked(residual_grad.astype(BF16), begin, end, side)
+        grad_chunks, parts, extra = chunked(residual_grad.astype(BF16), begin, end, side)
     else:
         parts = [None] * XN
         for k in (0, 1, 3, 2):
             parts[k] = end(k, begin(k, grad_chunks[k]))
     input_grad, gain_grad = norm_pull(scatter_chunks(parts))
-    residual_grad = residual_grad + input_grad
-    pre_grads, grad_chunks = after((pre_grads, grad_chunks), residual_grad)
-    unit_grad = chunk_product(chunks, pre_grads, unit_pieces(unit_weight.shape[1] // 2), True)
-    drop_grad = chunk_product(
-        [hidden for hidden, _ in kept], grad_chunks, row_pieces(drop_weight.shape[1]), False
-    )
-    return residual_grad, gain_grad, unit_grad, drop_grad, side
+
+    def products(done):
+        pre, grads = after((pre_grads, grad_chunks), done)
+        return (
+            chunk_product(chunks, pre, unit_pieces(unit_weight.shape[1] // 2), True),
+            chunk_product(
+                [hidden for hidden, _ in kept], grads, row_pieces(drop_weight.shape[1]), False
+            ),
+        )
+
+    return residual_grad + input_grad, gain_grad, products, extra
 
 
 def body(
@@ -739,36 +766,37 @@
     normed_attend, attend_pull = jax.vjp(normalize, start_rows, attend_gain)
     member_query = query_weight.reshape(-1, XN, query_width).transpose(1, 0, 2)
     member_kv = jnp.stack([keyval_weight[:, (m % 2) * size : (m % 2 + 1) * size] for m in range(XN)])
-    attend_columns = exchange_x(own_half(jnp.concatenate([member_query, member_kv], axis=2)))
-    lower_gate, lower_lift = after((lower_gate, lower_lift), attend_columns)
     lower_columns = exchange_x(
         jnp.concatenate([unit_slices(lower_gate), unit_slices(lower_lift)], axis=2)
     )
     unit_width = lower_columns.shape[2]
+    attend_columns = own_half(jnp.concatenate([member_query, member_kv], axis=2))
+    half_in = lax.all_to_all(jnp.repeat(attend_columns, 4, axis=0), X + ("z",), 0, 0)
+    attend_in = row_join(half_in.reshape(features, -1))
+    half_out = gather_direct(own_half(attend_output)[None])
     lower_rows = lax.all_gather(own_half(lower_drop), "z", axis=0, tiled=True)
-    half_in = gather_direct(attend_columns).reshape(features, -1)
-    attend_in = row_join(half_in)
 
     attend_rows = jnp.concatenate(gather_rows(normed_attend.astype(BF16)), axis=0)
-    attend_rows, lower_columns = tie(attend_rows, lower_columns)
-    later = (recur_input, recur_branch, upper_gate, upper_lift)
-    recur_input, recur_branch, upper_gate, upper_lift = after(later, lower_columns)
-    upper_columns = exchange_x(
+    attend_rows, attend_in, lower_columns, lower_rows, half_out = tie(
+        attend_rows, attend_in, lower_columns, lower_rows, half_out
+    )
+    lower_columns = lax.all_gather(lower_columns, "z", axis=0)
+    recur_input, recur_branch, upper_gate, upper_lift = after(
+        (recur_input, recur_branch, upper_gate, upper_lift), attend_rows
+    )
+    upper_columns = exchange_direct(
         jnp.concatenate(
             [
+                half_slices(recur_input),
+                half_slices(recur_branch),
                 unit_slices(upper_gate),
                 unit_slices(upper_lift),
-                half_slices(recur_input),
-                half_slices(recur_branch),
             ],
             axis=2,
         )
     )
-    lower_columns = lax.all_gather(lower_columns, "z", axis=0)
     mixed_in = matmul(attend_rows, attend_in).astype(BF16).reshape(XN, row_count, -1)
-    mixed_in, lower_rows, upper_columns = tie(mixed_in, lower_rows, upper_columns)
-    half_out = own_half(after(attend_output, mixed_in))
-    attend_out = row_join(gather_direct(half_out[None]).reshape(query_width, -1))
+    attend_out = row_join(half_out.reshape(query_width, -1))
     queries = mixed_in[:, :, :query_width]
     kv_part = mixed_in[:, :, query_width:]
     kv_send = jnp.stack(
@@ -777,26 +805,28 @@
     kv = lax.all_to_all(
         jnp.broadcast_to(kv_send[None], (16,) + kv_send.shape), X + ("z",), 0, 0
     )
-    kv, attend_out = tie(kv, attend_out)
+    out_grad = cotangent[0].astype(F32) * valid
+    out_grad_chunks = gather_rows(after(out_grad.astype(BF16), kv))
     attended, log_total = attend_forward(positions, queries, kv)
+    attended, out_grad_chunks = tie(attended, out_grad_chunks)
     attend_back = attended.reshape(XN * row_count, query_width)
     parts = [matmul(attended[k], attend_out) for k in range(XN)]
     first_rows = start_rows + scatter_chunks(parts)
-
-    lower_columns = after(lower_columns, parts)
+    first_rows, upper_columns = tie(first_rows, upper_columns)
+
+    lower_columns, lower_rows = after((lower_columns, lower_rows), first_rows)
     (lower_unit,) = column_join(lower_columns, (unit_plan(unit_width),))
     lower_down = row_join(lower_rows)
+    recur_columns = lax.all_gather(upper_columns[:, :, :channels], "z", axis=0)
     upper_rows = own_half(jnp.concatenate([recur_output, upper_drop], axis=0))
     upper_rows = lax.all_gather(after(upper_rows, parts), "z", axis=0)
-    upper_columns = lax.all_gather(upper_columns, "z", axis=0)
-    upper_unit, recur_in = column_join(
-        upper_columns, (unit_plan(unit_width), half_plan(unit_width, channels))
-    )
-    recur_out = row_join(upper_rows[:, :recur_rows].reshape(4 * recur_rows, -1))
-    upper_down = row_join(upper_rows[:, recur_rows:].reshape(4 * drop_rows, -1))
+    upper_columns = lax.all_gather(after(upper_columns, parts)[:, :, channels:], "z", axis=0)
 
     parts, lower_kept = dense_forward(first_rows, lower_gain, lower_unit, lower_down)
     second_rows = first_rows + scatter_chunks(parts)
+    recur_columns, upper_rows = after((recur_columns, upper_rows), second_rows)
+    (recur_in,) = column_join(recur_columns, (half_plan(0, channels),))
+    recur_out = row_join(upper_rows[:, :recur_rows].reshape(4 * recur_rows, -1))
 
     normed_recur, recur_pull = jax.vjp(normalize, second_rows, recur_gain)
     recur_chunks, branches, _ = chunked(
@@ -804,6 +834,9 @@
     )
     branch_y = [part[:, channels:] for part in branches]
     x_seq = to_sequence([part[:, :channels].astype(BF16) for part in branches]).astype(F32)
+    upper_columns, upper_rows = after((upper_columns, upper_rows), branches)
+    (upper_unit,) = column_join(upper_columns, (unit_plan(unit_width),))
+    upper_down = row_join(upper_rows[:, recur_rows:].reshape(4 * drop_rows, -1))
     block = x * 4 + z
     width = decay_gate.shape[1]
     own_decay = lax.dynamic_slice_in_dim(decay_rate, block * width, width, 0)
@@ -817,10 +850,7 @@
     pre_admit = matmul(conv_low, own_input_gate)
     (factors, updates), gate_pull = jax.vjp(gate_terms, pre_decay, pre_admit, conv_out, own_decay)
     states = linear_scan(factors, updates, False)
-    out_grad = cotangent[0].astype(F32) * valid
-    out_grad_chunks = gather_rows(after(out_grad.astype(BF16), x_seq))
     states_back = from_sequence(states.astype(BF16))
-    states_back, out_grad_chunks = tie(states_back, out_grad_chunks)
     merge_pulls, merged_low, parts = [], [], []
     for part, y_part in zip(states_back, branch_y):
         merged, merge_pull = jax.vjp(branch_merge, part.astype(F32), y_part)
@@ -831,16 +861,14 @@
 
     out_parts, upper_kept = dense_forward(third_rows, upper_gain, upper_unit, upper_down)
 
-    residual_grad, grad_upper_gain, upper_unit_grad, upper_drop_grad, _ = dense_backward(
+    residual_grad, grad_upper_gain, upper_products, _ = dense_backward(
         out_grad, upper_kept, upper_unit, upper_down, out_grad_chunks
     )
-    upper_unit_grad = reduce_z(upper_unit_grad)
-    upper_drop_grad = reduce_z(upper_drop_grad)
-
-    recur_grad_chunks, merged_grads, _ = chunked(
+    recur_grad_chunks, merged_grads, upper_grads = chunked(
         residual_grad.astype(BF16),
         lambda k, rows: times_transposed(rows, recur_out),
         lambda k, merged_grad: merge_pulls[k](merged_grad),
+        upper_products,
     )
     fourth_rows = third_rows + scatter_chunks(after(out_parts, merged_grads))
     out_tokens = (fourth_rows * valid).astype(BF16)[None]
@@ -869,7 +897,6 @@
         ],
         axis=0,
     )
-    channel_grads = butterfly(channel_grads, ("c", "y"))
     branch_x_grad = from_sequence(x_seq_grad.astype(BF16))
     branch_x_grad, out_tokens = tie(branch_x_grad, out_tokens)
     branch_grad = [
@@ -879,35 +906,39 @@
     normed_grad = scatter_chunks([times_transposed(part, recur_in) for part in branch_grad])
     recur_input_grad, grad_recur_gain = recur_pull(normed_grad)
     residual_grad = residual_grad + recur_input_grad
-    residual_grad, upper_unit_grad, upper_drop_grad, channel_grads = tie(
-        residual_grad, upper_unit_grad, upper_drop_grad, channel_grads
-    )
-    branch_grad, recur_grad_chunks = after((branch_grad, recur_grad_chunks), residual_grad)
-    recur_in_grad = chunk_product(recur_chunks, branch_grad, half_pieces(2 * channels), True)
-    recur_out_grad = chunk_product(merged_low, recur_grad_chunks, row_pieces(features), False)
-    channel_grads = lax.all_gather(channel_grads, X + ("z",), axis=0)
-
-    residual_grad, grad_lower_gain, lower_unit_grad, lower_drop_grad, recur_grads = dense_backward(
-        residual_grad, lower_kept, lower_unit, lower_down, None, (recur_in_grad, recur_out_grad)
+    residual_grad, upper_grads = tie(residual_grad, upper_grads)
+    upper_unit_grad, upper_drop_grad = (reduce_z(grad) for grad in upper_grads)
+
+    def recur_products(done):
+        branch, grads = after((branch_grad, recur_grad_chunks), done)
+        return (
+            chunk_product(recur_chunks, branch, half_pieces(2 * channels), True),
+            chunk_product(merged_low, grads, row_pieces(features), False),
+        )
+
+    residual_grad, grad_lower_gain, lower_products, recur_grads = dense_backward(
+        residual_grad, lower_kept, lower_unit, lower_down, None, recur_products
+    )
+    residual_grad, recur_grads, upper_drop_grad = tie(
+        residual_grad, recur_grads, upper_drop_grad
     )
     recur_in_grad, recur_out_grad = (reduce_z(grad) for grad in recur_grads)
-    residual_grad, channel_grads = tie(residual_grad, channel_grads)
-    grad_chunks = gather_rows(residual_grad.astype(BF16))
-    grad_chunks, lower_unit_grad, lower_drop_grad = tie(
-        grad_chunks, lower_unit_grad, lower_drop_grad
-    )
-    grad_rows = jnp.concatenate(grad_chunks, axis=0)
-    lower_unit_grad = reduce_z(lower_unit_grad)
-    lower_drop_grad = reduce_z(lower_drop_grad)
-    attend_grad = times_transposed(grad_rows, attend_out).astype(BF16)
+    grad_chunks, attend_grad, lower_grads = chunked(
+        residual_grad.astype(BF16),
+        lambda k, rows: times_transposed(rows, attend_out).astype(BF16),
+        lambda k, grad: grad,
+        lambda done: lower_products((done, upper_unit_grad)),
+    )
+    attend_grad = jnp.stack(attend_grad)
     query_grad, kv_grad = attend_backward(
-        positions, queries, kv, attend_grad.reshape(queries.shape), log_total
+        positions, queries, kv, attend_grad, log_total
     )
     kv_grad = lax.all_to_all(kv_grad, X + ("z",), 0, 0)
-    packed, upper_plan = pack([upper_unit_grad, recur_in_grad], [upper_drop_grad, recur_out_grad])
-    kv_grad, query_grad, packed = tie(kv_grad, query_grad, packed)
-    packed = lax.psum_scatter(packed, "y", scatter_dimension=0, tiled=True)
-    upper_packed = to_owners(packed, upper_plan)
+    out_grad = chunk_product(
+        [attended[k] for k in range(XN)], grad_chunks, row_pieces(features), False
+    )
+    kv_grad, query_grad, out_grad, lower_grads = tie(kv_grad, query_grad, out_grad, lower_grads)
+    lower_unit_grad, lower_drop_grad = (reduce_z(grad) for grad in lower_grads)
     kv_grad = jnp.sum(kv_grad.astype(F32), axis=0).astype(BF16)
     nothing = jnp.zeros_like(kv_grad[0])
     kv_grad = jnp.stack(
@@ -919,26 +950,36 @@
         ]
     )
     mixed_grad = jnp.concatenate([query_grad, kv_grad], axis=2).reshape(XN * row_count, -1)
-    normed_grad = scatter_chunks(
-        [
-            times_transposed(mixed_grad[k * row_count : (k + 1) * row_count], attend_in)
-            for k in range(XN)
-        ]
-    )
     mixed_chunks = [mixed_grad[k * row_count : (k + 1) * row_count] for k in range(XN)]
     attend_chunks = [attend_rows[k * row_count : (k + 1) * row_count] for k in range(XN)]
-    in_grad = reduce_z_direct(
-        chunk_product(attend_chunks, mixed_chunks, row_pieces(mixed_grad.shape[1]), True)
-    )
-    out_grad = reduce_z_direct(
-        chunk_product([attended[k] for k in range(XN)], grad_chunks, row_pieces(features), False)
-    )
+    in_grad = chunk_product(attend_chunks, mixed_chunks, row_pieces(mixed_grad.shape[1]), True)
+    lanes = in_grad.shape[1]
+    out_rows = out_grad.reshape(4, -1, features // 2)
+    both = [in_grad.reshape(4, -1, lanes)]
+    both += [out_rows[:, :, at : at + lanes] for at in range(0, features // 2, lanes)]
+    both = reduce_direct(jnp.concatenate(both, axis=1).reshape(-1, lanes), "z")
+    normed_grad = scatter_chunks(
+        [times_transposed(part, attend_in) for part in after(mixed_chunks, in_grad)]
+    )
+    channel_grads = butterfly(after(channel_grads, kv_grad), ("c", "y"))
+    both, normed_grad, channel_grads = tie(both, normed_grad, channel_grads)
+    recur_in_grad, recur_out_grad = after((recur_in_grad, recur_out_grad), both)
+    packed, upper_plan = pack([upper_unit_grad, recur_in_grad], [upper_drop_grad, recur_out_grad])
+    channel_grads = lax.all_to_all(
+        jnp.broadcast_to(channel_grads, (16,) + channel_grads.shape), X + ("z",), 0, 0
+    )
+    packed, channel_grads = tie(reduce_direct(packed, "y"), channel_grads)
+    upper_packed = spread(to_owners(packed, upper_plan))
+    in_grad, out_grad = both[: features // 4], both[features // 4 :].reshape(-1, features // 16, lanes)
+    out_grad = jnp.concatenate([out_grad[k] for k in range(out_grad.shape[0])], axis=1)
     packed, lower_plan = pack([lower_unit_grad, in_grad], [lower_drop_grad, out_grad])
-    packed = lax.psum_scatter(packed, "y", scatter_dimension=0, tiled=True)
-    packed, normed_grad, upper_packed = tie(packed, normed_grad, upper_packed)
-    upper_packed = spread(upper_packed)
+    packed, upper_packed = tie(reduce_direct(packed, "y"), upper_packed)
     lower_packed = spread(to_owners(packed, lower_plan))
     attend_input_grad, grad_attend_gain = attend_pull(normed_grad)
+    gains = butterfly(
+        jnp.stack([grad_attend_gain, grad_lower_gain, grad_recur_gain, grad_upper_gain]),
+        ("c", "xl", "xh", "z", "y"),
+    )
     residual_grad = residual_grad + attend_input_grad
     grad_decay_gate = channel_grads[:, :width]
     grad_input_gate = channel_grads[:, width : 2 * width]
@@ -948,10 +989,6 @@
         .reshape(tap_count, -1)
     )
     grad_decay_rate = channel_grads[:, 2 * width + tap_count].reshape(-1)
-    gains = butterfly(
-        jnp.stack([grad_attend_gain, grad_lower_gain, grad_recur_gain, grad_upper_gain]),
-        ("c", "xl", "xh", "z", "y"),
-    )
     upper_grads = unpack(
         upper_packed,
         upper_plan,

time: 905 us -> 874 us (0.966)
  waiting for transfers between devices: 375 us -> 304 us
  local copies, waits for them, and re-layouts: 59.6 us -> 82.5 us
  starting transfers between devices: 165 us -> 184 us
  matrix products: 120 us -> 107 us
    ppermute x22, waiting for transfers between devices: 41.8 us -> 84.8 us  [flip(): lax.ppermute(value, axis, [(i, i ^ by) for i in range(lax.axis_size(axis))])]
    ppermute x24, waiting for transfers between devices: 98.4 us -> 57.1 us  [from_x(): return lax.ppermute(value, X, [((i + by) % XN, i) for i in range(XN)])]
    reduce_scatter x2 -> x0, waiting for transfers between devices: 33.2 us -> none  [body(): packed = lax.psum_scatter(packed, 'y', scatter_dimension=0, tiled=True)]
    reduce_scatter x6, waiting for transfers between devices: 31.6 us -> 0.08 us  [reduce_z(): return lax.psum_scatter(grad, 'z', scatter_dimension=0, tiled=True)]
    ppermute x24 -> x27, waiting for transfers between devices: 71.3 us -> 102 us  [to_x(): return lax.ppermute(value, X, [(i, (i + by) % XN) for i in range(XN)])]
    unnamed x429 -> x531, local copies, waits for them, and re-layouts: 23.9 us -> 47.3 us
    all_gather x2, waiting for transfers between devices: 28.5 us -> 9.08 us  [spread(): return lax.all_gather(part, ('y', 'c'), axis=0, tiled=True)]
    ppermute x15 -> x16, starting transfers between devices: 29.1 us -> 46 us  [swap(): return lax.ppermute(value, 'c', [(0, 1), (1, 0)])]
  transfers between devices with their start and end apart: 111 -> 113, of which waited for: 53 -> 54; matrix products, arithmetic and copies ran while one was open for 25% -> 24% of each run, Pallas kernels for 7% -> 7%
where the time goes in v3:
time: 874 us; the launch traced here: 857 us
  waiting for transfers between devices  304 us (35%)
  starting transfers between devices  184 us (21%)
  matrix products  107 us (12%)
  other arithmetic  91.8 us (11%)
  local copies, waits for them, and re-layouts  82.5 us (9%)
  Pallas kernels  69.6 us (8%)
  between operations  19 us (2%)
    ppermute x27, waiting for transfers between devices, to_x(): return lax.ppermute(value, X, [(i, (i + by) % XN) for i in range(XN)])  102 us
    ppermute x22, waiting for transfers between devices, flip(): lax.ppermute(value, axis, [(i, i ^ by) for i in range(lax.axis_size(axis))])  84.8 us
    dot_general x34, matrix products, times_transposed(): lax.dot_general(left, right, (((1,), (1,)), ((), ())), preferred_element_...  64.9 us
    ppermute x24, waiting for transfers between devices, from_x(): return lax.ppermute(value, X, [((i + by) % XN, i) for i in range(XN)])  57.1 us
    unnamed x531, local copies, waits for them, and re-layouts  47.3 us
    ppermute x16, starting transfers between devices, swap(): return lax.ppermute(value, 'c', [(0, 1), (1, 0)])  46 us
    dot_general x31, matrix products, matmul(): return jnp.dot(left, right, preferred_element_type=F32)  39.1 us
    ppermute x27, starting transfers between devices, to_x(): return lax.ppermute(value, X, [(i, (i + by) % XN) for i in range(XN)])  33.8 us
  transfers between devices with their start and end apart: 113, of which 54 were waited for; matrix products, arithmetic and copies ran while one was open for 24% of the time, Pallas kernels for 7%

profile of v3, /device:TPU:1, one launch (start us, length us, event | category | flops | bytes accessed | tf_op | source)
XLA Modules:
  0.0 857.1 jit_solution(4508452384282214020)
XLA Ops:
  33.2 11.0 %all-to-all-done = bf16[16,96,256]{2,1,0:T(8,128)(2,1)S(1)} async-done(((bf16[16,96,256]{2,1,0:T(8,128)(2,1)}), bf16[16,96,256]{2,1,0:T(8,128)(2,1)S(1)}, u32[]{:S(2)}, u32[]{:S(2)}) %all-to-all-start) | async-done | bytes 786464 | tf_op jit(solution)/shard_map/all_to_all | solution.py:774
  56.4 13.5 %collective-permute-done.2 = bf16[128,1536]{1,0:T(8,128)(2,1)S(1)} collective-permute-done((bf16[128,1536]{1,0:T(8,128)(2,1)S(1)}, bf16[128,1536]{1,0:T(8,128)(2,1)S(1)}, u32[]{:S(2)}, u32[]{:S(2)}) %collective-permute-start.2) | collective-permute-done | bytes 393248 | tf_op jit(solution)/shard_map/ppermute | solution.py:26
  96.0 12.7 %collective-permute-done.14 = bf16[1,96,1792]{2,1,0:T(8,128)(2,1)S(1)} collective-permute-done((bf16[1,96,1792]{2,1,0:T(8,128)(2,1)S(1)}, bf16[1,96,1792]{2,1,0:T(8,128)(2,1)S(1)}, u32[]{:S(2)}, u32[]{:S(2)}) %collective-permute-start.14) | collective-permute-done | bytes 344096 | tf_op jit(solution)/shard_map/ppermute | solution.py:30
  119.4 6.8 shard_map.390
  144.4 13.1 %collective-permute-start.17 = (bf16[4,4,96,1280]{3,2,1,0:T(8,128)(2,1)}, bf16[4,4,96,1280]{3,2,1,0:T(8,128)(2,1)}, u32[]{:S(2)}, u32[]{:S(2)}) collective-permute-start(bf16[4,4,96,1280]{3,2,1,0:T(8,128)(2,1)} %bitcast.452), channel_id=1, source_target_pairs={{0,16},{16,0},{1,17},{17,1},{2,18},{18,2},{3,19},{19,3},{4,20},{20... | collective-permute-start | bytes 11796488 | tf_op jit(solution)/shard_map/ppermute | solution.py:46
  205.6 10.1 %collective-permute-done.23 = bf16[128,1536]{1,0:T(8,128)(2,1)S(1)} collective-permute-done((bf16[128,1536]{1,0:T(8,128)(2,1)S(1)}, bf16[128,1536]{1,0:T(8,128)(2,1)S(1)}, u32[]{:S(2)}, u32[]{:S(2)}) %collective-permute-start.23) | collective-permute-done | bytes 393248 | tf_op jit(solution)/shard_map/ppermute | solution.py:30
  240.0 6.8 collective-permute-done.26.refs_2_
  258.3 9.7 %all-to-all-done.3 = bf16[4,4,128,128]{3,2,1,0:T(8,128)(2,1)S(1)} async-done(((bf16[4,4,128,128]{3,2,1,0:T(8,128)(2,1)}), bf16[4,4,128,128]{3,2,1,0:T(8,128)(2,1)S(1)}, u32[]{:S(2)}, u32[]{:S(2)}) %all-to-all-start.3) | async-done | bytes 524320 | tf_op jit(solution)/shard_map/all_to_all | solution.py:399
  298.3 11.7 %collective-permute-done.32 = bf16[128,1536]{1,0:T(8,128)(2,1)S(1)} collective-permute-done((bf16[128,1536]{1,0:T(8,128)(2,1)S(1)}, bf16[128,1536]{1,0:T(8,128)(2,1)S(1)}, u32[]{:S(2)}, u32[]{:S(2)}) %collective-permute-start.32) | collective-permute-done | bytes 393248 | tf_op jit(solution)/shard_map/ppermute | solution.py:30
  411.3 8.7 %collective-permute-start.51 = (bf16[1152,768]{1,0:T(8,128)(2,1)}, bf16[1152,768]{1,0:T(8,128)(2,1)}, u32[]{:S(2)}, u32[]{:S(2)}) collective-permute-start(bf16[1152,768]{1,0:T(8,128)(2,1)} %get-tuple-element.239), channel_id=1, source_target_pairs={{0,16},{16,0},{1,17},{17,1},{2,18},{18,2},{3,19},{19,3},{4,20},{20... | collective-permute-start | bytes 5308424 | tf_op jit(solution)/shard_map/ppermute | solution.py:46
  466.1 11.1 %collective-permute-done.48 = bf16[128,1536]{1,0:T(8,128)(2,1)S(1)} collective-permute-done((bf16[128,1536]{1,0:T(8,128)(2,1)S(1)}, bf16[128,1536]{1,0:T(8,128)(2,1)S(1)}, u32[]{:S(2)}, u32[]{:S(2)}) %collective-permute-start.48) | collective-permute-done | bytes 393248 | tf_op jit(solution)/shard_map/ppermute | solution.py:30
  518.5 7.6 collective-permute-start.59
  547.2 8.9 %collective-permute-done.56 = bf16[128,1536]{1,0:T(8,128)(2,1)S(1)} collective-permute-done((bf16[128,1536]{1,0:T(8,128)(2,1)}, bf16[128,1536]{1,0:T(8,128)(2,1)S(1)}, u32[]{:S(2)}, u32[]{:S(2)}) %collective-permute-start.56) | collective-permute-done | bytes 393248 | tf_op jit(solution)/shard_map/ppermute | solution.py:30
  602.6 9.0 %collective-permute-done.60.refs_6_ = bf16[128,1536]{1,0:T(8,128)(2,1)S(1)} collective-permute-done((bf16[128,1536]{1,0:T(8,128)(2,1)}, bf16[128,1536]{1,0:T(8,128)(2,1)S(1)}, u32[]{:S(2)}, u32[]{:S(2)}) %collective-permute-start.60) | collective-permute-done | bytes 393248 | tf_op jit(solution)/shard_map/ppermute | solution.py:26
  616.4 8.1 shard_map.400
  678.8 8.8 %collective-permute-done.71 = bf16[128,1536]{1,0:T(8,128)(2,1)S(1)} collective-permute-done((bf16[128,1536]{1,0:T(8,128)(2,1)S(1)}, bf16[128,1536]{1,0:T(8,128)(2,1)S(1)}, u32[]{:S(2)}, u32[]{:S(2)}) %collective-permute-start.71) | collective-permute-done | bytes 393248 | tf_op jit(solution)/shard_map/ppermute | solution.py:30
  689.2 8.8 %collective-permute-done.68 = bf16[672,256]{1,0:T(8,128)(2,1)S(1)} collective-permute-done((bf16[672,256]{1,0:T(8,128)(2,1)S(1)}, bf16[672,256]{1,0:T(8,128)(2,1)S(1)}, u32[]{:S(2)}, u32[]{:S(2)}) %collective-permute-start.68) | collective-permute-done | bytes 344096 | tf_op jit(solution)/shard_map/ppermute | solution.py:34
  714.8 10.9 %collective-permute-done.86 = bf16[2048,128]{1,0:T(8,128)(2,1)} collective-permute-done((bf16[2048,128]{1,0:T(8,128)(2,1)}, bf16[2048,128]{1,0:T(8,128)(2,1)}, u32[]{:S(2)}, u32[]{:S(2)}) %collective-permute-start.86) | collective-permute-done | bytes 524320 | tf_op jit(solution)/shard_map/ppermute | solution.py:34
  725.7 8.1 collective-permute-done.87
  745.1 6.7 all-to-all-done.9
  758.7 9.6 %collective-permute-done.83 = bf16[1728,128]{1,0:T(8,128)(2,1)S(1)} collective-permute-done((bf16[1728,128]{1,0:T(8,128)(2,1)S(1)}, bf16[1728,128]{1,0:T(8,128)(2,1)S(1)}, u32[]{:S(2)}, u32[]{:S(2)}) %collective-permute-start.83) | collective-permute-done | bytes 442400 | tf_op jit(solution)/shard_map/ppermute | solution.py:34
  768.4 14.8 %collective-permute-done.84 = bf16[1728,128]{1,0:T(8,128)(2,1)S(1)} collective-permute-done((bf16[1728,128]{1,0:T(8,128)(2,1)S(1)}, bf16[1728,128]{1,0:T(8,128)(2,1)S(1)}, u32[]{:S(2)}, u32[]{:S(2)}) %collective-permute-start.84) | collective-permute-done | bytes 442400 | tf_op jit(solution)/shard_map/ppermute | solution.py:34
  788.2 9.1 %all-gather.14.cloned.1.call-done.packed = bf16[16384,128]{1,0:T(8,128)(2,1)} async-done(((bf16[2048,128]{1,0:T(8,128)(2,1)}), bf16[16384,128]{1,0:T(8,128)(2,1)}) %all-gather.14.cloned.1.call-update) | async-done | bytes 4194320 | tf_op jit(solution)/shard_map/all_gather | solution.py:647
  801.7 6.8 all-to-all-done.10
  (1028 shorter events, 605.8 us)
Async XLA Ops:
  9.0 40.1 %collective-permute-start.4 = (bf16[1,96,768]{2,1,0:T(8,128)(2,1)}, bf16[1,96,768]{2,1,0:T(8,128)(2,1)}, u32[]{:S(2)}, u32[]{:S(2)}) collective-permute-start(bf16[1,96,768]{2,1,0:T(8,128)(2,1)} %fusion.146), channel_id=1, source_target_pairs={{0,1},{1,0},{2,3},{3,2},{4,5},{5,4},{6,7},{7,6},{8,9},{9,8},{10,11... | collective-permute-start | bytes 442376 | tf_op jit(solution)/shard_map/ppermute | solution.py:34
  11.4 42.2 %collective-permute-start.5 = (bf16[1,96,768]{2,1,0:T(8,128)(2,1)}, bf16[1,96,768]{2,1,0:T(8,128)(2,1)}, u32[]{:S(2)}, u32[]{:S(2)}) collective-permute-start(bf16[1,96,768]{2,1,0:T(8,128)(2,1)} %fusion.146), channel_id=1, source_target_pairs={{0,2},{1,3},{2,0},{3,1},{4,6},{5,7},{6,4},{7,5},{8,10},{9,11},{10,... | collective-permute-start | bytes 442376 | tf_op jit(solution)/shard_map/ppermute | solution.py:34
  14.7 41.6 %collective-permute-start.6 = (bf16[1,96,768]{2,1,0:T(8,128)(2,1)}, bf16[1,96,768]{2,1,0:T(8,128)(2,1)S(1)}, u32[]{:S(2)}, u32[]{:S(2)}) collective-permute-start(bf16[1,96,768]{2,1,0:T(8,128)(2,1)} %fusion.146), channel_id=1, source_target_pairs={{0,3},{1,2},{2,1},{3,0},{4,7},{5,6},{6,5},{7,4},{8,11},{9,10},{10,... | collective-permute-start | bytes 442376 | tf_op jit(solution)/shard_map/ppermute | solution.py:34
  17.1 39.3 %collective-permute-start = (bf16[128,1536]{1,0:T(8,128)(2,1)S(1)}, bf16[128,1536]{1,0:T(8,128)(2,1)}, u32[]{:S(2)}, u32[]{:S(2)}) collective-permute-start(bf16[128,1536]{1,0:T(8,128)(2,1)S(1)} %fusion.30), channel_id=1, source_target_pairs={{4,0},{8,4},{12,8},{0,12},{5,1},{9,5},{13,9},{1,13},{6,2},{10,6},{... | collective-permute-start | bytes 1179656 | tf_op jit(solution)/shard_map/ppermute | solution.py:26
  28.5 44.2 %all-gather.12.cloned.1.call-start = ((), (), s32[]{:S(2)}) async-start(), calls=%async_computation.17 | async-start | bytes 2211840 | tf_op jit(solution)/shard_map/all_gather | solution.py:777
  49.0 95.4 %all-gather.18.cloned.1.call-start = ((), (), s32[]{:S(2)}) async-start(), calls=%async_computation.26 | async-start | bytes 4915200 | tf_op jit(solution)/shard_map/all_gather | solution.py:783
  74.4 43.8 %collective-permute-start.10 = (bf16[384,768]{1,0:T(8,128)(2,1)}, bf16[384,768]{1,0:T(8,128)(2,1)}, u32[]{:S(2)}, u32[]{:S(2)}) collective-permute-start(bf16[384,768]{1,0:T(8,128)(2,1)} %bitcast.475), channel_id=1, source_target_pairs={{0,16},{16,0},{1,17},{17,1},{2,18},{18,2},{3,19},{19,3},{4,20},{20... | collective-permute-start | bytes 1769480 | tf_op jit(solution)/shard_map/ppermute | solution.py:46
  86.7 131.5 %all-gather.20.cloned.1.call-start = ((), (), s32[]{:S(2)}) async-start(), calls=%async_computation.27 | async-start | bytes 1966080 | tf_op jit(solution)/shard_map/all_gather | solution.py:820
  144.3 76.1 %all-gather.22.cloned.1.call-start = ((), (), s32[]{:S(2)}) async-start(), calls=%async_computation.28 | async-start | bytes 3194880 | tf_op jit(solution)/shard_map/all_gather | solution.py:822
  159.6 118.7 %all-gather.24.cloned.1.call-start = ((), (), s32[]{:S(2)}) async-start(), calls=%async_computation.29 | async-start | bytes 4915200 | tf_op jit(solution)/shard_map/all_gather | solution.py:823
  278.3 40.0 %collective-permute-start.34 = (bf16[4,4,96,1280]{3,2,1,0:T(8,128)(2,1)}, bf16[4,4,96,1280]{3,2,1,0:T(8,128)(2,1)}, u32[]{:S(2)}, u32[]{:S(2)}) collective-permute-start(bf16[4,4,96,1280]{3,2,1,0:T(8,128)(2,1)} %bitcast.454), channel_id=1, source_target_pairs={{0,16},{16,0},{1,17},{17,1},{2,18},{18,2},{3,19},{19,3},{4,20},{20... | collective-permute-start | bytes 11796488 | tf_op jit(solution)/shard_map/ppermute | solution.py:46
  411.3 68.6 %collective-permute-start.51 = (bf16[1152,768]{1,0:T(8,128)(2,1)}, bf16[1152,768]{1,0:T(8,128)(2,1)}, u32[]{:S(2)}, u32[]{:S(2)}) collective-permute-start(bf16[1152,768]{1,0:T(8,128)(2,1)} %get-tuple-element.239), channel_id=1, source_target_pairs={{0,16},{16,0},{1,17},{17,1},{2,18},{18,2},{3,19},{19,3},{4,20},{20... | collective-permute-start | bytes 5308424 | tf_op jit(solution)/shard_map/ppermute | solution.py:46
  426.3 57.3 %collective-permute-start.50 = (bf16[4,4,96,1280]{3,2,1,0:T(8,128)(2,1)}, bf16[4,4,96,1280]{3,2,1,0:T(8,128)(2,1)}, u32[]{:S(2)}, u32[]{:S(2)}) collective-permute-start(bf16[4,4,96,1280]{3,2,1,0:T(8,128)(2,1)} %get-tuple-element.233), channel_id=1, source_target_pairs={{0,16},{16,0},{1,17},{17,1},{2,18},{18,2},{3,19},{19,3},{4,20},{20... | collective-permute-start | bytes 11796488 | tf_op jit(solution)/shard_map/ppermute | solution.py:46
  444.9 117.0 %reduce-scatter.7.cloned.1.call-start = ((), (), s32[]{:S(2)}) async-start(), calls=%async_computation.18 | async-start | bytes 2211840 | tf_op jit(solution)/shard_map/reduce_scatter | solution.py:516
  490.0 84.4 %reduce-scatter.9.cloned.1.call-start = ((), (), s32[]{:S(2)}) async-start(), calls=%async_computation.19 | async-start | bytes 4915200 | tf_op jit(solution)/shard_map/reduce_scatter | solution.py:516
  490.8 216.2 %reduce-scatter.17.cloned.1.call-start = ((), (), s32[]{:S(2)}) async-start(), calls=%async_computation.23 | async-start | bytes 983040 | tf_op jit(solution)/shard_map/reduce_scatter | solution.py:516
  518.5 39.2 %collective-permute-start.59 = (bf16[512,768]{1,0:T(8,128)(2,1)S(1)}, bf16[512,768]{1,0:T(8,128)(2,1)S(1)}, u32[]{:S(2)}, u32[]{:S(2)}) collective-permute-start(bf16[512,768]{1,0:T(8,128)(2,1)S(1)} %get-tuple-element.257), channel_id=1, source_target_pairs={{0,16},{16,0},{1,17},{17,1},{2,18},{18,2},{3,19},{19,3},{4,20},{20... | collective-permute-start | bytes 2359304 | tf_op jit(solution)/shard_map/ppermute | solution.py:46
  585.1 50.8 %collective-permute-start.64 = (bf16[4,4,96,1280]{3,2,1,0:T(8,128)(2,1)}, bf16[4,4,96,1280]{3,2,1,0:T(8,128)(2,1)}, u32[]{:S(2)}, u32[]{:S(2)}) collective-permute-start(bf16[4,4,96,1280]{3,2,1,0:T(8,128)(2,1)} %get-tuple-element.276), channel_id=1, source_target_pairs={{0,16},{16,0},{1,17},{17,1},{2,18},{18,2},{3,19},{19,3},{4,20},{20... | collective-permute-start | bytes 11796488 | tf_op jit(solution)/shard_map/ppermute | solution.py:46
  586.9 120.1 %reduce-scatter.15.cloned.1.call-start = ((), (), s32[]{:S(2)}) async-start(), calls=%async_computation.22 | async-start | bytes 1966080 | tf_op jit(solution)/shard_map/reduce_scatter | solution.py:516
  630.7 122.0 %reduce-scatter.13.cloned.1.call-start = ((), (), s32[]{:S(2)}) async-start(), calls=%async_computation.21 | async-start | bytes 2211840 | tf_op jit(solution)/shard_map/reduce_scatter | solution.py:516
  646.6 106.2 %reduce-scatter.11.cloned.1.call-start = ((), (), s32[]{:S(2)}) async-start(), calls=%async_computation.20 | async-start | bytes 4915200 | tf_op jit(solution)/shard_map/reduce_scatter | solution.py:516
  702.1 38.0 %all-to-all-start.8 = ((f32[16,264,128]{2,1,0:T(8,128)}), f32[16,264,128]{2,1,0:T(8,128)}, u32[]{:S(2)}, u32[]{:S(2)}) async-start(f32[16,264,128]{2,1,0:T(8,128)} %broadcast_in_dim.114), calls=%async_computation.14 | async-start | bytes 4325376 | tf_op jit(solution)/shard_map/all_to_all | solution.py:968
  745.1 52.2 %all-gather.14.cloned.1.call-start = ((), (), s32[]{:S(2)}) async-start(), calls=%async_computation.24 | async-start | bytes 4718592 | tf_op jit(solution)/shard_map/all_gather | solution.py:647
  801.6 43.6 %all-gather.16.cloned.1.call-start = ((), (), s32[]{:S(2)}) async-start(), calls=%async_computation.25 | async-start | bytes 3981312 | tf_op jit(solution)/shard_map/all_gather | solution.py:647
  (354 other events, 3705.0 us)
Sparse Core Ops, SparseCore 0:
  31.5 31.7 all-gather.11
  73.7 59.3 all-gather.17
  144.5 39.1 all-gather.19
  185.7 34.7 all-gather.21
  223.7 51.2 all-gather.23
  490.1 25.3 reduce-scatter.6
  518.0 44.4 reduce-scatter.8
  587.0 18.9 reduce-scatter.16
  609.1 25.7 reduce-scatter.14
  646.6 27.5 reduce-scatter.12
  676.6 73.9 reduce-scatter.10
  752.8 44.4 all-gather.13
  809.4 27.2 all-gather.15

commit v4 on v3

--- a/solution.py
+++ b/solution.py
@@ -777,8 +777,8 @@
     lower_rows = lax.all_gather(own_half(lower_drop), "z", axis=0, tiled=True)
 
     attend_rows = jnp.concatenate(gather_rows(normed_attend.astype(BF16)), axis=0)
-    attend_rows, attend_in, lower_columns, lower_rows, half_out = tie(
-        attend_rows, attend_in, lower_columns, lower_rows, half_out
+    attend_rows, attend_in, lower_columns, lower_rows = tie(
+        attend_rows, attend_in, lower_columns, lower_rows
     )
     lower_columns = lax.all_gather(lower_columns, "z", axis=0)
     recur_input, recur_branch, upper_gate, upper_lift = after(
@@ -796,7 +796,6 @@
         )
     )
     mixed_in = matmul(attend_rows, attend_in).astype(BF16).reshape(XN, row_count, -1)
-    attend_out = row_join(half_out.reshape(query_width, -1))
     queries = mixed_in[:, :, :query_width]
     kv_part = mixed_in[:, :, query_width:]
     kv_send = jnp.stack(
@@ -807,6 +806,8 @@
     )
     out_grad = cotangent[0].astype(F32) * valid
     out_grad_chunks = gather_rows(after(out_grad.astype(BF16), kv))
+    kv, half_out = tie(kv, half_out)
+    attend_out = row_join(half_out.reshape(query_width, -1))
     attended, log_total = attend_forward(positions, queries, kv)
     attended, out_grad_chunks = tie(attended, out_grad_chunks)
     attend_back = attended.reshape(XN * row_count, query_width)

time: 874 us -> 864 us (0.989)
  starting transfers between devices: 184 us -> 171 us
    all_to_all x1, waiting for transfers between devices: 0.01 us -> 8.83 us  [body(): lax.all_to_all(jnp.broadcast_to(kv_send[None], (16,) + kv_send.shape), X...]
    unnamed x531 -> x529, local copies, waits for them, and re-layouts: 47.3 us -> 47.7 us
  transfers between devices with their start and end apart: 113 -> 113, of which waited for: 54 -> 55; matrix products, arithmetic and copies ran while one was open for 24% -> 25% of each run, Pallas kernels for 7% -> 7%
where the time goes in v4:
time: 864 us; the launch traced here: 848 us
  waiting for transfers between devices  300 us (35%)
  starting transfers between devices  171 us (20%)
  matrix products  107 us (12%)
  other arithmetic  93.4 us (11%)
  local copies, waits for them, and re-layouts  86.9 us (10%)
  Pallas kernels  69.6 us (8%)
  between operations  19.1 us (2%)
    ppermute x27, waiting for transfers between devices, to_x(): return lax.ppermute(value, X, [(i, (i + by) % XN) for i in range(XN)])  97.1 us
    ppermute x22, waiting for transfers between devices, flip(): lax.ppermute(value, axis, [(i, i ^ by) for i in range(lax.axis_size(axis))])  84.9 us
    dot_general x34, matrix products, times_transposed(): lax.dot_general(left, right, (((1,), (1,)), ((), ())), preferred_element_...  64.9 us
    ppermute x24, waiting for transfers between devices, from_x(): return lax.ppermute(value, X, [((i + by) % XN, i) for i in range(XN)])  54.8 us
    unnamed x529, local copies, waits for them, and re-layouts  47.7 us
    ppermute x16, starting transfers between devices, swap(): return lax.ppermute(value, 'c', [(0, 1), (1, 0)])  41.3 us
    dot_general x31, matrix products, matmul(): return jnp.dot(left, right, preferred_element_type=F32)  39.3 us
    pallas_call x8, Pallas kernels, chunk_product(): pl.pallas_call(functools.partial(product_kernel, count, pieces, split), g...  30.8 us
  transfers between devices with their start and end apart: 113, of which 55 were waited for; matrix products, arithmetic and copies ran while one was open for 25% of the time, Pallas kernels for 7%

profile of v4, /device:TPU:1, one launch (start us, length us, event | category | flops | bytes accessed | tf_op | source)
XLA Modules:
  0.0 847.8 jit_solution(14760694951898639026)
XLA Ops:
  10.3 8.6 %all-to-all-start = ((bf16[16,96,256]{2,1,0:T(8,128)(2,1)}), bf16[16,96,256]{2,1,0:T(8,128)(2,1)S(1)}, u32[]{:S(2)}, u32[]{:S(2)}) async-start(bf16[16,96,256]{2,1,0:T(8,128)(2,1)} %bitcast.6), calls=%async_computation | async-start | bytes 1572864 | tf_op jit(solution)/shard_map/all_to_all | solution.py:774
  31.5 11.1 %collective-permute-start.3 = (bf16[1536,256]{1,0:T(8,128)(2,1)S(1)}, bf16[1536,256]{1,0:T(8,128)(2,1)}, u32[]{:S(2)}, u32[]{:S(2)}) collective-permute-start(bf16[1536,256]{1,0:T(8,128)(2,1)S(1)} %bitcast.471), channel_id=1, source_target_pairs={{0,16},{16,0},{1,17},{17,1},{2,18},{18,2},{3,19},{19,3},{4,20},{20... | collective-permute-start | bytes 2359304 | tf_op jit(solution)/shard_map/ppermute | solution.py:46
  84.3 8.8 %all-to-all-done.2.kv_ref = bf16[16,2,128,128]{3,2,1,0:T(8,128)(2,1)S(1)} async-done(((bf16[16,2,128,128]{3,2,1,0:T(8,128)(2,1)}), bf16[16,2,128,128]{3,2,1,0:T(8,128)(2,1)S(1)}, u32[]{:S(2)}, u32[]{:S(2)}) %all-to-all-start.2) | async-done | bytes 1048608 | tf_op jit(solution)/shard_map/all_to_all | solution.py:804
  107.7 6.8 shard_map.390
  115.0 9.6 %collective-permute-done.9.refs_7_ = bf16[128,1536]{1,0:T(8,128)(2,1)S(1)} collective-permute-done((bf16[128,1536]{1,0:T(8,128)(2,1)S(1)}, bf16[128,1536]{1,0:T(8,128)(2,1)S(1)}, u32[]{:S(2)}, u32[]{:S(2)}) %collective-permute-start.9) | collective-permute-done | bytes 393248 | tf_op jit(solution)/shard_map/ppermute | solution.py:26
  129.6 7.9 collective-permute-done.11
  137.5 9.1 %collective-permute-done.12 = bf16[128,1536]{1,0:T(8,128)(2,1)S(1)} collective-permute-done((bf16[128,1536]{1,0:T(8,128)(2,1)S(1)}, bf16[128,1536]{1,0:T(8,128)(2,1)S(1)}, u32[]{:S(2)}, u32[]{:S(2)}) %collective-permute-start.12) | collective-permute-done | bytes 393248 | tf_op jit(solution)/shard_map/ppermute | solution.py:30
  189.9 7.8 collective-permute-done.22
  197.7 9.7 %collective-permute-done.23 = bf16[128,1536]{1,0:T(8,128)(2,1)S(1)} collective-permute-done((bf16[128,1536]{1,0:T(8,128)(2,1)S(1)}, bf16[128,1536]{1,0:T(8,128)(2,1)S(1)}, u32[]{:S(2)}, u32[]{:S(2)}) %collective-permute-start.23) | collective-permute-done | bytes 393248 | tf_op jit(solution)/shard_map/ppermute | solution.py:30
  249.3 9.5 %all-to-all-done.3 = bf16[4,4,128,128]{3,2,1,0:T(8,128)(2,1)S(1)} async-done(((bf16[4,4,128,128]{3,2,1,0:T(8,128)(2,1)}), bf16[4,4,128,128]{3,2,1,0:T(8,128)(2,1)S(1)}, u32[]{:S(2)}, u32[]{:S(2)}) %all-to-all-start.3) | async-done | bytes 524320 | tf_op jit(solution)/shard_map/all_to_all | solution.py:399
  289.0 11.8 %collective-permute-done.32 = bf16[128,1536]{1,0:T(8,128)(2,1)S(1)} collective-permute-done((bf16[128,1536]{1,0:T(8,128)(2,1)S(1)}, bf16[128,1536]{1,0:T(8,128)(2,1)S(1)}, u32[]{:S(2)}, u32[]{:S(2)}) %collective-permute-start.32) | collective-permute-done | bytes 393248 | tf_op jit(solution)/shard_map/ppermute | solution.py:30
  401.9 8.6 %collective-permute-start.51 = (bf16[1152,768]{1,0:T(8,128)(2,1)}, bf16[1152,768]{1,0:T(8,128)(2,1)}, u32[]{:S(2)}, u32[]{:S(2)}) collective-permute-start(bf16[1152,768]{1,0:T(8,128)(2,1)} %get-tuple-element.241), channel_id=1, source_target_pairs={{0,16},{16,0},{1,17},{17,1},{2,18},{18,2},{3,19},{19,3},{4,20},{20... | collective-permute-start | bytes 5308424 | tf_op jit(solution)/shard_map/ppermute | solution.py:46
  456.6 11.1 %collective-permute-done.48 = bf16[128,1536]{1,0:T(8,128)(2,1)S(1)} collective-permute-done((bf16[128,1536]{1,0:T(8,128)(2,1)S(1)}, bf16[128,1536]{1,0:T(8,128)(2,1)S(1)}, u32[]{:S(2)}, u32[]{:S(2)}) %collective-permute-start.48) | collective-permute-done | bytes 393248 | tf_op jit(solution)/shard_map/ppermute | solution.py:30
  509.0 7.5 collective-permute-start.59
  537.4 9.0 %collective-permute-done.56 = bf16[128,1536]{1,0:T(8,128)(2,1)S(1)} collective-permute-done((bf16[128,1536]{1,0:T(8,128)(2,1)}, bf16[128,1536]{1,0:T(8,128)(2,1)S(1)}, u32[]{:S(2)}, u32[]{:S(2)}) %collective-permute-start.56) | collective-permute-done | bytes 393248 | tf_op jit(solution)/shard_map/ppermute | solution.py:30
  592.8 9.1 %collective-permute-done.60.refs_6_ = bf16[128,1536]{1,0:T(8,128)(2,1)S(1)} collective-permute-done((bf16[128,1536]{1,0:T(8,128)(2,1)}, bf16[128,1536]{1,0:T(8,128)(2,1)S(1)}, u32[]{:S(2)}, u32[]{:S(2)}) %collective-permute-start.60) | collective-permute-done | bytes 393248 | tf_op jit(solution)/shard_map/ppermute | solution.py:26
  606.8 8.1 shard_map.400
  669.2 8.8 %collective-permute-done.71 = bf16[128,1536]{1,0:T(8,128)(2,1)S(1)} collective-permute-done((bf16[128,1536]{1,0:T(8,128)(2,1)S(1)}, bf16[128,1536]{1,0:T(8,128)(2,1)S(1)}, u32[]{:S(2)}, u32[]{:S(2)}) %collective-permute-start.71) | collective-permute-done | bytes 393248 | tf_op jit(solution)/shard_map/ppermute | solution.py:30
  679.5 8.8 %collective-permute-done.68 = bf16[672,256]{1,0:T(8,128)(2,1)S(1)} collective-permute-done((bf16[672,256]{1,0:T(8,128)(2,1)S(1)}, bf16[672,256]{1,0:T(8,128)(2,1)S(1)}, u32[]{:S(2)}, u32[]{:S(2)}) %collective-permute-start.68) | collective-permute-done | bytes 344096 | tf_op jit(solution)/shard_map/ppermute | solution.py:34
  705.3 11.0 %collective-permute-done.86 = bf16[2048,128]{1,0:T(8,128)(2,1)} collective-permute-done((bf16[2048,128]{1,0:T(8,128)(2,1)}, bf16[2048,128]{1,0:T(8,128)(2,1)}, u32[]{:S(2)}, u32[]{:S(2)}) %collective-permute-start.86) | collective-permute-done | bytes 524320 | tf_op jit(solution)/shard_map/ppermute | solution.py:34
  716.2 8.3 collective-permute-done.87
  749.2 9.6 %collective-permute-done.83 = bf16[1728,128]{1,0:T(8,128)(2,1)S(1)} collective-permute-done((bf16[1728,128]{1,0:T(8,128)(2,1)S(1)}, bf16[1728,128]{1,0:T(8,128)(2,1)S(1)}, u32[]{:S(2)}, u32[]{:S(2)}) %collective-permute-start.83) | collective-permute-done | bytes 442400 | tf_op jit(solution)/shard_map/ppermute | solution.py:34
  758.8 14.8 %collective-permute-done.84 = bf16[1728,128]{1,0:T(8,128)(2,1)S(1)} collective-permute-done((bf16[1728,128]{1,0:T(8,128)(2,1)S(1)}, bf16[1728,128]{1,0:T(8,128)(2,1)S(1)}, u32[]{:S(2)}, u32[]{:S(2)}) %collective-permute-start.84) | collective-permute-done | bytes 442400 | tf_op jit(solution)/shard_map/ppermute | solution.py:34
  778.7 9.1 %all-gather.14.cloned.1.call-done.packed = bf16[16384,128]{1,0:T(8,128)(2,1)} async-done(((bf16[2048,128]{1,0:T(8,128)(2,1)}), bf16[16384,128]{1,0:T(8,128)(2,1)}) %all-gather.14.cloned.1.call-update) | async-done | bytes 4194320 | tf_op jit(solution)/shard_map/all_gather | solution.py:647
  (1026 shorter events, 604.2 us)
Async XLA Ops:
  18.9 43.9 %all-gather.12.cloned.1.call-start = ((), (), s32[]{:S(2)}) async-start(), calls=%async_computation.17 | async-start | bytes 2211840 | tf_op jit(solution)/shard_map/all_gather | solution.py:777
  48.3 100.8 %all-gather.18.cloned.1.call-start = ((), (), s32[]{:S(2)}) async-start(), calls=%async_computation.26 | async-start | bytes 4915200 | tf_op jit(solution)/shard_map/all_gather | solution.py:783
  77.6 132.3 %all-gather.20.cloned.1.call-start = ((), (), s32[]{:S(2)}) async-start(), calls=%async_computation.27 | async-start | bytes 1966080 | tf_op jit(solution)/shard_map/all_gather | solution.py:821
  93.1 31.5 %collective-permute-start.10 = (bf16[384,768]{1,0:T(8,128)(2,1)}, bf16[384,768]{1,0:T(8,128)(2,1)S(1)}, u32[]{:S(2)}, u32[]{:S(2)}) collective-permute-start(bf16[384,768]{1,0:T(8,128)(2,1)} %bitcast.475), channel_id=1, source_target_pairs={{0,16},{16,0},{1,17},{17,1},{2,18},{18,2},{3,19},{19,3},{4,20},{20... | collective-permute-start | bytes 1769480 | tf_op jit(solution)/shard_map/ppermute | solution.py:46
  149.0 62.6 %all-gather.22.cloned.1.call-start = ((), (), s32[]{:S(2)}) async-start(), calls=%async_computation.28 | async-start | bytes 3194880 | tf_op jit(solution)/shard_map/all_gather | solution.py:823
  152.9 116.2 %all-gather.24.cloned.1.call-start = ((), (), s32[]{:S(2)}) async-start(), calls=%async_computation.29 | async-start | bytes 4915200 | tf_op jit(solution)/shard_map/all_gather | solution.py:824
  269.1 39.7 %collective-permute-start.34 = (bf16[4,4,96,1280]{3,2,1,0:T(8,128)(2,1)}, bf16[4,4,96,1280]{3,2,1,0:T(8,128)(2,1)}, u32[]{:S(2)}, u32[]{:S(2)}) collective-permute-start(bf16[4,4,96,1280]{3,2,1,0:T(8,128)(2,1)} %bitcast.454), channel_id=1, source_target_pairs={{0,16},{16,0},{1,17},{17,1},{2,18},{18,2},{3,19},{19,3},{4,20},{20... | collective-permute-start | bytes 11796488 | tf_op jit(solution)/shard_map/ppermute | solution.py:46
  274.9 29.8 %collective-permute-start.29 = (bf16[1152,768]{1,0:T(8,128)(2,1)}, bf16[1152,768]{1,0:T(8,128)(2,1)}, u32[]{:S(2)}, u32[]{:S(2)}) collective-permute-start(bf16[1152,768]{1,0:T(8,128)(2,1)} %bitcast.80), channel_id=1, source_target_pairs={{0,16},{16,0},{1,17},{17,1},{2,18},{18,2},{3,19},{19,3},{4,20},{20... | collective-permute-start | bytes 5308424 | tf_op jit(solution)/shard_map/ppermute | solution.py:46
  385.0 34.6 %all-to-all-start.5 = ((bf16[4,4,128,128]{3,2,1,0:T(8,128)(2,1)}), bf16[4,4,128,128]{3,2,1,0:T(8,128)(2,1)}, u32[]{:S(2)}, u32[]{:S(2)}) async-start(bf16[4,4,128,128]{3,2,1,0:T(8,128)(2,1)} %pad_maximum_fusion.16), calls=%async_computation.5 | async-start | bytes 1048576 | tf_op jit(solution)/shard_map/all_to_all | solution.py:399
  401.9 68.5 %collective-permute-start.51 = (bf16[1152,768]{1,0:T(8,128)(2,1)}, bf16[1152,768]{1,0:T(8,128)(2,1)}, u32[]{:S(2)}, u32[]{:S(2)}) collective-permute-start(bf16[1152,768]{1,0:T(8,128)(2,1)} %get-tuple-element.241), channel_id=1, source_target_pairs={{0,16},{16,0},{1,17},{17,1},{2,18},{18,2},{3,19},{19,3},{4,20},{20... | collective-permute-start | bytes 5308424 | tf_op jit(solution)/shard_map/ppermute | solution.py:46
  416.9 57.3 %collective-permute-start.50 = (bf16[4,4,96,1280]{3,2,1,0:T(8,128)(2,1)}, bf16[4,4,96,1280]{3,2,1,0:T(8,128)(2,1)}, u32[]{:S(2)}, u32[]{:S(2)}) collective-permute-start(bf16[4,4,96,1280]{3,2,1,0:T(8,128)(2,1)} %get-tuple-element.235), channel_id=1, source_target_pairs={{0,16},{16,0},{1,17},{17,1},{2,18},{18,2},{3,19},{19,3},{4,20},{20... | collective-permute-start | bytes 11796488 | tf_op jit(solution)/shard_map/ppermute | solution.py:46
  435.4 116.8 %reduce-scatter.7.cloned.1.call-start = ((), (), s32[]{:S(2)}) async-start(), calls=%async_computation.18 | async-start | bytes 2211840 | tf_op jit(solution)/shard_map/reduce_scatter | solution.py:516
  480.5 84.2 %reduce-scatter.9.cloned.1.call-start = ((), (), s32[]{:S(2)}) async-start(), calls=%async_computation.19 | async-start | bytes 4915200 | tf_op jit(solution)/shard_map/reduce_scatter | solution.py:516
  481.4 216.0 %reduce-scatter.17.cloned.1.call-start = ((), (), s32[]{:S(2)}) async-start(), calls=%async_computation.23 | async-start | bytes 983040 | tf_op jit(solution)/shard_map/reduce_scatter | solution.py:516
  509.0 39.0 %collective-permute-start.59 = (bf16[512,768]{1,0:T(8,128)(2,1)S(1)}, bf16[512,768]{1,0:T(8,128)(2,1)S(1)}, u32[]{:S(2)}, u32[]{:S(2)}) collective-permute-start(bf16[512,768]{1,0:T(8,128)(2,1)S(1)} %get-tuple-element.259), channel_id=1, source_target_pairs={{0,16},{16,0},{1,17},{17,1},{2,18},{18,2},{3,19},{19,3},{4,20},{20... | collective-permute-start | bytes 2359304 | tf_op jit(solution)/shard_map/ppermute | solution.py:46
  575.4 51.0 %collective-permute-start.64 = (bf16[4,4,96,1280]{3,2,1,0:T(8,128)(2,1)}, bf16[4,4,96,1280]{3,2,1,0:T(8,128)(2,1)}, u32[]{:S(2)}, u32[]{:S(2)}) collective-permute-start(bf16[4,4,96,1280]{3,2,1,0:T(8,128)(2,1)} %get-tuple-element.278), channel_id=1, source_target_pairs={{0,16},{16,0},{1,17},{17,1},{2,18},{18,2},{3,19},{19,3},{4,20},{20... | collective-permute-start | bytes 11796488 | tf_op jit(solution)/shard_map/ppermute | solution.py:46
  577.2 120.2 %reduce-scatter.15.cloned.1.call-start = ((), (), s32[]{:S(2)}) async-start(), calls=%async_computation.22 | async-start | bytes 1966080 | tf_op jit(solution)/shard_map/reduce_scatter | solution.py:516
  588.6 34.6 %collective-permute-start.65 = (bf16[1152,768]{1,0:T(8,128)(2,1)}, bf16[1152,768]{1,0:T(8,128)(2,1)}, u32[]{:S(2)}, u32[]{:S(2)}) collective-permute-start(bf16[1152,768]{1,0:T(8,128)(2,1)} %get-tuple-element.284), channel_id=1, source_target_pairs={{0,16},{16,0},{1,17},{17,1},{2,18},{18,2},{3,19},{19,3},{4,20},{20... | collective-permute-start | bytes 5308424 | tf_op jit(solution)/shard_map/ppermute | solution.py:46
  621.1 122.0 %reduce-scatter.13.cloned.1.call-start = ((), (), s32[]{:S(2)}) async-start(), calls=%async_computation.21 | async-start | bytes 2211840 | tf_op jit(solution)/shard_map/reduce_scatter | solution.py:516
  637.0 106.2 %reduce-scatter.11.cloned.1.call-start = ((), (), s32[]{:S(2)}) async-start(), calls=%async_computation.20 | async-start | bytes 4915200 | tf_op jit(solution)/shard_map/reduce_scatter | solution.py:516
  692.5 38.0 %all-to-all-start.8 = ((f32[16,264,128]{2,1,0:T(8,128)}), f32[16,264,128]{2,1,0:T(8,128)}, u32[]{:S(2)}, u32[]{:S(2)}) async-start(f32[16,264,128]{2,1,0:T(8,128)} %broadcast_in_dim.114), calls=%async_computation.14 | async-start | bytes 4325376 | tf_op jit(solution)/shard_map/all_to_all | solution.py:969
  735.5 52.2 %all-gather.14.cloned.1.call-start = ((), (), s32[]{:S(2)}) async-start(), calls=%async_computation.24 | async-start | bytes 4718592 | tf_op jit(solution)/shard_map/all_gather | solution.py:647
  746.0 32.3 %collective-permute-start.85 = (bf16[1728,128]{1,0:T(8,128)(2,1)S(1)}, bf16[1728,128]{1,0:T(8,128)(2,1)S(1)}, u32[]{:S(2)}, u32[]{:S(2)}) collective-permute-start(bf16[1728,128]{1,0:T(8,128)(2,1)S(1)} %get-tuple-element.357), channel_id=1, source_target_pairs={{0,96},{32,64},{64,32},{96,0},{1,97},{33,65},{65,33},{97,1},{2,98}... | collective-permute-start | bytes 1327112 | tf_op jit(solution)/shard_map/ppermute | solution.py:34
  792.1 43.6 %all-gather.16.cloned.1.call-start = ((), (), s32[]{:S(2)}) async-start(), calls=%async_computation.25 | async-start | bytes 3981312 | tf_op jit(solution)/shard_map/all_gather | solution.py:647
  (353 other events, 3646.8 us)
Sparse Core Ops, SparseCore 0:
  21.9 30.6 all-gather.11
  63.9 54.7 all-gather.17
  149.1 25.5 all-gather.19
  176.8 34.7 all-gather.21
  214.7 51.3 all-gather.23
  480.7 25.2 reduce-scatter.6
  508.5 44.4 reduce-scatter.8
  577.3 18.7 reduce-scatter.16
  599.3 25.7 reduce-scatter.14
  637.1 27.3 reduce-scatter.12
  666.9 73.9 reduce-scatter.10
  743.2 44.4 all-gather.13
  799.9 27.2 all-gather.15
